TPU v7x, 256 devices: a whole 4x4x8 slice. The times are simulated.
256 devices in a mesh: modes: 16 (over x, y_hi, core), axial: 16 (over z, y_lo).
Axes of the slice: x: 4, y: 4 (y_hi: 2, y_lo: 2; y = y_hi * 2 + y_lo), z: 8, core: 2. Of those that a mesh axis runs over, the one named last changes fastest.
Arguments:
- potential_dual: float32 [512, 512, 128], P('modes', 'axial'), may hold values from -6 to 6
- velocity_dual: float32 [512, 512, 128], P('modes', 'axial'), may hold values from -6 to 6
- diffusivity: float32 [512, 128], P('axial'), may hold values from 0.3 to 1.4
- induct_self: float32 [512, 512, 128], P(None, ('axial', 'modes')), may hold values from -4 to 4
- induct_cross: float32 [512, 512, 128], P(None, ('axial', 'modes')), may hold values from -4 to 4
- lorentz_cross: float32 [512, 512, 128], P(None, ('axial', 'modes')), may hold values from -4 to 4
- advect_self: float32 [512, 512, 128], P(None, ('axial', 'modes')), may hold values from -4 to 4
Outputs:
- potential_grad: float32 [512, 512, 128], P('modes', 'axial')
- velocity_grad: float32 [512, 512, 128], P('modes', 'axial')
All inputs are finite; a program needn't handle non-finite values.
Results may differ from a plain program's by a relative error of at most 0.0001.
Values sent between devices are 32-bit elements; how exact they have to be, the bound alone decides.
No kernel may reach another device: no remote copies, remote signals or barrier semaphores. Data moves between devices by JAX's collectives and lax.ppermute only.
A program may use at most 64 MiB of HBM per device.

v0:
```python
import math

import jax
import jax.numpy as jnp
import numpy as np
from jax import lax
from jax.experimental import pallas as pl
from jax.experimental.pallas import tpu as pltpu
from jax.sharding import PartitionSpec as P

K = 512
HALF = K // 2
NR = 128
STEPS = 4
DT = 0.1
PEERS = 16
PER = K // PEERS
AXES = ("modes", "axial")
VMEM_BYTES = 24 * 1024 * 1024
F32 = jnp.float32
BF16 = jnp.bfloat16


def tables():
    idx = np.arange(HALF)

    def cas(rows):
        angle = 2.0 * np.pi / K * ((rows[:, None] * idx[None, :]) % K)
        return ((np.cos(angle) + np.sin(angle)) / math.sqrt(K)).astype(np.float32)

    def split(matrix):
        high = matrix.astype(jnp.bfloat16)
        low = (matrix - high.astype(np.float32)).astype(jnp.bfloat16)
        return np.concatenate([high, high, low], axis=1)

    even, odd = cas(2 * idx), cas(2 * idx + 1)
    return np.stack([split(even), split(odd), split(np.ascontiguousarray(odd.T))])


def call(body, out_shapes, args, flops, scratch=(), smem=0):
    space = [pl.BlockSpec(memory_space=pltpu.SMEM)] * smem
    space += [pl.BlockSpec(memory_space=pltpu.VMEM)] * (len(args) - smem)
    size = sum(math.prod(a.shape) * a.dtype.itemsize for a in list(args) + list(out_shapes))
    return pl.pallas_call(
        body,
        out_shape=out_shapes,
        in_specs=space,
        out_specs=[pl.BlockSpec(memory_space=pltpu.VMEM)] * len(out_shapes),
        scratch_shapes=scratch,
        compiler_params=pltpu.CompilerParams(vmem_limit_bytes=VMEM_BYTES),
        cost_estimate=pl.CostEstimate(flops=flops, bytes_accessed=size, transcendentals=0),
    )(*args)


def pack_kernel(pot_ref, vel_ref, out_ref):
    for dest in range(PEERS):
        for side in range(2):
            plane = 2 * dest + (side if dest % 2 == 0 else 1 - side)
            for field, ref in enumerate((pot_ref, vel_ref)):
                out_ref[dest, side, field] = ref[pl.ds(plane, PER, stride=32), :]


def unpack_kernel(in_ref, pot_ref, vel_ref):
    for src in range(PEERS):
        for side in range(2):
            plane = 2 * src + (side if src % 2 == 0 else 1 - side)
            for field, ref in enumerate((pot_ref, vel_ref)):
                ref[pl.ds(plane, PER, stride=32), :] = in_ref[src, side, field]


def factor_kernel(core_ref, *refs):
    ins, out_ref = refs[:4], refs[4]
    first = jnp.full((HALF, NR), core_ref[0], jnp.int32) == 0
    for which, ref in enumerate(ins):
        for parity in range(2):
            lower = ref[pl.ds(2 * parity, HALF, stride=4), :] * DT
            upper = ref[pl.ds(2 * parity + 1, HALF, stride=4), :] * DT
            rows = pl.ds(parity * HALF, HALF)
            out_ref[which, 0, rows, :] = jnp.where(first, lower, upper)
            out_ref[which, 1, rows, :] = jnp.where(first, upper, lower)


def stacked(value):
    high = value.astype(BF16)
    low = (value - high.astype(F32)).astype(BF16)
    return jnp.concatenate([high, low, high], axis=0)


def product(table, value):
    return jnp.dot(table, stacked(value), preferred_element_type=F32)


def step_kernel(outer_ref, inner_ref, factor_ref, table_ref, coef_ref, out_outer, out_inner):
    sides = (outer_ref, inner_ref)
    lo, hi = pl.ds(0, HALF), pl.ds(HALF, HALF)
    for side, (ref, out_ref) in enumerate(zip(sides, (out_outer, out_inner))):
        low = jnp.concatenate([ref[0, lo, :], ref[1, lo, :]], axis=1)
        high = jnp.concatenate([ref[0, hi, :], ref[1, hi, :]], axis=1)
        terms = []
        for parity, (mixed, rows) in enumerate(((low + high, lo), (low - high, hi))):
            spatial = product(table_ref[parity], mixed)
            pot, vel = spatial[:, :NR], spatial[:, NR:]
            terms.append(
                jnp.concatenate(
                    [
                        factor_ref[0, side, rows, :] * pot + factor_ref[1, side, rows, :] * vel,
                        factor_ref[2, side, rows, :] * pot + factor_ref[3, side, rows, :] * vel,
                    ],
                    axis=1,
                )
            )
        even = product(table_ref[0], terms[0])
        odd = product(table_ref[2], terms[1])
        back = (even + odd, even - odd)
        other = sides[1 - side]
        for half, rows in enumerate((lo, hi)):
            k = lax.broadcasted_iota(jnp.int32, (HALF, NR), 0) + half * HALF
            mode = jnp.minimum(k, K - k).astype(F32)
            mode_sq = mode * mode
            for field in range(2):
                value = ref[field, rows, :]
                coef = lambda row: coef_ref[side, field, pl.ds(row, 1), :]
                out_ref[field, rows, :] = (
                    (coef(0) - coef(1) * mode_sq) * value
                    + coef(2) * pltpu.roll(value, NR - 1, 1)
                    + coef(3) * pltpu.roll(value, 1, 1)
                    + coef(4) * other[field, rows, :]
                    + back[half][:, field * NR : (field + 1) * NR]
                )


def join_kernel(part_outer, part_inner, rim_outer, rim_inner, coef_ref, out_outer, out_inner):
    pairs = ((part_outer, rim_outer, out_outer), (part_inner, rim_inner, out_inner))
    for side, (part, rim, out) in enumerate(pairs):
        for field in range(2):
            out[field] = part[field] + coef_ref[side, field, pl.ds(5, 1), :] * rim[field]


def last_kernel(part_outer, part_inner, rim_outer, rim_inner, coef_ref, out_ref):
    for side, (part, rim) in enumerate(((part_outer, rim_outer), (part_inner, rim_inner))):
        for field in range(2):
            coef = coef_ref[side, field, pl.ds(5, 1), :]
            for dest in range(PEERS):
                rows = pl.ds(dest * PER, PER)
                out_ref[dest, side, field] = part[field, rows, :] + coef * rim[field, rows, :]


def coefficients(diffusivity, core):
    count = lax.axis_size("axial")
    up = [(i, i + 1) for i in range(count - 1)]
    down = [(i + 1, i) for i in range(count - 1)]
    modes, axial = lax.axis_index("modes"), lax.axis_index("axial")
    below = lax.ppermute(diffusivity[-1:], "axial", up)
    above = lax.ppermute(diffusivity[:1], "axial", down)
    rims = jnp.concatenate([below, diffusivity, above], axis=0)
    four = lax.dynamic_slice_in_dim(rims, 2 * modes, 4, axis=0)
    plane = axial * 32 + 2 * modes - 1 + jnp.arange(4)
    ones = jnp.where((plane >= 0) & (plane < 512), 1.0, 0.0).astype(F32)
    ones = jnp.broadcast_to(ones[:, None], (4, NR))
    four = jnp.stack([four, ones], axis=1)
    four = jnp.where(core == 0, four, four[::-1])
    near = four[1:3]
    beyond = 0.5 * (near + jnp.stack([four[0], four[3]]))
    middle = jnp.broadcast_to(0.5 * (four[1:2] + four[2:3]), near.shape)
    radius = NR + jnp.arange(NR, dtype=jnp.int32).astype(F32) + 0.5
    radius_face = NR + jnp.arange(1, NR, dtype=jnp.int32).astype(F32)
    face = 0.5 * (near[..., 1:] + near[..., :-1]) * radius_face
    face = jnp.pad(face, ((0, 0), (0, 0), (1, 1)))
    right = jnp.pad(face[..., 1:-1] / radius[1:], ((0, 0), (0, 0), (0, 1)))
    left = jnp.pad(face[..., 1:-1] / radius[:-1], ((0, 0), (0, 0), (1, 0)))
    own = -(face[..., 1:] + face[..., :-1]) / radius - (beyond + middle)
    rows = [
        1.0 + DT * own,
        DT * near / (radius * radius),
        DT * right,
        DT * left,
        DT * middle,
        DT * beyond,
    ]
    rows += [jnp.zeros_like(near)] * 2
    return jnp.stack(rows, axis=2)


def swaps():
    spot = lambda g: (g % 16) * 16 + g // 16
    inner, outer = [], []
    for g in range(255):
        (inner if g % 2 == 0 else outer).extend([(spot(g), spot(g + 1)), (spot(g + 1), spot(g))])
    return inner, outer


def on_device(pot, vel, diffusivity, *factors):
    shape = jax.ShapeDtypeStruct
    core = lax.rem(lax.axis_index("modes"), 2)
    inner_pairs, outer_pairs = swaps()
    table = jnp.asarray(tables())
    block = shape((PEERS, 2, 2, PER, NR), F32)
    plane = shape((2, K, NR), F32)
    flat = [a.reshape(-1, NR) for a in (pot, vel)]
    (sent,) = call(pack_kernel, [block], flat, 0)
    got = lax.all_to_all(sent, "modes", split_axis=0, concat_axis=0, tiled=True)
    (factor,) = call(
        factor_kernel,
        [shape((4, 2, K, NR), F32)],
        [core.reshape(1).astype(jnp.int32)] + [f.reshape(-1, NR) for f in factors],
        0,
        smem=1,
    )
    coef = coefficients(diffusivity, core)
    outer, inner = (got[:, side].transpose(1, 0, 2, 3).reshape(2, K, NR) for side in range(2))
    for step in range(STEPS):
        rim_outer = lax.ppermute(outer, AXES, outer_pairs)
        rim_inner = lax.ppermute(inner, AXES, inner_pairs)
        parts = call(
            step_kernel, [plane, plane], [outer, inner, factor, table, coef], 8 * 2 * 768 * 256 * 256
        )
        rims = [*parts, rim_outer, rim_inner, coef]
        if step < STEPS - 1:
            outer, inner = call(join_kernel, [plane, plane], rims, 0)
    (sent,) = call(last_kernel, [block], rims, 0)
    got = lax.all_to_all(sent, "modes", split_axis=0, concat_axis=0, tiled=True)
    outs = call(unpack_kernel, [shape((1024, NR), F32)] * 2, [got], 0)
    return tuple(a.reshape(32, 32, NR) for a in outs)


def solution(mesh):
    whole = P(None, ("axial", "modes"), None)
    modal = P("modes", "axial", None)
    return jax.shard_map(
        on_device,
        mesh=mesh,
        in_specs=(modal, modal, P("axial", None), whole, whole, whole, whole),
        out_specs=(modal, modal),
        check_vma=False,
    )
```

profile of v0, /device:TPU:1, one launch (start us, length us, event | category | flops | bytes accessed | tf_op | source)
XLA Modules:
  0.0 132.2 jit_solution(6037422482660020068)
XLA Ops:
  0.6 0.7 fusion.10
  1.3 1.3 collective-permute-start.1
  2.6 4.7 %collective-permute-start = (f32[1,128]{1,0:T(1,128)S(1)}, f32[1,128]{1,0:T(1,128)S(1)}, u32[]{:S(2)}, u32[]{:S(2)}) collective-permute-start(f32[1,128]{1,0:T(1,128)S(1)} %get-tuple-element.41), channel_id=1, source_target_pairs={{0,1},{1,2},{2,3},{3,4},{4,5},{5,6},{6,7},{7,8},{8,9},{9,10},{10,1... | collective-permute-start | bytes 1544 | tf_op jit(solution)/shard_map/ppermute | solution.py:153
  7.3 0.0 copy-start.5
  7.3 1.0 copy-done.5
  8.3 0.0 copy-start.6
  8.3 1.0 copy-done.6
  9.4 0.0 copy-start.1
  9.4 0.0 copy-start.2
  9.4 1.6 %shard_map.95 = f32[16,2,2,32,128]{4,3,2,1,0:T(8,128)} custom-call(f32[1024,128]{1,0:T(8,128)S(1)} %bitcast.40, f32[1024,128]{1,0:T(8,128)S(1)} %bitcast.41), custom_call_target="tpu_custom_call" | custom-call | bytes 2097152 | tf_op jit(solution)/shard_map/pallas_call | solution.py:44
  11.0 8.3 %all-to-all-start = ((f32[16,2,2,32,128]{4,3,2,1,0:T(8,128)}), f32[16,2,2,32,128]{4,3,2,1,0:T(8,128)}, u32[]{:S(2)}, u32[]{:S(2)}) async-start(f32[16,2,2,32,128]{4,3,2,1,0:T(8,128)} %shard_map.95), calls=%async_computation | async-start | bytes 2097152 | tf_op jit(solution)/shard_map/all_to_all | solution.py:201
  19.3 0.1 fusion.12
  19.4 0.0 copy-done.1
  19.4 0.0 copy-done.2
  19.4 0.0 copy-start.3
  19.4 1.0 copy-done.3
  20.5 0.0 copy-start.4
  20.5 1.0 copy-done.4
  21.5 0.0 copy-start.7
  21.5 0.2 shard_map.96.factor_ref
  21.7 0.0 collective-permute-done.1
  21.8 0.0 collective-permute-done
  21.8 0.5 copy-done.7
  22.2 0.1 stack_broadcast_in_dim.2
  22.4 0.1 broadcast_divide_fusion
  22.5 0.0 copy-start
  22.5 14.1 %all-to-all-done = f32[16,2,2,32,128]{4,3,2,1,0:T(8,128)} async-done(((f32[16,2,2,32,128]{4,3,2,1,0:T(8,128)}), f32[16,2,2,32,128]{4,3,2,1,0:T(8,128)}, u32[]{:S(2)}, u32[]{:S(2)}) %all-to-all-start) | async-done | bytes 1048608 | tf_op jit(solution)/shard_map/all_to_all | solution.py:201
  36.6 1.3 slice_bitcast_fusion
  37.9 0.8 copy.11
  38.8 0.8 copy.10
  39.6 2.8 %collective-permute-start.2 = (f32[2,512,128]{2,1,0:T(8,128)}, f32[2,512,128]{2,1,0:T(8,128)}, u32[]{:S(2)}, u32[]{:S(2)}) collective-permute-start(f32[2,512,128]{2,1,0:T(8,128)} %bitcast.4.outer_ref), channel_id=1, source_target_pairs={{16,32},{32,16},{48,64},{64,48},{80,96},{96,80},{112,128},{128,112... | collective-permute-start | bytes 1572872 | tf_op jit(solution)/shard_map/ppermute | solution.py:212
  42.4 0.1 collective-permute-start.3
  42.5 0.1 broadcast_multiply_fusion
  42.6 0.0 copy-done
  42.6 2.6 %shard_map.97 = (f32[2,512,128]{2,1,0:T(8,128)S(1)}, f32[2,512,128]{2,1,0:T(8,128)S(1)}) custom-call(f32[2,512,128]{2,1,0:T(8,128)} %bitcast.4.outer_ref, f32[2,512,128]{2,1,0:T(8,128)} %bitcast.7.inner_ref, f32[4,2,512,128]{3,2,1,0:T(8,128)S(1)} %shard_map.96.factor_ref, bf16[3,256,768]{2,1,0:T(8,128)(2,1)S(1)} %copy-done, f32[2,2,8,128]{3,2,1,0:T(8,128)S(1)} %stack.43.coef_ref), custom_call_target="tpu_custom_call" | custom-call | flops 805306368 | bytes 5390336 | tf_op jit(solution)/shard_map/pallas_call | solution.py:44
  45.3 9.1 %collective-permute-done.2.rim_outer = f32[2,512,128]{2,1,0:T(8,128)} collective-permute-done((f32[2,512,128]{2,1,0:T(8,128)}, f32[2,512,128]{2,1,0:T(8,128)}, u32[]{:S(2)}, u32[]{:S(2)}) %collective-permute-start.2) | collective-permute-done | bytes 524320 | tf_op jit(solution)/shard_map/ppermute | solution.py:212
  54.4 0.0 collective-permute-done.3.rim_inner
  54.4 1.3 shard_map.98
  55.7 5.9 %collective-permute-start.4 = (f32[2,512,128]{2,1,0:T(8,128)S(1)}, f32[2,512,128]{2,1,0:T(8,128)S(1)}, u32[]{:S(2)}, u32[]{:S(2)}) collective-permute-start(f32[2,512,128]{2,1,0:T(8,128)S(1)} %get-tuple-element.20.outer_ref), channel_id=1, source_target_pairs={{16,32},{32,16},{48,64},{64,48},{80,96},{96,80},{112,128},{128,112... | collective-permute-start | bytes 1572872 | tf_op jit(solution)/shard_map/ppermute | solution.py:212
  61.6 0.1 collective-permute-start.5
  61.7 1.4 %shard_map.99 = (f32[2,512,128]{2,1,0:T(8,128)S(1)}, f32[2,512,128]{2,1,0:T(8,128)S(1)}) custom-call(f32[2,512,128]{2,1,0:T(8,128)S(1)} %get-tuple-element.20.outer_ref, f32[2,512,128]{2,1,0:T(8,128)S(1)} %get-tuple-element.21.inner_ref, f32[4,2,512,128]{3,2,1,0:T(8,128)S(1)} %shard_map.96.factor_ref, bf16[3,256,768]{2,1,0:T(8,128)(2,1)S(1)} %copy-done, ...), custom_call_target="tpu_custom_call" | custom-call | flops 805306368 | bytes 5390336 | tf_op jit(solution)/shard_map/pallas_call | solution.py:44
  63.2 6.9 %collective-permute-done.4.rim_outer = f32[2,512,128]{2,1,0:T(8,128)S(1)} collective-permute-done((f32[2,512,128]{2,1,0:T(8,128)S(1)}, f32[2,512,128]{2,1,0:T(8,128)S(1)}, u32[]{:S(2)}, u32[]{:S(2)}) %collective-permute-start.4) | collective-permute-done | bytes 524320 | tf_op jit(solution)/shard_map/ppermute | solution.py:212
  70.1 0.0 collective-permute-done.5.rim_inner
  70.1 0.1 shard_map.100
  70.2 5.9 %collective-permute-start.6 = (f32[2,512,128]{2,1,0:T(8,128)S(1)}, f32[2,512,128]{2,1,0:T(8,128)S(1)}, u32[]{:S(2)}, u32[]{:S(2)}) collective-permute-start(f32[2,512,128]{2,1,0:T(8,128)S(1)} %get-tuple-element.24.outer_ref), channel_id=1, source_target_pairs={{16,32},{32,16},{48,64},{64,48},{80,96},{96,80},{112,128},{128,112... | collective-permute-start | bytes 1572872 | tf_op jit(solution)/shard_map/ppermute | solution.py:212
  76.1 0.1 collective-permute-start.7
  76.2 1.4 %shard_map.101 = (f32[2,512,128]{2,1,0:T(8,128)S(1)}, f32[2,512,128]{2,1,0:T(8,128)S(1)}) custom-call(f32[2,512,128]{2,1,0:T(8,128)S(1)} %get-tuple-element.24.outer_ref, f32[2,512,128]{2,1,0:T(8,128)S(1)} %get-tuple-element.25.inner_ref, f32[4,2,512,128]{3,2,1,0:T(8,128)S(1)} %shard_map.96.factor_ref, bf16[3,256,768]{2,1,0:T(8,128)(2,1)S(1)} %copy-done, ...), custom_call_target="tpu_custom_call" | custom-call | flops 805306368 | bytes 5390336 | tf_op jit(solution)/shard_map/pallas_call | solution.py:44
  77.7 5.6 %collective-permute-done.6.rim_outer = f32[2,512,128]{2,1,0:T(8,128)S(1)} collective-permute-done((f32[2,512,128]{2,1,0:T(8,128)S(1)}, f32[2,512,128]{2,1,0:T(8,128)S(1)}, u32[]{:S(2)}, u32[]{:S(2)}) %collective-permute-start.6) | collective-permute-done | bytes 524320 | tf_op jit(solution)/shard_map/ppermute | solution.py:212
  83.2 0.0 collective-permute-done.7.rim_inner
  83.2 0.1 shard_map.102
  83.4 5.9 %collective-permute-start.8 = (f32[2,512,128]{2,1,0:T(8,128)S(1)}, f32[2,512,128]{2,1,0:T(8,128)S(1)}, u32[]{:S(2)}, u32[]{:S(2)}) collective-permute-start(f32[2,512,128]{2,1,0:T(8,128)S(1)} %get-tuple-element.28.outer_ref), channel_id=1, source_target_pairs={{16,32},{32,16},{48,64},{64,48},{80,96},{96,80},{112,128},{128,112... | collective-permute-start | bytes 1572872 | tf_op jit(solution)/shard_map/ppermute | solution.py:212
  89.3 0.1 collective-permute-start.9
  89.4 1.4 %shard_map.103 = (f32[2,512,128]{2,1,0:T(8,128)S(1)}, f32[2,512,128]{2,1,0:T(8,128)S(1)}) custom-call(f32[2,512,128]{2,1,0:T(8,128)S(1)} %get-tuple-element.28.outer_ref, f32[2,512,128]{2,1,0:T(8,128)S(1)} %get-tuple-element.29.inner_ref, f32[4,2,512,128]{3,2,1,0:T(8,128)S(1)} %shard_map.96.factor_ref, bf16[3,256,768]{2,1,0:T(8,128)(2,1)S(1)} %copy-done, ...), custom_call_target="tpu_custom_call" | custom-call | flops 805306368 | bytes 5390336 | tf_op jit(solution)/shard_map/pallas_call | solution.py:44
  90.8 5.6 %collective-permute-done.8.rim_outer = f32[2,512,128]{2,1,0:T(8,128)S(1)} collective-permute-done((f32[2,512,128]{2,1,0:T(8,128)S(1)}, f32[2,512,128]{2,1,0:T(8,128)S(1)}, u32[]{:S(2)}, u32[]{:S(2)}) %collective-permute-start.8) | collective-permute-done | bytes 524320 | tf_op jit(solution)/shard_map/ppermute | solution.py:212
  96.4 0.0 collective-permute-done.9.rim_inner
  96.4 0.1 shard_map.104
  96.5 33.7 %all_to_all.10.in_ref = f32[16,2,2,32,128]{4,3,2,1,0:T(8,128)S(1)} all-to-all(f32[16,2,2,32,128]{4,3,2,1,0:T(8,128)S(1)} %shard_map.104), channel_id=1, replica_groups=mesh['modes'=16,'axial'=16] {'modes'}, dimensions={0} | all-to-all | bytes 2097152 | tf_op jit(solution)/shard_map/all_to_all | solution.py:221
  130.2 2.0 %shard_map.105 = (f32[1024,128]{1,0:T(8,128)}, f32[1024,128]{1,0:T(8,128)}) custom-call(f32[16,2,2,32,128]{4,3,2,1,0:T(8,128)S(1)} %all_to_all.10.in_ref), custom_call_target="tpu_custom_call" | custom-call | bytes 2097152 | tf_op jit(solution)/shard_map/pallas_call | solution.py:44
  (14 shorter events, 0.1 us)
Async XLA Ops:
  1.3 20.4 %collective-permute-start.1 = (f32[1,128]{1,0:T(1,128)S(1)}, f32[1,128]{1,0:T(1,128)S(1)}, u32[]{:S(2)}, u32[]{:S(2)}) collective-permute-start(f32[1,128]{1,0:T(1,128)S(1)} %get-tuple-element.40), channel_id=1, source_target_pairs={{1,0},{2,1},{3,2},{4,3},{5,4},{6,5},{7,6},{8,7},{9,8},{10,9},{11,1... | collective-permute-start | bytes 1544 | tf_op jit(solution)/shard_map/ppermute | solution.py:154
  2.6 19.1 %collective-permute-start = (f32[1,128]{1,0:T(1,128)S(1)}, f32[1,128]{1,0:T(1,128)S(1)}, u32[]{:S(2)}, u32[]{:S(2)}) collective-permute-start(f32[1,128]{1,0:T(1,128)S(1)} %get-tuple-element.41), channel_id=1, source_target_pairs={{0,1},{1,2},{2,3},{3,4},{4,5},{5,6},{6,7},{7,8},{8,9},{9,10},{10,1... | collective-permute-start | bytes 1544 | tf_op jit(solution)/shard_map/ppermute | solution.py:153
  7.3 1.0 copy-start.5
  8.3 1.0 copy-start.6
  9.4 10.0 %copy-start.1 = (f32[512,2,128]{2,1,0:T(2,128)S(1)}, f32[512,2,128]{2,1,0:T(2,128)}, u32[]{:S(2)}) copy-start(f32[512,2,128]{2,1,0:T(2,128)} %param.11) | copy-start | bytes 1572868
  9.4 10.0 %copy-start.2 = (f32[512,2,128]{2,1,0:T(2,128)S(1)}, f32[512,2,128]{2,1,0:T(2,128)}, u32[]{:S(2)}) copy-start(f32[512,2,128]{2,1,0:T(2,128)} %param.12) | copy-start | bytes 1572868
  11.0 25.6 %all-to-all-start = ((f32[16,2,2,32,128]{4,3,2,1,0:T(8,128)}), f32[16,2,2,32,128]{4,3,2,1,0:T(8,128)}, u32[]{:S(2)}, u32[]{:S(2)}) async-start(f32[16,2,2,32,128]{4,3,2,1,0:T(8,128)} %shard_map.95), calls=%async_computation | async-start | bytes 2097152 | tf_op jit(solution)/shard_map/all_to_all | solution.py:201
  19.4 1.0 copy-start.3
  20.5 1.0 copy-start.4
  21.5 0.7 copy-start.7
  22.5 20.2 %copy-start = (bf16[3,256,768]{2,1,0:T(8,128)(2,1)S(1)}, bf16[3,256,768]{2,1,0:T(8,128)(2,1)}, u32[]{:S(2)}) copy-start(bf16[3,256,768]{2,1,0:T(8,128)(2,1)} %constant.48.clone.table_ref) | copy-start | bytes 3538948
  39.6 14.8 %collective-permute-start.2 = (f32[2,512,128]{2,1,0:T(8,128)}, f32[2,512,128]{2,1,0:T(8,128)}, u32[]{:S(2)}, u32[]{:S(2)}) collective-permute-start(f32[2,512,128]{2,1,0:T(8,128)} %bitcast.4.outer_ref), channel_id=1, source_target_pairs={{16,32},{32,16},{48,64},{64,48},{80,96},{96,80},{112,128},{128,112... | collective-permute-start | bytes 1572872 | tf_op jit(solution)/shard_map/ppermute | solution.py:212
  42.4 12.0 %collective-permute-start.3 = (f32[2,512,128]{2,1,0:T(8,128)}, f32[2,512,128]{2,1,0:T(8,128)}, u32[]{:S(2)}, u32[]{:S(2)}) collective-permute-start(f32[2,512,128]{2,1,0:T(8,128)} %bitcast.7.inner_ref), channel_id=1, source_target_pairs={{0,16},{16,0},{32,48},{48,32},{64,80},{80,64},{96,112},{112,96},{1... | collective-permute-start | bytes 1572872 | tf_op jit(solution)/shard_map/ppermute | solution.py:213
  55.7 14.4 %collective-permute-start.4 = (f32[2,512,128]{2,1,0:T(8,128)S(1)}, f32[2,512,128]{2,1,0:T(8,128)S(1)}, u32[]{:S(2)}, u32[]{:S(2)}) collective-permute-start(f32[2,512,128]{2,1,0:T(8,128)S(1)} %get-tuple-element.20.outer_ref), channel_id=1, source_target_pairs={{16,32},{32,16},{48,64},{64,48},{80,96},{96,80},{112,128},{128,112... | collective-permute-start | bytes 1572872 | tf_op jit(solution)/shard_map/ppermute | solution.py:212
  61.6 8.5 %collective-permute-start.5 = (f32[2,512,128]{2,1,0:T(8,128)S(1)}, f32[2,512,128]{2,1,0:T(8,128)S(1)}, u32[]{:S(2)}, u32[]{:S(2)}) collective-permute-start(f32[2,512,128]{2,1,0:T(8,128)S(1)} %get-tuple-element.21.inner_ref), channel_id=1, source_target_pairs={{0,16},{16,0},{32,48},{48,32},{64,80},{80,64},{96,112},{112,96},{1... | collective-permute-start | bytes 1572872 | tf_op jit(solution)/shard_map/ppermute | solution.py:213
  70.2 13.0 %collective-permute-start.6 = (f32[2,512,128]{2,1,0:T(8,128)S(1)}, f32[2,512,128]{2,1,0:T(8,128)S(1)}, u32[]{:S(2)}, u32[]{:S(2)}) collective-permute-start(f32[2,512,128]{2,1,0:T(8,128)S(1)} %get-tuple-element.24.outer_ref), channel_id=1, source_target_pairs={{16,32},{32,16},{48,64},{64,48},{80,96},{96,80},{112,128},{128,112... | collective-permute-start | bytes 1572872 | tf_op jit(solution)/shard_map/ppermute | solution.py:212
  76.1 7.1 %collective-permute-start.7 = (f32[2,512,128]{2,1,0:T(8,128)S(1)}, f32[2,512,128]{2,1,0:T(8,128)S(1)}, u32[]{:S(2)}, u32[]{:S(2)}) collective-permute-start(f32[2,512,128]{2,1,0:T(8,128)S(1)} %get-tuple-element.25.inner_ref), channel_id=1, source_target_pairs={{0,16},{16,0},{32,48},{48,32},{64,80},{80,64},{96,112},{112,96},{1... | collective-permute-start | bytes 1572872 | tf_op jit(solution)/shard_map/ppermute | solution.py:213
  83.4 13.0 %collective-permute-start.8 = (f32[2,512,128]{2,1,0:T(8,128)S(1)}, f32[2,512,128]{2,1,0:T(8,128)S(1)}, u32[]{:S(2)}, u32[]{:S(2)}) collective-permute-start(f32[2,512,128]{2,1,0:T(8,128)S(1)} %get-tuple-element.28.outer_ref), channel_id=1, source_target_pairs={{16,32},{32,16},{48,64},{64,48},{80,96},{96,80},{112,128},{128,112... | collective-permute-start | bytes 1572872 | tf_op jit(solution)/shard_map/ppermute | solution.py:212
  89.3 7.1 %collective-permute-start.9 = (f32[2,512,128]{2,1,0:T(8,128)S(1)}, f32[2,512,128]{2,1,0:T(8,128)S(1)}, u32[]{:S(2)}, u32[]{:S(2)}) collective-permute-start(f32[2,512,128]{2,1,0:T(8,128)S(1)} %get-tuple-element.29.inner_ref), channel_id=1, source_target_pairs={{0,16},{16,0},{32,48},{48,32},{64,80},{80,64},{96,112},{112,96},{1... | collective-permute-start | bytes 1572872 | tf_op jit(solution)/shard_map/ppermute | solution.py:213
where the time goes:
time: 133 us; the launch traced here: 132 us
  waiting for transfers between devices  41.4 us (31%)
  starting transfers between devices  35.1 us (26%)
  blocking collectives  33.7 us (25%)
  Pallas kernels  12.3 us (9%)
  local copies, waits for them, and re-layouts  8.51 us (6%)
    all_to_all x1, blocking collectives, on_device(): got = lax.all_to_all(sent, 'modes', split_axis=0, concat_axis=0, tiled=True)  33.7 us
    ppermute x4, waiting for transfers between devices, on_device(): rim_outer = lax.ppermute(outer, AXES, outer_pairs)  27.2 us
    ppermute x4, starting transfers between devices, on_device(): rim_outer = lax.ppermute(outer, AXES, outer_pairs)  20.5 us
    all_to_all x1, waiting for transfers between devices, on_device(): got = lax.all_to_all(sent, 'modes', split_axis=0, concat_axis=0, tiled=True)  14.1 us
    pallas_call x11, Pallas kernels, call(): pl.pallas_call(body, out_shape=out_shapes, in_specs=space, out_specs=[pl....  12.3 us
    all_to_all x1, starting transfers between devices, on_device(): got = lax.all_to_all(sent, 'modes', split_axis=0, concat_axis=0, tiled=True)  8.33 us
    ppermute x1, starting transfers between devices, coefficients(): below = lax.ppermute(diffusivity[-1:], 'axial', up)  4.66 us
    unnamed x16, local copies, waits for them, and re-layouts  4.64 us
  transfers between devices with their start and end apart: 11, of which 5 were waited for; matrix products, arithmetic and copies ran while one was open for 0% of the time, Pallas kernels for 7%

commit v1 on v0

v1 whole, which is shorter than its diff:
```python
import functools
import math

import jax
import jax.numpy as jnp
import numpy as np
from jax import lax
from jax.experimental import pallas as pl
from jax.experimental.pallas import tpu as pltpu
from jax.sharding import PartitionSpec as P

K = 512
HALF = K // 2
NR = 128
STEPS = 4
DT = 0.1
PEERS = 16
PER = K // PEERS
CHUNK = 8
AXES = ("modes", "axial")
VMEM_BYTES = 24 * 1024 * 1024
F32 = jnp.float32
BF16 = jnp.bfloat16


def tables():
    idx = np.arange(HALF)

    def cas(rows):
        angle = 2.0 * np.pi / K * ((rows[:, None] * idx[None, :]) % K)
        return ((np.cos(angle) + np.sin(angle)) / math.sqrt(K)).astype(np.float32)

    def split(matrix):
        high = matrix.astype(jnp.bfloat16)
        low = (matrix - high.astype(np.float32)).astype(jnp.bfloat16)
        return np.concatenate([high, high, low], axis=1)

    even, odd = cas(2 * idx), cas(2 * idx + 1)
    return np.stack([split(even), split(odd), split(np.ascontiguousarray(odd.T))])


def call(body, out_shapes, args, flops, scratch=(), smem=0):
    space = [pl.BlockSpec(memory_space=pltpu.SMEM)] * smem
    space += [pl.BlockSpec(memory_space=pltpu.VMEM)] * (len(args) - smem)
    size = sum(math.prod(a.shape) * a.dtype.itemsize for a in list(args) + list(out_shapes))
    return pl.pallas_call(
        body,
        out_shape=out_shapes,
        in_specs=space,
        out_specs=[pl.BlockSpec(memory_space=pltpu.VMEM)] * len(out_shapes),
        scratch_shapes=scratch,
        compiler_params=pltpu.CompilerParams(vmem_limit_bytes=VMEM_BYTES),
        cost_estimate=pl.CostEstimate(flops=flops, bytes_accessed=size, transcendentals=0),
    )(*args)


def pack_kernel(pot_ref, vel_ref, out_ref):
    for dest in range(PEERS):
        for side in range(2):
            plane = 2 * dest + (side if dest % 2 == 0 else 1 - side)
            for field, ref in enumerate((pot_ref, vel_ref)):
                out_ref[dest, side, field] = ref[pl.ds(plane, CHUNK, stride=32), :]


def unpack_kernel(in_ref, pot_ref, vel_ref):
    for src in range(PEERS):
        for side in range(2):
            plane = 2 * src + (side if src % 2 == 0 else 1 - side)
            for field, ref in enumerate((pot_ref, vel_ref)):
                ref[pl.ds(plane, CHUNK, stride=32), :] = in_ref[src, side, field]


def by_mode(body, out_shapes, args):
    def spec(shape):
        if len(shape) == 2:
            return pl.BlockSpec((CHUNK * 32, NR), lambda i: (i, 0))
        return pl.BlockSpec((PEERS, 2, 2, CHUNK, NR), lambda i: (0, 0, 0, i, 0))

    args = [pltpu.with_memory_space_constraint(a, pltpu.HBM) for a in args]
    return pl.pallas_call(
        body,
        grid=(PER // CHUNK,),
        out_shape=[pltpu.HBM(a.shape, a.dtype) for a in out_shapes],
        in_specs=[spec(a.shape) for a in args],
        out_specs=[spec(a.shape) for a in out_shapes],
        compiler_params=pltpu.CompilerParams(vmem_limit_bytes=VMEM_BYTES),
        cost_estimate=pl.CostEstimate(flops=0, bytes_accessed=1 << 21, transcendentals=0),
    )(*args)


def split_kernel(core_ref, in_ref, diff_ref, out_outer, out_inner):
    for side, out in enumerate((out_outer, out_inner)):
        for src in range(PEERS):
            for field in range(2):
                out[pl.ds(field * K + src * PER, PER), :] = in_ref[src, side, field]
        own = near(core_ref, diff_ref, side)
        row = lax.broadcasted_iota(jnp.int32, (8, NR), 0)
        out[pl.ds(2 * K, 8), :] = jnp.where(row == 0, jnp.broadcast_to(own, (8, NR)), 1.0)


def near(core_ref, diff_ref, side):
    plane = core_ref[1] + (core_ref[0] if side == 0 else 1 - core_ref[0])
    return diff_ref[pl.ds(plane, 1), :]


def factor_kernel(core_ref, diff_ref, *refs):
    ins, out_ref, coef_ref = refs[:4], refs[4], refs[5]
    first = jnp.full((HALF, NR), core_ref[0], jnp.int32) == 0
    for which, ref in enumerate(ins):
        for parity in range(2):
            lower = ref[pl.ds(2 * parity, HALF, stride=4), :] * DT
            upper = ref[pl.ds(2 * parity + 1, HALF, stride=4), :] * DT
            rows = pl.ds(parity * HALF, HALF)
            out_ref[which, 0, rows, :] = jnp.where(first, lower, upper)
            out_ref[which, 1, rows, :] = jnp.where(first, upper, lower)
    tile = (8, NR)
    cell = lax.broadcasted_iota(jnp.int32, tile, 1)
    row = lax.broadcasted_iota(jnp.int32, tile, 0)
    face_radius = (cell + NR).astype(F32)
    radius = face_radius + 0.5
    values = [jnp.broadcast_to(near(core_ref, diff_ref, side), tile) for side in range(2)]
    for field in range(2):
        for side in range(2):
            own = values[side] if field == 0 else jnp.ones(tile, F32)
            middle = 0.5 * (values[0] + values[1]) if field == 0 else own
            face = jnp.where(cell > 0, 0.5 * (pltpu.roll(own, 1, 1) + own) * face_radius, 0.0)
            ahead = pltpu.roll(face, NR - 1, 1)
            terms = (
                1.0 - DT * ((ahead + face) / radius + middle),
                DT * own / (radius * radius),
                DT * ahead / (radius + 1.0),
                DT * face / (radius - 1.0),
                DT * middle,
            )
            total = jnp.zeros(tile, F32)
            for at, term in enumerate(terms):
                total = jnp.where(row == at, term, total)
            coef_ref[side, field] = total


def stacked(value):
    high = value.astype(BF16)
    low = (value - high.astype(F32)).astype(BF16)
    return jnp.concatenate([high, low, high], axis=0)


def product(table, value):
    return jnp.dot(table, stacked(value), preferred_element_type=F32)


def flux(edge_ref, side, field, rim, value, past):
    edge = lambda row: edge_ref[side, pl.ds(row, 1), :]
    beyond = rim if past is None else edge(2) * (rim - past)
    return edge(field) * (beyond - value)


def field_rows(field):
    return pl.ds(field * K, K)


def first_kernel(outer, inner, factor_ref, table_ref, coef_ref, out_outer, out_inner):
    step_alone((outer, inner), factor_ref, table_ref, coef_ref, (out_outer, out_inner))


def next_kernel(opening, *refs):
    refs = list(refs)
    take = lambda n: [refs.pop(0) for _ in range(n)]
    parts, olds, rims = take(2), take(2), take(2)
    pasts, edge_ref = ((None, None), None) if opening else (take(2), take(1)[0])
    factor_ref, table_ref, coef_ref = take(3)
    outs, fulls, fluxes = take(2), take(2), take(2)
    if opening:
        (edge_ref,) = take(1)
        for side in range(2):
            own, other = (ref[pl.ds(2 * K, 8), :] for ref in (olds[side], rims[side]))
            row = lax.broadcasted_iota(jnp.int32, (8, NR), 0)
            edge_ref[side] = jnp.where(row < 2, DT * 0.5 * (own + other), other)
    for side in range(2):
        for field in range(2):
            rows = field_rows(field)
            past = None if opening else pasts[side][rows, :]
            flow = flux(edge_ref, side, field, rims[side][rows, :], olds[side][rows, :], past)
            fluxes[side][rows, :] = flow
            fulls[side][rows, :] = parts[side][rows, :] + flow
    step_alone(fulls, factor_ref, table_ref, coef_ref, outs)


def step_alone(sides, factor_ref, table_ref, coef_ref, outs):
    spans = [[pl.ds(field * K + half * HALF, HALF) for half in range(2)] for field in range(2)]
    for side, (ref, out_ref) in enumerate(zip(sides, outs)):
        low, high = (
            jnp.concatenate([ref[spans[0][half], :], ref[spans[1][half], :]], axis=1)
            for half in range(2)
        )
        terms = []
        for parity, mixed in enumerate((low + high, low - high)):
            spatial = product(table_ref[parity], mixed)
            pot, vel = spatial[:, :NR], spatial[:, NR:]
            rows = pl.ds(parity * HALF, HALF)
            terms.append(
                jnp.concatenate(
                    [
                        factor_ref[0, side, rows, :] * pot + factor_ref[1, side, rows, :] * vel,
                        factor_ref[2, side, rows, :] * pot + factor_ref[3, side, rows, :] * vel,
                    ],
                    axis=1,
                )
            )
        even = product(table_ref[0], terms[0])
        odd = product(table_ref[2], terms[1])
        back = (even + odd, even - odd)
        other = sides[1 - side]
        for half in range(2):
            k = lax.broadcasted_iota(jnp.int32, (HALF, NR), 0) + half * HALF
            mode = jnp.minimum(k, K - k).astype(F32)
            mode_sq = mode * mode
            for field in range(2):
                rows = spans[field][half]
                value = ref[rows, :]
                coef = lambda row: coef_ref[side, field, pl.ds(row, 1), :]
                out_ref[rows, :] = (
                    (coef(0) - coef(1) * mode_sq) * value
                    + coef(2) * pltpu.roll(value, NR - 1, 1)
                    + coef(3) * pltpu.roll(value, 1, 1)
                    + coef(4) * other[rows, :]
                    + back[half][:, field * NR : (field + 1) * NR]
                )


def last_kernel(*refs):
    parts, olds, rims, pasts = (refs[i : i + 2] for i in range(0, 8, 2))
    edge_ref, out_ref = refs[8:]
    for side in range(2):
        for field in range(2):
            for dest in range(PEERS):
                rows = pl.ds(field * K + dest * PER, PER)
                flow = flux(
                    edge_ref, side, field, rims[side][rows, :], olds[side][rows, :], pasts[side][rows, :]
                )
                out_ref[dest, side, field] = parts[side][rows, :] + flow


def swaps():
    spot = lambda g: (g % 16) * 16 + g // 16
    inner, outer = [], []
    for g in range(255):
        (inner if g % 2 == 0 else outer).extend([(spot(g), spot(g + 1)), (spot(g + 1), spot(g))])
    return inner, outer


def on_device(pot, vel, diffusivity, *factors):
    shape = jax.ShapeDtypeStruct
    modes = lax.axis_index("modes").astype(jnp.int32)
    place = jnp.stack([modes % 2, 2 * modes])
    inner_pairs, outer_pairs = swaps()
    table = jnp.asarray(tables())
    block = shape((PEERS, 2, 2, PER, NR), F32)
    plane = shape((2 * K, NR), F32)
    opening = shape((2 * K + 8, NR), F32)
    tiles = shape((2, 2, 8, NR), F32)
    (sent,) = by_mode(pack_kernel, [block], [a.reshape(-1, NR) for a in (pot, vel)])
    sent, factors = lax.optimization_barrier((sent, factors))
    got = lax.all_to_all(sent, "modes", split_axis=0, concat_axis=0, tiled=True)
    factor, coef = call(
        factor_kernel,
        [shape((4, 2, K, NR), F32), tiles],
        [place, diffusivity] + [f.reshape(-1, NR) for f in factors],
        0,
        smem=1,
    )
    got, factor, coef = lax.optimization_barrier((got, factor, coef))
    start = call(split_kernel, [opening] * 2, [place, got, diffusivity], 0, smem=1)
    shared = [factor, table, coef]
    flops = 8 * 2 * 768 * 256 * 256

    def swap(planes):
        return [lax.ppermute(planes[0], AXES, outer_pairs), lax.ppermute(planes[1], AXES, inner_pairs)]

    rims = swap(start)
    parts = call(first_kernel, [plane] * 2, [*start, *shared], flops)
    olds, pasts = start, []
    for step in range(1, STEPS):
        coming = swap(parts)
        outs = call(
            functools.partial(next_kernel, step == 1),
            [plane] * 6 + ([shape((2, 8, NR), F32)] if step == 1 else []),
            [*parts, *olds, *rims, *pasts, *shared],
            flops,
        )
        parts, olds = outs[:2], outs[2:4]
        edge = outs[6] if step == 1 else edge
        pasts, rims = [*outs[4:6], edge], coming
    (sent,) = call(last_kernel, [block], [*parts, *olds, *rims, *pasts], 0)
    got = lax.all_to_all(sent, "modes", split_axis=0, concat_axis=0, tiled=True)
    outs = by_mode(unpack_kernel, [shape((32 * PER, NR), F32)] * 2, [got])
    return tuple(a.reshape(PER, 32, NR) for a in outs)


def solution(mesh):
    whole = P(None, ("axial", "modes"), None)
    modal = P("modes", "axial", None)
    return jax.shard_map(
        on_device,
        mesh=mesh,
        in_specs=(modal, modal, P("axial", None), whole, whole, whole, whole),
        out_specs=(modal, modal),
        check_vma=False,
    )
```

time: 133 us -> 111 us (0.83)
  the two profiles are of different devices: /device:TPU:1 before, /device:TPU:104 now
where the time goes in v1:
time: 111 us; the launch traced here: 109 us
  starting transfers between devices  32.9 us (30%)
  waiting for transfers between devices  30.5 us (27%)
  blocking collectives  23.6 us (21%)
  Pallas kernels  17 us (15%)
  local copies, waits for them, and re-layouts  4.25 us (4%)
    all_to_all x1, blocking collectives, on_device(): got = lax.all_to_all(sent, 'modes', split_axis=0, concat_axis=0, tiled=True)  23.6 us
    ppermute x4, waiting for transfers between devices, swap(): lax.ppermute(planes[0], AXES, outer_pairs)  17.8 us
    ppermute x4, starting transfers between devices, swap(): lax.ppermute(planes[1], AXES, inner_pairs)  13.7 us
    ppermute x4, starting transfers between devices, swap(): lax.ppermute(planes[0], AXES, outer_pairs)  13 us
    all_to_all x1, waiting for transfers between devices, on_device(): got = lax.all_to_all(sent, 'modes', split_axis=0, concat_axis=0, tiled=True)  12.7 us
    pallas_call x7, Pallas kernels, call(): pl.pallas_call(body, out_shape=out_shapes, in_specs=space, out_specs=[pl....  9.49 us
    pallas_call x2, Pallas kernels, by_mode(): pl.pallas_call(body, grid=(PER // CHUNK,), out_shape=[pltpu.HBM(a.shape,...  7.52 us
    all_to_all x1, starting transfers between devices, on_device(): got = lax.all_to_all(sent, 'modes', split_axis=0, concat_axis=0, tiled=True)  6.19 us
  transfers between devices with their start and end apart: 9, of which 3 were waited for; matrix products, arithmetic and copies ran while one was open for 0% of the time, Pallas kernels for 7%

profile of v1, /device:TPU:104, one launch (start us, length us, event | category | flops | bytes accessed | tf_op | source)
XLA Modules:
  0.0 109.1 jit_solution(894953791522612925)
XLA Ops:
  0.6 0.0 copy-start.5
  0.6 3.8 %shard_map.95 = f32[16,2,2,32,128]{4,3,2,1,0:T(8,128)} custom-call(f32[1024,128]{1,0:T(8,128)} %bitcast.14, f32[1024,128]{1,0:T(8,128)} %bitcast.15), custom_call_target="tpu_custom_call" | custom-call | bytes 2097152 | tf_op jit(solution)/shard_map/pallas_call | solution.py:80
  4.4 6.2 %all-to-all-start = ((f32[16,2,2,32,128]{4,3,2,1,0:T(8,128)}), f32[16,2,2,32,128]{4,3,2,1,0:T(8,128)}, u32[]{:S(2)}, u32[]{:S(2)}) async-start(f32[16,2,2,32,128]{4,3,2,1,0:T(8,128)} %shard_map.95), calls=%async_computation | async-start | bytes 2097152 | tf_op jit(solution)/shard_map/all_to_all | solution.py:263
  10.6 0.0 copy-start
  10.7 0.1 pad_add_fusion.core_ref
  10.7 0.0 copy-done.5
  10.7 0.0 copy-start.1
  10.7 1.1 %copy-done.1 = f32[512,2,128]{2,1,0:T(2,128)S(1)} copy-done((f32[512,2,128]{2,1,0:T(2,128)S(1)}, f32[512,2,128]{2,1,0:T(2,128)}, u32[]{:S(2)}) %copy-start.1) | copy-done | bytes 524312
  11.9 0.0 copy-start.2
  11.9 1.0 copy-done.2
  12.9 0.0 copy-start.3
  12.9 1.0 copy-done.3
  13.9 0.0 copy-start.4
  13.9 1.0 copy-done.4
  15.0 1.0 shard_map.96
  16.0 12.7 %all-to-all-done.in_ref = f32[16,2,2,32,128]{4,3,2,1,0:T(8,128)} async-done(((f32[16,2,2,32,128]{4,3,2,1,0:T(8,128)}), f32[16,2,2,32,128]{4,3,2,1,0:T(8,128)}, u32[]{:S(2)}, u32[]{:S(2)}) %all-to-all-start) | async-done | bytes 1048608 | tf_op jit(solution)/shard_map/all_to_all | solution.py:263
  28.7 1.3 %shard_map.97 = (f32[1032,128]{1,0:T(8,128)S(1)}, f32[1032,128]{1,0:T(8,128)S(1)}) custom-call(s32[2]{0:T(128)S(1)} %pad_add_fusion.core_ref, f32[16,2,2,32,128]{4,3,2,1,0:T(8,128)} %all-to-all-done.in_ref, f32[32,128]{1,0:T(8,128)S(1)} %copy-done.5), custom_call_target="tpu_custom_call" | custom-call | bytes 2121736 | tf_op jit(solution)/shard_map/pallas_call | solution.py:46
  30.0 1.9 %collective-permute-start = (f32[1032,128]{1,0:T(8,128)S(1)}, f32[1032,128]{1,0:T(8,128)S(1)}, u32[]{:S(2)}, u32[]{:S(2)}) collective-permute-start(f32[1032,128]{1,0:T(8,128)S(1)} %get-tuple-element.45.outer.refs_2_), channel_id=1, source_target_pairs={{16,32},{32,16},{48,64},{64,48},{80,96},{96,80},{112,128},{128,112... | collective-permute-start | bytes 1585160 | tf_op jit(solution)/shard_map/ppermute | solution.py:277
  31.9 0.6 collective-permute-start.1
  32.5 0.0 copy-done
  32.5 1.6 %shard_map.98 = (f32[1024,128]{1,0:T(8,128)S(1)}, f32[1024,128]{1,0:T(8,128)S(1)}) custom-call(f32[1032,128]{1,0:T(8,128)S(1)} %get-tuple-element.45.outer.refs_2_, f32[1032,128]{1,0:T(8,128)S(1)} %get-tuple-element.46.inner.refs_3_, f32[4,2,512,128]{3,2,1,0:T(8,128)S(1)} %get-tuple-element.47.factor_ref.refs_6_.refs_9_, bf16[3,256,768]{2,1,0:T(8,128)(2,1)S(1)} %copy-done, ...), custom_call_target="tpu_custom_call" | custom-call | flops 805306368 | bytes 5398528 | tf_op jit(solution)/shard_map/pallas_call | solution.py:46
  34.1 5.2 %collective-permute-start.2 = (f32[1024,128]{1,0:T(8,128)S(1)}, f32[1024,128]{1,0:T(8,128)S(1)}, u32[]{:S(2)}, u32[]{:S(2)}) collective-permute-start(f32[1024,128]{1,0:T(8,128)S(1)} %get-tuple-element.49.refs_0_), channel_id=1, source_target_pairs={{16,32},{32,16},{48,64},{64,48},{80,96},{96,80},{112,128},{128,112... | collective-permute-start | bytes 1572872 | tf_op jit(solution)/shard_map/ppermute | solution.py:277
  39.4 0.1 collective-permute-start.3
  39.5 7.1 %collective-permute-done.refs_4_ = f32[1032,128]{1,0:T(8,128)S(1)} collective-permute-done((f32[1032,128]{1,0:T(8,128)S(1)}, f32[1032,128]{1,0:T(8,128)S(1)}, u32[]{:S(2)}, u32[]{:S(2)}) %collective-permute-start) | collective-permute-done | bytes 528416 | tf_op jit(solution)/shard_map/ppermute | solution.py:277
  46.6 0.0 collective-permute-done.1.refs_5_
  46.6 1.7 %shard_map.99 = (f32[1024,128]{1,0:T(8,128)S(1)}, f32[1024,128]{1,0:T(8,128)S(1)}, f32[1024,128]{1,0:T(8,128)S(1)}, f32[1024,128]{1,0:T(8,128)S(1)}, f32[1024,12...) custom-call(f32[1024,128]{1,0:T(8,128)S(1)} %get-tuple-element.49.refs_0_, ...), custom_call_target="tpu_custom_call" | custom-call | flops 805306368 | bytes 9609216 | tf_op jit(solution)/shard_map/pallas_call | solution.py:46
  48.3 1.9 %collective-permute-start.4 = (f32[1024,128]{1,0:T(8,128)S(1)}, f32[1024,128]{1,0:T(8,128)S(1)}, u32[]{:S(2)}, u32[]{:S(2)}) collective-permute-start(f32[1024,128]{1,0:T(8,128)S(1)} %get-tuple-element.51.refs_0_), channel_id=1, source_target_pairs={{16,32},{32,16},{48,64},{64,48},{80,96},{96,80},{112,128},{128,112... | collective-permute-start | bytes 1572872 | tf_op jit(solution)/shard_map/ppermute | solution.py:277
  50.3 12.9 %collective-permute-start.5 = (f32[1024,128]{1,0:T(8,128)S(1)}, f32[1024,128]{1,0:T(8,128)S(1)}, u32[]{:S(2)}, u32[]{:S(2)}) collective-permute-start(f32[1024,128]{1,0:T(8,128)S(1)} %get-tuple-element.52.refs_1_), channel_id=1, source_target_pairs={{0,16},{16,0},{32,48},{48,32},{64,80},{80,64},{96,112},{112,96},{1... | collective-permute-start | bytes 1572872 | tf_op jit(solution)/shard_map/ppermute | solution.py:277
  63.2 0.0 collective-permute-done.2.refs_4_
  63.2 0.0 collective-permute-done.3.refs_5_
  63.2 1.9 %shard_map.100 = (f32[1024,128]{1,0:T(8,128)S(1)}, f32[1024,128]{1,0:T(8,128)S(1)}, f32[1024,128]{1,0:T(8,128)S(1)}, f32[1024,128]{1,0:T(8,128)S(1)}, f32[1024,128]{1,0:T(8,128)S(1)}, /*index=5*/f32[1024,128]{1,0:T(8,128)S(1)}) custom-call(f32[1024,128]{1,0:T(8,128)S(1)} %get-tuple-element.51.refs_0_, f32[1024,128]{1,0:T(8,128)S(1)} %get-tuple-element.52.refs_1_, ...), custom_call_target="tpu_custom_call" | custom-call | flops 805306368 | bytes 10641408 | tf_op jit(solution)/shard_map/pallas_call | solution.py:46
  65.1 3.9 %collective-permute-start.6 = (f32[1024,128]{1,0:T(8,128)S(1)}, f32[1024,128]{1,0:T(8,128)S(1)}, u32[]{:S(2)}, u32[]{:S(2)}) collective-permute-start(f32[1024,128]{1,0:T(8,128)S(1)} %get-tuple-element.58.refs_0_), channel_id=1, source_target_pairs={{16,32},{32,16},{48,64},{64,48},{80,96},{96,80},{112,128},{128,112... | collective-permute-start | bytes 1572872 | tf_op jit(solution)/shard_map/ppermute | solution.py:277
  69.0 0.1 collective-permute-start.7
  69.1 0.0 collective-permute-done.4.refs_4_
  69.1 0.0 collective-permute-done.5.refs_5_
  69.1 1.9 %shard_map.101 = (f32[1024,128]{1,0:T(8,128)S(1)}, f32[1024,128]{1,0:T(8,128)S(1)}, f32[1024,128]{1,0:T(8,128)S(1)}, f32[1024,128]{1,0:T(8,128)S(1)}, f32[1024,128]{1,0:T(8,128)S(1)}, /*index=5*/f32[1024,128]{1,0:T(8,128)S(1)}) custom-call(f32[1024,128]{1,0:T(8,128)S(1)} %get-tuple-element.58.refs_0_, f32[1024,128]{1,0:T(8,128)S(1)} %get-tuple-element.59.refs_1_, ...), custom_call_target="tpu_custom_call" | custom-call | flops 805306368 | bytes 10641408 | tf_op jit(solution)/shard_map/pallas_call | solution.py:46
  71.0 10.6 %collective-permute-done.6.refs_4_ = f32[1024,128]{1,0:T(8,128)S(1)} collective-permute-done((f32[1024,128]{1,0:T(8,128)S(1)}, f32[1024,128]{1,0:T(8,128)S(1)}, u32[]{:S(2)}, u32[]{:S(2)}) %collective-permute-start.6) | collective-permute-done | bytes 524320 | tf_op jit(solution)/shard_map/ppermute | solution.py:277
  81.6 0.0 collective-permute-done.7.refs_5_
  81.6 0.2 shard_map.102
  81.8 23.6 %all_to_all.10.in_ref = f32[16,2,2,32,128]{4,3,2,1,0:T(8,128)} all-to-all(f32[16,2,2,32,128]{4,3,2,1,0:T(8,128)S(1)} %shard_map.102), channel_id=1, replica_groups=mesh['modes'=16,'axial'=16] {'modes'}, dimensions={0} | all-to-all | bytes 2097152 | tf_op jit(solution)/shard_map/all_to_all | solution.py:294
  105.4 3.7 %shard_map.103 = (f32[1024,128]{1,0:T(8,128)}, f32[1024,128]{1,0:T(8,128)}) custom-call(f32[16,2,2,32,128]{4,3,2,1,0:T(8,128)} %all_to_all.10.in_ref), custom_call_target="tpu_custom_call" | custom-call | bytes 2097152 | tf_op jit(solution)/shard_map/pallas_call | solution.py:80
Async XLA Ops:
  0.6 10.1 %copy-start.5 = (f32[32,128]{1,0:T(8,128)S(1)}, f32[32,128]{1,0:T(8,128)}, u32[]{:S(2)}) copy-start(f32[32,128]{1,0:T(8,128)} %diff_ref.3) | copy-start | bytes 49156
  4.4 24.2 %all-to-all-start = ((f32[16,2,2,32,128]{4,3,2,1,0:T(8,128)}), f32[16,2,2,32,128]{4,3,2,1,0:T(8,128)}, u32[]{:S(2)}, u32[]{:S(2)}) async-start(f32[16,2,2,32,128]{4,3,2,1,0:T(8,128)} %shard_map.95), calls=%async_computation | async-start | bytes 2097152 | tf_op jit(solution)/shard_map/all_to_all | solution.py:263
  10.6 21.9 %copy-start = (bf16[3,256,768]{2,1,0:T(8,128)(2,1)S(1)}, bf16[3,256,768]{2,1,0:T(8,128)(2,1)}, u32[]{:S(2)}) copy-start(bf16[3,256,768]{2,1,0:T(8,128)(2,1)} %constant.20.clone.table_ref.refs_7_.refs_10_) | copy-start | bytes 3538948
  10.7 1.1 %copy-start.1 = (f32[512,2,128]{2,1,0:T(2,128)S(1)}, f32[512,2,128]{2,1,0:T(2,128)}, u32[]{:S(2)}) copy-start(f32[512,2,128]{2,1,0:T(2,128)} %param.11) | copy-start | bytes 1572868
  11.9 1.0 copy-start.2
  12.9 1.0 copy-start.3
  13.9 1.0 copy-start.4
  30.0 16.6 %collective-permute-start = (f32[1032,128]{1,0:T(8,128)S(1)}, f32[1032,128]{1,0:T(8,128)S(1)}, u32[]{:S(2)}, u32[]{:S(2)}) collective-permute-start(f32[1032,128]{1,0:T(8,128)S(1)} %get-tuple-element.45.outer.refs_2_), channel_id=1, source_target_pairs={{16,32},{32,16},{48,64},{64,48},{80,96},{96,80},{112,128},{128,112... | collective-permute-start | bytes 1585160 | tf_op jit(solution)/shard_map/ppermute | solution.py:277
  31.9 14.7 %collective-permute-start.1 = (f32[1032,128]{1,0:T(8,128)S(1)}, f32[1032,128]{1,0:T(8,128)S(1)}, u32[]{:S(2)}, u32[]{:S(2)}) collective-permute-start(f32[1032,128]{1,0:T(8,128)S(1)} %get-tuple-element.46.inner.refs_3_), channel_id=1, source_target_pairs={{0,16},{16,0},{32,48},{48,32},{64,80},{80,64},{96,112},{112,96},{1... | collective-permute-start | bytes 1585160 | tf_op jit(solution)/shard_map/ppermute | solution.py:277
  34.1 29.1 %collective-permute-start.2 = (f32[1024,128]{1,0:T(8,128)S(1)}, f32[1024,128]{1,0:T(8,128)S(1)}, u32[]{:S(2)}, u32[]{:S(2)}) collective-permute-start(f32[1024,128]{1,0:T(8,128)S(1)} %get-tuple-element.49.refs_0_), channel_id=1, source_target_pairs={{16,32},{32,16},{48,64},{64,48},{80,96},{96,80},{112,128},{128,112... | collective-permute-start | bytes 1572872 | tf_op jit(solution)/shard_map/ppermute | solution.py:277
  39.4 23.8 %collective-permute-start.3 = (f32[1024,128]{1,0:T(8,128)S(1)}, f32[1024,128]{1,0:T(8,128)S(1)}, u32[]{:S(2)}, u32[]{:S(2)}) collective-permute-start(f32[1024,128]{1,0:T(8,128)S(1)} %get-tuple-element.50.refs_1_), channel_id=1, source_target_pairs={{0,16},{16,0},{32,48},{48,32},{64,80},{80,64},{96,112},{112,96},{1... | collective-permute-start | bytes 1572872 | tf_op jit(solution)/shard_map/ppermute | solution.py:277
  48.3 20.8 %collective-permute-start.4 = (f32[1024,128]{1,0:T(8,128)S(1)}, f32[1024,128]{1,0:T(8,128)S(1)}, u32[]{:S(2)}, u32[]{:S(2)}) collective-permute-start(f32[1024,128]{1,0:T(8,128)S(1)} %get-tuple-element.51.refs_0_), channel_id=1, source_target_pairs={{16,32},{32,16},{48,64},{64,48},{80,96},{96,80},{112,128},{128,112... | collective-permute-start | bytes 1572872 | tf_op jit(solution)/shard_map/ppermute | solution.py:277
  50.3 18.8 %collective-permute-start.5 = (f32[1024,128]{1,0:T(8,128)S(1)}, f32[1024,128]{1,0:T(8,128)S(1)}, u32[]{:S(2)}, u32[]{:S(2)}) collective-permute-start(f32[1024,128]{1,0:T(8,128)S(1)} %get-tuple-element.52.refs_1_), channel_id=1, source_target_pairs={{0,16},{16,0},{32,48},{48,32},{64,80},{80,64},{96,112},{112,96},{1... | collective-permute-start | bytes 1572872 | tf_op jit(solution)/shard_map/ppermute | solution.py:277
  65.1 16.6 %collective-permute-start.6 = (f32[1024,128]{1,0:T(8,128)S(1)}, f32[1024,128]{1,0:T(8,128)S(1)}, u32[]{:S(2)}, u32[]{:S(2)}) collective-permute-start(f32[1024,128]{1,0:T(8,128)S(1)} %get-tuple-element.58.refs_0_), channel_id=1, source_target_pairs={{16,32},{32,16},{48,64},{64,48},{80,96},{96,80},{112,128},{128,112... | collective-permute-start | bytes 1572872 | tf_op jit(solution)/shard_map/ppermute | solution.py:277
  69.0 12.6 %collective-permute-start.7 = (f32[1024,128]{1,0:T(8,128)S(1)}, f32[1024,128]{1,0:T(8,128)S(1)}, u32[]{:S(2)}, u32[]{:S(2)}) collective-permute-start(f32[1024,128]{1,0:T(8,128)S(1)} %get-tuple-element.59.refs_1_), channel_id=1, source_target_pairs={{0,16},{16,0},{32,48},{48,32},{64,80},{80,64},{96,112},{112,96},{1... | collective-permute-start | bytes 1572872 | tf_op jit(solution)/shard_map/ppermute | solution.py:277

commit v2 on v1

--- a/solution.py
+++ b/solution.py
@@ -54,35 +54,77 @@
     )(*args)
 
 
-def pack_kernel(pot_ref, vel_ref, out_ref):
-    for dest in range(PEERS):
+def chunk_rows(chunk):
+    return pl.ds(chunk * CHUNK * 32, CHUNK * 32)
+
+
+def chunk_block(ref, chunk):
+    return ref.at[:, :, :, pl.ds(chunk * CHUNK, CHUNK)]
+
+
+def planes():
+    for peer in range(PEERS):
         for side in range(2):
-            plane = 2 * dest + (side if dest % 2 == 0 else 1 - side)
-            for field, ref in enumerate((pot_ref, vel_ref)):
-                out_ref[dest, side, field] = ref[pl.ds(plane, CHUNK, stride=32), :]
-
-
-def unpack_kernel(in_ref, pot_ref, vel_ref):
-    for src in range(PEERS):
-        for side in range(2):
-            plane = 2 * src + (side if src % 2 == 0 else 1 - side)
-            for field, ref in enumerate((pot_ref, vel_ref)):
-                ref[pl.ds(plane, CHUNK, stride=32), :] = in_ref[src, side, field]
-
-
-def by_mode(body, out_shapes, args):
-    def spec(shape):
-        if len(shape) == 2:
-            return pl.BlockSpec((CHUNK * 32, NR), lambda i: (i, 0))
-        return pl.BlockSpec((PEERS, 2, 2, CHUNK, NR), lambda i: (0, 0, 0, i, 0))
-
-    args = [pltpu.with_memory_space_constraint(a, pltpu.HBM) for a in args]
+            yield peer, side, 2 * peer + (side if peer % 2 == 0 else 1 - side)
+
+
+def pack_kernel(pot_ref, vel_ref, out_ref, rows, block, in_sems, out_sems):
+    chunks = range(PER // CHUNK)
+    arrive = [
+        [
+            pltpu.make_async_copy(
+                ref.at[chunk_rows(chunk)], rows.at[field, chunk_rows(chunk)], in_sems.at[field, chunk]
+            )
+            for field, ref in enumerate((pot_ref, vel_ref))
+        ]
+        for chunk in chunks
+    ]
+    for pair in arrive:
+        for copy in pair:
+            copy.start()
+    leave = []
+    for chunk in chunks:
+        for field in range(2):
+            arrive[chunk][field].wait()
+            for peer, side, plane in planes():
+                block[peer, side, field, pl.ds(chunk * CHUNK, CHUNK)] = rows[
+                    field, pl.ds(chunk * CHUNK * 32 + plane, CHUNK, stride=32), :
+                ]
+        leave.append(
+            pltpu.make_async_copy(chunk_block(block, chunk), chunk_block(out_ref, chunk), out_sems.at[chunk])
+        )
+        leave[-1].start()
+    for copy in leave:
+        copy.wait()
+
+
+def unpack_kernel(in_ref, pot_ref, vel_ref, rows, sems):
+    leave = []
+    for chunk in range(PER // CHUNK):
+        for field, ref in enumerate((pot_ref, vel_ref)):
+            for peer, side, plane in planes():
+                rows[field, pl.ds(chunk * CHUNK * 32 + plane, CHUNK, stride=32), :] = in_ref[
+                    peer, side, field, pl.ds(chunk * CHUNK, CHUNK)
+                ]
+            leave.append(
+                pltpu.make_async_copy(
+                    rows.at[field, chunk_rows(chunk)], ref.at[chunk_rows(chunk)], sems.at[field, chunk]
+                )
+            )
+            leave[-1].start()
+    for copy in leave:
+        copy.wait()
+
+
+def moved(body, out_shapes, args, in_space, scratch):
+    if in_space == pltpu.HBM:
+        args = [pltpu.with_memory_space_constraint(a, in_space) for a in args]
     return pl.pallas_call(
         body,
-        grid=(PER // CHUNK,),
         out_shape=[pltpu.HBM(a.shape, a.dtype) for a in out_shapes],
-        in_specs=[spec(a.shape) for a in args],
-        out_specs=[spec(a.shape) for a in out_shapes],
+        in_specs=[pl.BlockSpec(memory_space=in_space)] * len(args),
+        out_specs=[pl.BlockSpec(memory_space=pltpu.HBM)] * len(out_shapes),
+        scratch_shapes=scratch,
         compiler_params=pltpu.CompilerParams(vmem_limit_bytes=VMEM_BYTES),
         cost_estimate=pl.CostEstimate(flops=0, bytes_accessed=1 << 21, transcendentals=0),
     )(*args)
@@ -258,7 +300,15 @@
     plane = shape((2 * K, NR), F32)
     opening = shape((2 * K + 8, NR), F32)
     tiles = shape((2, 2, 8, NR), F32)
-    (sent,) = by_mode(pack_kernel, [block], [a.reshape(-1, NR) for a in (pot, vel)])
+    rows = pltpu.VMEM((2, 32 * PER, NR), F32)
+    sems = pltpu.SemaphoreType.DMA((2, PER // CHUNK))
+    (sent,) = moved(
+        pack_kernel,
+        [block],
+        [a.reshape(-1, NR) for a in (pot, vel)],
+        pltpu.HBM,
+        [rows, pltpu.VMEM(block.shape, F32), sems, pltpu.SemaphoreType.DMA((PER // CHUNK,))],
+    )
     sent, factors = lax.optimization_barrier((sent, factors))
     got = lax.all_to_all(sent, "modes", split_axis=0, concat_axis=0, tiled=True)
     factor, coef = call(
@@ -292,7 +342,7 @@
         pasts, rims = [*outs[4:6], edge], coming
     (sent,) = call(last_kernel, [block], [*parts, *olds, *rims, *pasts], 0)
     got = lax.all_to_all(sent, "modes", split_axis=0, concat_axis=0, tiled=True)
-    outs = by_mode(unpack_kernel, [shape((32 * PER, NR), F32)] * 2, [got])
+    outs = moved(unpack_kernel, [shape((32 * PER, NR), F32)] * 2, [got], pltpu.VMEM, [rows, sems])
     return tuple(a.reshape(PER, 32, NR) for a in outs)
 
 

time: 111 us -> 107 us (0.964)
  Pallas kernels: 17 us -> 13.2 us
    pallas_call x2, Pallas kernels: 7.52 us -> 3.75 us  [moved(): pl.pallas_call(body, out_shape=[pltpu.HBM(a.shape, a.dtype) for a in out_...]
  transfers between devices with their start and end apart: 9 -> 9, of which waited for: 3 -> 3; matrix products, arithmetic and copies ran while one was open for 0% -> 0% of each run, Pallas kernels for 7% -> 8%
where the time goes in v2:
time: 107 us; the launch traced here: 105 us
  starting transfers between devices  32.9 us (31%)
  waiting for transfers between devices  30.5 us (29%)
  blocking collectives  23.4 us (22%)
  Pallas kernels  13.2 us (12%)
  local copies, waits for them, and re-layouts  4.25 us (4%)
    all_to_all x1, blocking collectives, on_device(): got = lax.all_to_all(sent, 'modes', split_axis=0, concat_axis=0, tiled=True)  23.4 us
    ppermute x4, waiting for transfers between devices, swap(): lax.ppermute(planes[0], AXES, outer_pairs)  17.8 us
    ppermute x4, starting transfers between devices, swap(): lax.ppermute(planes[1], AXES, inner_pairs)  13.7 us
    ppermute x4, starting transfers between devices, swap(): lax.ppermute(planes[0], AXES, outer_pairs)  13 us
    all_to_all x1, waiting for transfers between devices, on_device(): got = lax.all_to_all(sent, 'modes', split_axis=0, concat_axis=0, tiled=True)  12.7 us
    pallas_call x7, Pallas kernels, call(): pl.pallas_call(body, out_shape=out_shapes, in_specs=space, out_specs=[pl....  9.49 us
    all_to_all x1, starting transfers between devices, on_device(): got = lax.all_to_all(sent, 'modes', split_axis=0, concat_axis=0, tiled=True)  6.2 us
    unnamed x12, local copies, waits for them, and re-layouts  4.25 us
  transfers between devices with their start and end apart: 9, of which 3 were waited for; matrix products, arithmetic and copies ran while one was open for 0% of the time, Pallas kernels for 8%

profile of v2, /device:TPU:104, one launch (start us, length us, event | category | flops | bytes accessed | tf_op | source)
XLA Modules:
  0.0 105.2 jit_solution(10251312259444086783)
XLA Ops:
  0.6 0.0 copy-start.5
  0.6 2.4 %shard_map.95 = f32[16,2,2,32,128]{4,3,2,1,0:T(8,128)} custom-call(f32[1024,128]{1,0:T(8,128)} %bitcast.14, f32[1024,128]{1,0:T(8,128)} %bitcast.15), custom_call_target="tpu_custom_call" | custom-call | bytes 2097152 | tf_op jit(solution)/shard_map/pallas_call | solution.py:122
  3.1 6.2 %all-to-all-start = ((f32[16,2,2,32,128]{4,3,2,1,0:T(8,128)}), f32[16,2,2,32,128]{4,3,2,1,0:T(8,128)}, u32[]{:S(2)}, u32[]{:S(2)}) async-start(f32[16,2,2,32,128]{4,3,2,1,0:T(8,128)} %shard_map.95), calls=%async_computation | async-start | bytes 2097152 | tf_op jit(solution)/shard_map/all_to_all | solution.py:313
  9.3 0.0 copy-start
  9.3 0.1 pad_add_fusion.core_ref
  9.4 0.0 copy-done.5
  9.4 0.0 copy-start.1
  9.4 1.1 %copy-done.1 = f32[512,2,128]{2,1,0:T(2,128)S(1)} copy-done((f32[512,2,128]{2,1,0:T(2,128)S(1)}, f32[512,2,128]{2,1,0:T(2,128)}, u32[]{:S(2)}) %copy-start.1) | copy-done | bytes 524312
  10.5 0.0 copy-start.2
  10.5 1.0 copy-done.2
  11.5 0.0 copy-start.3
  11.5 1.0 copy-done.3
  12.6 0.0 copy-start.4
  12.6 1.0 copy-done.4
  13.6 1.0 shard_map.96
  14.6 12.7 %all-to-all-done.in_ref = f32[16,2,2,32,128]{4,3,2,1,0:T(8,128)} async-done(((f32[16,2,2,32,128]{4,3,2,1,0:T(8,128)}), f32[16,2,2,32,128]{4,3,2,1,0:T(8,128)}, u32[]{:S(2)}, u32[]{:S(2)}) %all-to-all-start) | async-done | bytes 1048608 | tf_op jit(solution)/shard_map/all_to_all | solution.py:313
  27.3 1.3 %shard_map.97 = (f32[1032,128]{1,0:T(8,128)S(1)}, f32[1032,128]{1,0:T(8,128)S(1)}) custom-call(s32[2]{0:T(128)S(1)} %pad_add_fusion.core_ref, f32[16,2,2,32,128]{4,3,2,1,0:T(8,128)} %all-to-all-done.in_ref, f32[32,128]{1,0:T(8,128)S(1)} %copy-done.5), custom_call_target="tpu_custom_call" | custom-call | bytes 2121736 | tf_op jit(solution)/shard_map/pallas_call | solution.py:46
  28.6 1.9 %collective-permute-start = (f32[1032,128]{1,0:T(8,128)S(1)}, f32[1032,128]{1,0:T(8,128)S(1)}, u32[]{:S(2)}, u32[]{:S(2)}) collective-permute-start(f32[1032,128]{1,0:T(8,128)S(1)} %get-tuple-element.45.outer.refs_2_), channel_id=1, source_target_pairs={{16,32},{32,16},{48,64},{64,48},{80,96},{96,80},{112,128},{128,112... | collective-permute-start | bytes 1585160 | tf_op jit(solution)/shard_map/ppermute | solution.py:327
  30.6 0.6 collective-permute-start.1
  31.2 0.0 copy-done
  31.2 1.6 %shard_map.98 = (f32[1024,128]{1,0:T(8,128)S(1)}, f32[1024,128]{1,0:T(8,128)S(1)}) custom-call(f32[1032,128]{1,0:T(8,128)S(1)} %get-tuple-element.45.outer.refs_2_, f32[1032,128]{1,0:T(8,128)S(1)} %get-tuple-element.46.inner.refs_3_, f32[4,2,512,128]{3,2,1,0:T(8,128)S(1)} %get-tuple-element.47.factor_ref.refs_6_.refs_9_, bf16[3,256,768]{2,1,0:T(8,128)(2,1)S(1)} %copy-done, ...), custom_call_target="tpu_custom_call" | custom-call | flops 805306368 | bytes 5398528 | tf_op jit(solution)/shard_map/pallas_call | solution.py:46
  32.8 5.2 %collective-permute-start.2 = (f32[1024,128]{1,0:T(8,128)S(1)}, f32[1024,128]{1,0:T(8,128)S(1)}, u32[]{:S(2)}, u32[]{:S(2)}) collective-permute-start(f32[1024,128]{1,0:T(8,128)S(1)} %get-tuple-element.49.refs_0_), channel_id=1, source_target_pairs={{16,32},{32,16},{48,64},{64,48},{80,96},{96,80},{112,128},{128,112... | collective-permute-start | bytes 1572872 | tf_op jit(solution)/shard_map/ppermute | solution.py:327
  38.0 0.1 collective-permute-start.3
  38.1 7.1 %collective-permute-done.refs_4_ = f32[1032,128]{1,0:T(8,128)S(1)} collective-permute-done((f32[1032,128]{1,0:T(8,128)S(1)}, f32[1032,128]{1,0:T(8,128)S(1)}, u32[]{:S(2)}, u32[]{:S(2)}) %collective-permute-start) | collective-permute-done | bytes 528416 | tf_op jit(solution)/shard_map/ppermute | solution.py:327
  45.3 0.0 collective-permute-done.1.refs_5_
  45.3 1.7 %shard_map.99 = (f32[1024,128]{1,0:T(8,128)S(1)}, f32[1024,128]{1,0:T(8,128)S(1)}, f32[1024,128]{1,0:T(8,128)S(1)}, f32[1024,128]{1,0:T(8,128)S(1)}, f32[1024,12...) custom-call(f32[1024,128]{1,0:T(8,128)S(1)} %get-tuple-element.49.refs_0_, ...), custom_call_target="tpu_custom_call" | custom-call | flops 805306368 | bytes 9609216 | tf_op jit(solution)/shard_map/pallas_call | solution.py:46
  47.0 1.9 %collective-permute-start.4 = (f32[1024,128]{1,0:T(8,128)S(1)}, f32[1024,128]{1,0:T(8,128)S(1)}, u32[]{:S(2)}, u32[]{:S(2)}) collective-permute-start(f32[1024,128]{1,0:T(8,128)S(1)} %get-tuple-element.51.refs_0_), channel_id=1, source_target_pairs={{16,32},{32,16},{48,64},{64,48},{80,96},{96,80},{112,128},{128,112... | collective-permute-start | bytes 1572872 | tf_op jit(solution)/shard_map/ppermute | solution.py:327
  48.9 12.9 %collective-permute-start.5 = (f32[1024,128]{1,0:T(8,128)S(1)}, f32[1024,128]{1,0:T(8,128)S(1)}, u32[]{:S(2)}, u32[]{:S(2)}) collective-permute-start(f32[1024,128]{1,0:T(8,128)S(1)} %get-tuple-element.52.refs_1_), channel_id=1, source_target_pairs={{0,16},{16,0},{32,48},{48,32},{64,80},{80,64},{96,112},{112,96},{1... | collective-permute-start | bytes 1572872 | tf_op jit(solution)/shard_map/ppermute | solution.py:327
  61.9 0.0 collective-permute-done.2.refs_4_
  61.9 0.0 collective-permute-done.3.refs_5_
  61.9 1.9 %shard_map.100 = (f32[1024,128]{1,0:T(8,128)S(1)}, f32[1024,128]{1,0:T(8,128)S(1)}, f32[1024,128]{1,0:T(8,128)S(1)}, f32[1024,128]{1,0:T(8,128)S(1)}, f32[1024,128]{1,0:T(8,128)S(1)}, /*index=5*/f32[1024,128]{1,0:T(8,128)S(1)}) custom-call(f32[1024,128]{1,0:T(8,128)S(1)} %get-tuple-element.51.refs_0_, f32[1024,128]{1,0:T(8,128)S(1)} %get-tuple-element.52.refs_1_, ...), custom_call_target="tpu_custom_call" | custom-call | flops 805306368 | bytes 10641408 | tf_op jit(solution)/shard_map/pallas_call | solution.py:46
  63.7 3.9 %collective-permute-start.6 = (f32[1024,128]{1,0:T(8,128)S(1)}, f32[1024,128]{1,0:T(8,128)S(1)}, u32[]{:S(2)}, u32[]{:S(2)}) collective-permute-start(f32[1024,128]{1,0:T(8,128)S(1)} %get-tuple-element.58.refs_0_), channel_id=1, source_target_pairs={{16,32},{32,16},{48,64},{64,48},{80,96},{96,80},{112,128},{128,112... | collective-permute-start | bytes 1572872 | tf_op jit(solution)/shard_map/ppermute | solution.py:327
  67.6 0.1 collective-permute-start.7
  67.7 0.0 collective-permute-done.4.refs_4_
  67.8 0.0 collective-permute-done.5.refs_5_
  67.8 1.9 %shard_map.101 = (f32[1024,128]{1,0:T(8,128)S(1)}, f32[1024,128]{1,0:T(8,128)S(1)}, f32[1024,128]{1,0:T(8,128)S(1)}, f32[1024,128]{1,0:T(8,128)S(1)}, f32[1024,128]{1,0:T(8,128)S(1)}, /*index=5*/f32[1024,128]{1,0:T(8,128)S(1)}) custom-call(f32[1024,128]{1,0:T(8,128)S(1)} %get-tuple-element.58.refs_0_, f32[1024,128]{1,0:T(8,128)S(1)} %get-tuple-element.59.refs_1_, ...), custom_call_target="tpu_custom_call" | custom-call | flops 805306368 | bytes 10641408 | tf_op jit(solution)/shard_map/pallas_call | solution.py:46
  69.6 10.6 %collective-permute-done.6.refs_4_ = f32[1024,128]{1,0:T(8,128)S(1)} collective-permute-done((f32[1024,128]{1,0:T(8,128)S(1)}, f32[1024,128]{1,0:T(8,128)S(1)}, u32[]{:S(2)}, u32[]{:S(2)}) %collective-permute-start.6) | collective-permute-done | bytes 524320 | tf_op jit(solution)/shard_map/ppermute | solution.py:327
  80.3 0.0 collective-permute-done.7.refs_5_
  80.3 0.2 shard_map.102
  80.5 23.4 %all_to_all.10.in_ref = f32[16,2,2,32,128]{4,3,2,1,0:T(8,128)S(1)} all-to-all(f32[16,2,2,32,128]{4,3,2,1,0:T(8,128)S(1)} %shard_map.102), channel_id=1, replica_groups=mesh['modes'=16,'axial'=16] {'modes'}, dimensions={0} | all-to-all | bytes 2097152 | tf_op jit(solution)/shard_map/all_to_all | solution.py:344
  103.9 1.3 %shard_map.103 = (f32[1024,128]{1,0:T(8,128)}, f32[1024,128]{1,0:T(8,128)}) custom-call(f32[16,2,2,32,128]{4,3,2,1,0:T(8,128)S(1)} %all_to_all.10.in_ref), custom_call_target="tpu_custom_call" | custom-call | bytes 2097152 | tf_op jit(solution)/shard_map/pallas_call | solution.py:122
Async XLA Ops:
  0.6 8.8 %copy-start.5 = (f32[32,128]{1,0:T(8,128)S(1)}, f32[32,128]{1,0:T(8,128)}, u32[]{:S(2)}) copy-start(f32[32,128]{1,0:T(8,128)} %diff_ref.3) | copy-start | bytes 49156
  3.1 24.2 %all-to-all-start = ((f32[16,2,2,32,128]{4,3,2,1,0:T(8,128)}), f32[16,2,2,32,128]{4,3,2,1,0:T(8,128)}, u32[]{:S(2)}, u32[]{:S(2)}) async-start(f32[16,2,2,32,128]{4,3,2,1,0:T(8,128)} %shard_map.95), calls=%async_computation | async-start | bytes 2097152 | tf_op jit(solution)/shard_map/all_to_all | solution.py:313
  9.3 21.9 %copy-start = (bf16[3,256,768]{2,1,0:T(8,128)(2,1)S(1)}, bf16[3,256,768]{2,1,0:T(8,128)(2,1)}, u32[]{:S(2)}) copy-start(bf16[3,256,768]{2,1,0:T(8,128)(2,1)} %constant.20.clone.table_ref.refs_7_.refs_10_) | copy-start | bytes 3538948
  9.4 1.1 %copy-start.1 = (f32[512,2,128]{2,1,0:T(2,128)S(1)}, f32[512,2,128]{2,1,0:T(2,128)}, u32[]{:S(2)}) copy-start(f32[512,2,128]{2,1,0:T(2,128)} %param.11) | copy-start | bytes 1572868
  10.5 1.0 copy-start.2
  11.5 1.0 copy-start.3
  12.6 1.0 copy-start.4
  28.6 16.6 %collective-permute-start = (f32[1032,128]{1,0:T(8,128)S(1)}, f32[1032,128]{1,0:T(8,128)S(1)}, u32[]{:S(2)}, u32[]{:S(2)}) collective-permute-start(f32[1032,128]{1,0:T(8,128)S(1)} %get-tuple-element.45.outer.refs_2_), channel_id=1, source_target_pairs={{16,32},{32,16},{48,64},{64,48},{80,96},{96,80},{112,128},{128,112... | collective-permute-start | bytes 1585160 | tf_op jit(solution)/shard_map/ppermute | solution.py:327
  30.6 14.7 %collective-permute-start.1 = (f32[1032,128]{1,0:T(8,128)S(1)}, f32[1032,128]{1,0:T(8,128)S(1)}, u32[]{:S(2)}, u32[]{:S(2)}) collective-permute-start(f32[1032,128]{1,0:T(8,128)S(1)} %get-tuple-element.46.inner.refs_3_), channel_id=1, source_target_pairs={{0,16},{16,0},{32,48},{48,32},{64,80},{80,64},{96,112},{112,96},{1... | collective-permute-start | bytes 1585160 | tf_op jit(solution)/shard_map/ppermute | solution.py:327
  32.8 29.1 %collective-permute-start.2 = (f32[1024,128]{1,0:T(8,128)S(1)}, f32[1024,128]{1,0:T(8,128)S(1)}, u32[]{:S(2)}, u32[]{:S(2)}) collective-permute-start(f32[1024,128]{1,0:T(8,128)S(1)} %get-tuple-element.49.refs_0_), channel_id=1, source_target_pairs={{16,32},{32,16},{48,64},{64,48},{80,96},{96,80},{112,128},{128,112... | collective-permute-start | bytes 1572872 | tf_op jit(solution)/shard_map/ppermute | solution.py:327
  38.0 23.8 %collective-permute-start.3 = (f32[1024,128]{1,0:T(8,128)S(1)}, f32[1024,128]{1,0:T(8,128)S(1)}, u32[]{:S(2)}, u32[]{:S(2)}) collective-permute-start(f32[1024,128]{1,0:T(8,128)S(1)} %get-tuple-element.50.refs_1_), channel_id=1, source_target_pairs={{0,16},{16,0},{32,48},{48,32},{64,80},{80,64},{96,112},{112,96},{1... | collective-permute-start | bytes 1572872 | tf_op jit(solution)/shard_map/ppermute | solution.py:327
  47.0 20.8 %collective-permute-start.4 = (f32[1024,128]{1,0:T(8,128)S(1)}, f32[1024,128]{1,0:T(8,128)S(1)}, u32[]{:S(2)}, u32[]{:S(2)}) collective-permute-start(f32[1024,128]{1,0:T(8,128)S(1)} %get-tuple-element.51.refs_0_), channel_id=1, source_target_pairs={{16,32},{32,16},{48,64},{64,48},{80,96},{96,80},{112,128},{128,112... | collective-permute-start | bytes 1572872 | tf_op jit(solution)/shard_map/ppermute | solution.py:327
  48.9 18.8 %collective-permute-start.5 = (f32[1024,128]{1,0:T(8,128)S(1)}, f32[1024,128]{1,0:T(8,128)S(1)}, u32[]{:S(2)}, u32[]{:S(2)}) collective-permute-start(f32[1024,128]{1,0:T(8,128)S(1)} %get-tuple-element.52.refs_1_), channel_id=1, source_target_pairs={{0,16},{16,0},{32,48},{48,32},{64,80},{80,64},{96,112},{112,96},{1... | collective-permute-start | bytes 1572872 | tf_op jit(solution)/shard_map/ppermute | solution.py:327
  63.7 16.6 %collective-permute-start.6 = (f32[1024,128]{1,0:T(8,128)S(1)}, f32[1024,128]{1,0:T(8,128)S(1)}, u32[]{:S(2)}, u32[]{:S(2)}) collective-permute-start(f32[1024,128]{1,0:T(8,128)S(1)} %get-tuple-element.58.refs_0_), channel_id=1, source_target_pairs={{16,32},{32,16},{48,64},{64,48},{80,96},{96,80},{112,128},{128,112... | collective-permute-start | bytes 1572872 | tf_op jit(solution)/shard_map/ppermute | solution.py:327
  67.6 12.6 %collective-permute-start.7 = (f32[1024,128]{1,0:T(8,128)S(1)}, f32[1024,128]{1,0:T(8,128)S(1)}, u32[]{:S(2)}, u32[]{:S(2)}) collective-permute-start(f32[1024,128]{1,0:T(8,128)S(1)} %get-tuple-element.59.refs_1_), channel_id=1, source_target_pairs={{0,16},{16,0},{32,48},{48,32},{64,80},{80,64},{96,112},{112,96},{1... | collective-permute-start | bytes 1572872 | tf_op jit(solution)/shard_map/ppermute | solution.py:327

commit v3 on v2

--- a/solution.py
+++ b/solution.py
@@ -58,44 +58,32 @@
     return pl.ds(chunk * CHUNK * 32, CHUNK * 32)
 
 
-def chunk_block(ref, chunk):
-    return ref.at[:, :, :, pl.ds(chunk * CHUNK, CHUNK)]
-
-
 def planes():
     for peer in range(PEERS):
         for side in range(2):
             yield peer, side, 2 * peer + (side if peer % 2 == 0 else 1 - side)
 
 
-def pack_kernel(pot_ref, vel_ref, out_ref, rows, block, in_sems, out_sems):
-    chunks = range(PER // CHUNK)
+def pack_kernel(pot_ref, vel_ref, out_ref, rows, sems):
     arrive = [
         [
             pltpu.make_async_copy(
-                ref.at[chunk_rows(chunk)], rows.at[field, chunk_rows(chunk)], in_sems.at[field, chunk]
+                ref.at[chunk_rows(chunk)], rows.at[field, chunk_rows(chunk)], sems.at[field, chunk]
             )
             for field, ref in enumerate((pot_ref, vel_ref))
         ]
-        for chunk in chunks
+        for chunk in range(PER // CHUNK)
     ]
     for pair in arrive:
         for copy in pair:
             copy.start()
-    leave = []
-    for chunk in chunks:
-        for field in range(2):
-            arrive[chunk][field].wait()
+    for chunk, pair in enumerate(arrive):
+        for field, copy in enumerate(pair):
+            copy.wait()
             for peer, side, plane in planes():
-                block[peer, side, field, pl.ds(chunk * CHUNK, CHUNK)] = rows[
+                out_ref[peer, side, field, pl.ds(chunk * CHUNK, CHUNK)] = rows[
                     field, pl.ds(chunk * CHUNK * 32 + plane, CHUNK, stride=32), :
                 ]
-        leave.append(
-            pltpu.make_async_copy(chunk_block(block, chunk), chunk_block(out_ref, chunk), out_sems.at[chunk])
-        )
-        leave[-1].start()
-    for copy in leave:
-        copy.wait()
 
 
 def unpack_kernel(in_ref, pot_ref, vel_ref, rows, sems):
@@ -116,14 +104,16 @@
         copy.wait()
 
 
-def moved(body, out_shapes, args, in_space, scratch):
-    if in_space == pltpu.HBM:
-        args = [pltpu.with_memory_space_constraint(a, in_space) for a in args]
+def moved(body, out_shapes, args, spaces, scratch):
+    if spaces[0] == pltpu.HBM:
+        args = [pltpu.with_memory_space_constraint(a, pltpu.HBM) for a in args]
+    else:
+        out_shapes = [pltpu.HBM(a.shape, a.dtype) for a in out_shapes]
     return pl.pallas_call(
         body,
-        out_shape=[pltpu.HBM(a.shape, a.dtype) for a in out_shapes],
-        in_specs=[pl.BlockSpec(memory_space=in_space)] * len(args),
-        out_specs=[pl.BlockSpec(memory_space=pltpu.HBM)] * len(out_shapes),
+        out_shape=out_shapes,
+        in_specs=[pl.BlockSpec(memory_space=spaces[0])] * len(args),
+        out_specs=[pl.BlockSpec(memory_space=spaces[1])] * len(out_shapes),
         scratch_shapes=scratch,
         compiler_params=pltpu.CompilerParams(vmem_limit_bytes=VMEM_BYTES),
         cost_estimate=pl.CostEstimate(flops=0, bytes_accessed=1 << 21, transcendentals=0),
@@ -300,17 +290,19 @@
     plane = shape((2 * K, NR), F32)
     opening = shape((2 * K + 8, NR), F32)
     tiles = shape((2, 2, 8, NR), F32)
-    rows = pltpu.VMEM((2, 32 * PER, NR), F32)
-    sems = pltpu.SemaphoreType.DMA((2, PER // CHUNK))
-    (sent,) = moved(
-        pack_kernel,
-        [block],
-        [a.reshape(-1, NR) for a in (pot, vel)],
-        pltpu.HBM,
-        [rows, pltpu.VMEM(block.shape, F32), sems, pltpu.SemaphoreType.DMA((PER // CHUNK,))],
-    )
-    sent, factors = lax.optimization_barrier((sent, factors))
+    staging = [pltpu.VMEM((2, 32 * PER, NR), F32), pltpu.SemaphoreType.DMA((2, PER // CHUNK))]
+
+    def swap(planes):
+        return [lax.ppermute(planes[0], AXES, outer_pairs), lax.ppermute(planes[1], AXES, inner_pairs)]
+
+    flat = [a.reshape(-1, NR) for a in (pot, vel)]
+    (sent,) = moved(pack_kernel, [block], flat, (pltpu.HBM, pltpu.VMEM), staging)
+    sent, place = lax.optimization_barrier((sent, place))
     got = lax.all_to_all(sent, "modes", split_axis=0, concat_axis=0, tiled=True)
+    got, place, diffusivity, table = lax.optimization_barrier((got, place, diffusivity, table))
+    start = call(split_kernel, [opening] * 2, [place, got, diffusivity], 0, smem=1)
+    rims = swap(start)
+    start, factors = lax.optimization_barrier((start, factors))
     factor, coef = call(
         factor_kernel,
         [shape((4, 2, K, NR), F32), tiles],
@@ -318,15 +310,8 @@
         0,
         smem=1,
     )
-    got, factor, coef = lax.optimization_barrier((got, factor, coef))
-    start = call(split_kernel, [opening] * 2, [place, got, diffusivity], 0, smem=1)
     shared = [factor, table, coef]
     flops = 8 * 2 * 768 * 256 * 256
-
-    def swap(planes):
-        return [lax.ppermute(planes[0], AXES, outer_pairs), lax.ppermute(planes[1], AXES, inner_pairs)]
-
-    rims = swap(start)
     parts = call(first_kernel, [plane] * 2, [*start, *shared], flops)
     olds, pasts = start, []
     for step in range(1, STEPS):
@@ -342,7 +327,7 @@
         pasts, rims = [*outs[4:6], edge], coming
     (sent,) = call(last_kernel, [block], [*parts, *olds, *rims, *pasts], 0)
     got = lax.all_to_all(sent, "modes", split_axis=0, concat_axis=0, tiled=True)
-    outs = moved(unpack_kernel, [shape((32 * PER, NR), F32)] * 2, [got], pltpu.VMEM, [rows, sems])
+    outs = moved(unpack_kernel, [shape((32 * PER, NR), F32)] * 2, [got], (pltpu.VMEM, pltpu.HBM), staging)
     return tuple(a.reshape(PER, 32, NR) for a in outs)
 
 

time: 107 us -> 105 us (0.981)
  blocking collectives: 23.4 us -> 47.4 us
  waiting for transfers between devices: 30.5 us -> 16.9 us
  starting transfers between devices: 32.9 us -> 26.5 us
  local copies, waits for them, and re-layouts: 4.25 us -> 0.03 us
  Pallas kernels: 13.2 us -> 11.8 us
    all_to_all x1 -> x2, blocking collectives: 23.4 us -> 47.4 us  [on_device(): got = lax.all_to_all(sent, 'modes', split_axis=0, concat_axis=0, tiled=True)]
    all_to_all x1 -> x0, waiting for transfers between devices: 12.7 us -> none  [on_device(): got = lax.all_to_all(sent, 'modes', split_axis=0, concat_axis=0, tiled=True)]
    all_to_all x1 -> x0, starting transfers between devices: 6.2 us -> none  [on_device(): got = lax.all_to_all(sent, 'modes', split_axis=0, concat_axis=0, tiled=True)]
    unnamed x12, local copies, waits for them, and re-layouts: 4.25 us -> 0.03 us
  transfers between devices with their start and end apart: 9 -> 8, of which waited for: 3 -> 2; matrix products, arithmetic and copies ran while one was open for 0% -> 0% of each run, Pallas kernels for 8% -> 8%
where the time goes in v3:
time: 105 us; the launch traced here: 104 us
  blocking collectives  47.4 us (45%)
  starting transfers between devices  26.5 us (25%)
  waiting for transfers between devices  16.9 us (16%)
  Pallas kernels  11.8 us (11%)
    all_to_all x2, blocking collectives, on_device(): got = lax.all_to_all(sent, 'modes', split_axis=0, concat_axis=0, tiled=True)  47.4 us
    ppermute x4, waiting for transfers between devices, swap(): lax.ppermute(planes[0], AXES, outer_pairs)  16.9 us
    ppermute x4, starting transfers between devices, swap(): lax.ppermute(planes[1], AXES, inner_pairs)  13.8 us
    ppermute x4, starting transfers between devices, swap(): lax.ppermute(planes[0], AXES, outer_pairs)  12.7 us
    pallas_call x7, Pallas kernels, call(): pl.pallas_call(body, out_shape=out_shapes, in_specs=space, out_specs=[pl....  8.85 us
    pallas_call x2, Pallas kernels, moved(): pl.pallas_call(body, out_shape=out_shapes, in_specs=[pl.BlockSpec(memory_...  2.96 us
  transfers between devices with their start and end apart: 8, of which 2 were waited for; matrix products, arithmetic and copies ran while one was open for 0% of the time, Pallas kernels for 8%

profile of v3, /device:TPU:104, one launch (start us, length us, event | category | flops | bytes accessed | tf_op | source)
XLA Modules:
  0.0 103.6 jit_solution(1078541353896667364)
XLA Ops:
  0.6 0.1 pad_add_fusion.core_ref
  0.7 0.0 copy-start.5
  0.7 1.6 %shard_map.95 = f32[16,2,2,32,128]{4,3,2,1,0:T(8,128)S(1)} custom-call(f32[1024,128]{1,0:T(8,128)} %bitcast.14, f32[1024,128]{1,0:T(8,128)} %bitcast.15), custom_call_target="tpu_custom_call" | custom-call | bytes 2097152 | tf_op jit(solution)/shard_map/pallas_call | solution.py:112
  2.4 0.0 copy-start.1
  2.4 0.0 copy-start.2
  2.4 0.0 copy-start.3
  2.4 0.0 copy-start.4
  2.4 24.0 %all_to_all.10.in_ref = f32[16,2,2,32,128]{4,3,2,1,0:T(8,128)S(1)} all-to-all(f32[16,2,2,32,128]{4,3,2,1,0:T(8,128)S(1)} %shard_map.95), channel_id=1, replica_groups=mesh['modes'=16,'axial'=16] {'modes'}, dimensions={0} | all-to-all | bytes 2097152 | tf_op jit(solution)/shard_map/all_to_all | solution.py:301
  26.5 0.0 copy-done.5
  26.5 0.0 copy-start
  26.5 0.6 shard_map.96
  27.1 1.9 %collective-permute-start = (f32[1032,128]{1,0:T(8,128)S(1)}, f32[1032,128]{1,0:T(8,128)S(1)}, u32[]{:S(2)}, u32[]{:S(2)}) collective-permute-start(f32[1032,128]{1,0:T(8,128)S(1)} %get-tuple-element.48.outer.refs_2_), channel_id=1, source_target_pairs={{16,32},{32,16},{48,64},{64,48},{80,96},{96,80},{112,128},{128,112... | collective-permute-start | bytes 1585160 | tf_op jit(solution)/shard_map/ppermute | solution.py:296
  29.0 0.6 collective-permute-start.1
  29.6 0.0 copy-done.1
  29.6 0.0 copy-done.2
  29.6 0.0 copy-done.3
  29.6 0.0 copy-done.4
  29.6 1.0 shard_map.97
  30.6 0.0 copy-done
  30.6 1.6 %shard_map.98 = (f32[1024,128]{1,0:T(8,128)S(1)}, f32[1024,128]{1,0:T(8,128)S(1)}) custom-call(f32[1032,128]{1,0:T(8,128)S(1)} %get-tuple-element.48.outer.refs_2_, f32[1032,128]{1,0:T(8,128)S(1)} %get-tuple-element.49.inner.refs_3_, f32[4,2,512,128]{3,2,1,0:T(8,128)S(1)} %get-tuple-element.54.factor_ref.refs_6_.refs_9_, bf16[3,256,768]{2,1,0:T(8,128)(2,1)S(1)} %copy-done, ...), custom_call_target="tpu_custom_call" | custom-call | flops 805306368 | bytes 5398528 | tf_op jit(solution)/shard_map/pallas_call | solution.py:46
  32.2 5.3 %collective-permute-start.2 = (f32[1024,128]{1,0:T(8,128)S(1)}, f32[1024,128]{1,0:T(8,128)S(1)}, u32[]{:S(2)}, u32[]{:S(2)}) collective-permute-start(f32[1024,128]{1,0:T(8,128)S(1)} %get-tuple-element.57.refs_0_), channel_id=1, source_target_pairs={{16,32},{32,16},{48,64},{64,48},{80,96},{96,80},{112,128},{128,112... | collective-permute-start | bytes 1572872 | tf_op jit(solution)/shard_map/ppermute | solution.py:296
  37.6 0.1 collective-permute-start.3
  37.7 6.1 %collective-permute-done.refs_4_ = f32[1032,128]{1,0:T(8,128)S(1)} collective-permute-done((f32[1032,128]{1,0:T(8,128)S(1)}, f32[1032,128]{1,0:T(8,128)S(1)}, u32[]{:S(2)}, u32[]{:S(2)}) %collective-permute-start) | collective-permute-done | bytes 528416 | tf_op jit(solution)/shard_map/ppermute | solution.py:296
  43.7 0.0 collective-permute-done.1.refs_5_
  43.7 1.8 %shard_map.99 = (f32[1024,128]{1,0:T(8,128)S(1)}, f32[1024,128]{1,0:T(8,128)S(1)}, f32[1024,128]{1,0:T(8,128)S(1)}, f32[1024,128]{1,0:T(8,128)S(1)}, f32[1024,12...) custom-call(f32[1024,128]{1,0:T(8,128)S(1)} %get-tuple-element.57.refs_0_, ...), custom_call_target="tpu_custom_call" | custom-call | flops 805306368 | bytes 9609216 | tf_op jit(solution)/shard_map/pallas_call | solution.py:46
  45.5 1.9 %collective-permute-start.4 = (f32[1024,128]{1,0:T(8,128)S(1)}, f32[1024,128]{1,0:T(8,128)S(1)}, u32[]{:S(2)}, u32[]{:S(2)}) collective-permute-start(f32[1024,128]{1,0:T(8,128)S(1)} %get-tuple-element.59.refs_0_), channel_id=1, source_target_pairs={{16,32},{32,16},{48,64},{64,48},{80,96},{96,80},{112,128},{128,112... | collective-permute-start | bytes 1572872 | tf_op jit(solution)/shard_map/ppermute | solution.py:296
  47.4 12.9 %collective-permute-start.5 = (f32[1024,128]{1,0:T(8,128)S(1)}, f32[1024,128]{1,0:T(8,128)S(1)}, u32[]{:S(2)}, u32[]{:S(2)}) collective-permute-start(f32[1024,128]{1,0:T(8,128)S(1)} %get-tuple-element.60.refs_1_), channel_id=1, source_target_pairs={{0,16},{16,0},{32,48},{48,32},{64,80},{80,64},{96,112},{112,96},{1... | collective-permute-start | bytes 1572872 | tf_op jit(solution)/shard_map/ppermute | solution.py:296
  60.3 0.0 collective-permute-done.2.refs_4_
  60.3 0.0 collective-permute-done.3.refs_5_
  60.3 1.8 %shard_map.100 = (f32[1024,128]{1,0:T(8,128)S(1)}, f32[1024,128]{1,0:T(8,128)S(1)}, f32[1024,128]{1,0:T(8,128)S(1)}, f32[1024,128]{1,0:T(8,128)S(1)}, f32[1024,128]{1,0:T(8,128)S(1)}, /*index=5*/f32[1024,128]{1,0:T(8,128)S(1)}) custom-call(f32[1024,128]{1,0:T(8,128)S(1)} %get-tuple-element.59.refs_0_, f32[1024,128]{1,0:T(8,128)S(1)} %get-tuple-element.60.refs_1_, ...), custom_call_target="tpu_custom_call" | custom-call | flops 805306368 | bytes 10641408 | tf_op jit(solution)/shard_map/pallas_call | solution.py:46
  62.1 3.6 %collective-permute-start.6 = (f32[1024,128]{1,0:T(8,128)S(1)}, f32[1024,128]{1,0:T(8,128)S(1)}, u32[]{:S(2)}, u32[]{:S(2)}) collective-permute-start(f32[1024,128]{1,0:T(8,128)S(1)} %get-tuple-element.66.refs_0_), channel_id=1, source_target_pairs={{16,32},{32,16},{48,64},{64,48},{80,96},{96,80},{112,128},{128,112... | collective-permute-start | bytes 1572872 | tf_op jit(solution)/shard_map/ppermute | solution.py:296
  65.7 0.2 collective-permute-start.7
  66.0 0.0 collective-permute-done.4.refs_4_
  66.0 0.0 collective-permute-done.5.refs_5_
  66.0 1.9 %shard_map.101 = (f32[1024,128]{1,0:T(8,128)S(1)}, f32[1024,128]{1,0:T(8,128)S(1)}, f32[1024,128]{1,0:T(8,128)S(1)}, f32[1024,128]{1,0:T(8,128)S(1)}, f32[1024,128]{1,0:T(8,128)S(1)}, /*index=5*/f32[1024,128]{1,0:T(8,128)S(1)}) custom-call(f32[1024,128]{1,0:T(8,128)S(1)} %get-tuple-element.66.refs_0_, f32[1024,128]{1,0:T(8,128)S(1)} %get-tuple-element.67.refs_1_, ...), custom_call_target="tpu_custom_call" | custom-call | flops 805306368 | bytes 10641408 | tf_op jit(solution)/shard_map/pallas_call | solution.py:46
  67.8 10.8 %collective-permute-done.6.refs_4_ = f32[1024,128]{1,0:T(8,128)S(1)} collective-permute-done((f32[1024,128]{1,0:T(8,128)S(1)}, f32[1024,128]{1,0:T(8,128)S(1)}, u32[]{:S(2)}, u32[]{:S(2)}) %collective-permute-start.6) | collective-permute-done | bytes 524320 | tf_op jit(solution)/shard_map/ppermute | solution.py:296
  78.7 0.0 collective-permute-done.7.refs_5_
  78.7 0.2 shard_map.102
  78.9 23.4 %all_to_all.11.in_ref = f32[16,2,2,32,128]{4,3,2,1,0:T(8,128)S(1)} all-to-all(f32[16,2,2,32,128]{4,3,2,1,0:T(8,128)S(1)} %shard_map.102), channel_id=1, replica_groups=mesh['modes'=16,'axial'=16] {'modes'}, dimensions={0} | all-to-all | bytes 2097152 | tf_op jit(solution)/shard_map/all_to_all | solution.py:329
  102.2 1.3 %shard_map.103 = (f32[1024,128]{1,0:T(8,128)}, f32[1024,128]{1,0:T(8,128)}) custom-call(f32[16,2,2,32,128]{4,3,2,1,0:T(8,128)S(1)} %all_to_all.11.in_ref), custom_call_target="tpu_custom_call" | custom-call | bytes 2097152 | tf_op jit(solution)/shard_map/pallas_call | solution.py:112
Async XLA Ops:
  0.7 25.7 %copy-start.5 = (f32[32,128]{1,0:T(8,128)S(1)}, f32[32,128]{1,0:T(8,128)}, u32[]{:S(2)}) copy-start(f32[32,128]{1,0:T(8,128)} %diff_ref.1) | copy-start | bytes 49156
  2.4 27.2 %copy-start.1 = (f32[512,2,128]{2,1,0:T(2,128)S(1)}, f32[512,2,128]{2,1,0:T(2,128)}, u32[]{:S(2)}) copy-start(f32[512,2,128]{2,1,0:T(2,128)} %param.11) | copy-start | bytes 1572868
  2.4 27.2 %copy-start.2 = (f32[512,2,128]{2,1,0:T(2,128)S(1)}, f32[512,2,128]{2,1,0:T(2,128)}, u32[]{:S(2)}) copy-start(f32[512,2,128]{2,1,0:T(2,128)} %param.12) | copy-start | bytes 1572868
  2.4 27.2 %copy-start.3 = (f32[512,2,128]{2,1,0:T(2,128)S(1)}, f32[512,2,128]{2,1,0:T(2,128)}, u32[]{:S(2)}) copy-start(f32[512,2,128]{2,1,0:T(2,128)} %param.13) | copy-start | bytes 1572868
  2.4 27.2 %copy-start.4 = (f32[512,2,128]{2,1,0:T(2,128)S(1)}, f32[512,2,128]{2,1,0:T(2,128)}, u32[]{:S(2)}) copy-start(f32[512,2,128]{2,1,0:T(2,128)} %param.14) | copy-start | bytes 1572868
  26.5 4.1 %copy-start = (bf16[3,256,768]{2,1,0:T(8,128)(2,1)S(1)}, bf16[3,256,768]{2,1,0:T(8,128)(2,1)}, u32[]{:S(2)}) copy-start(bf16[3,256,768]{2,1,0:T(8,128)(2,1)} %constant.20.clone.table_ref.refs_7_.refs_10_) | copy-start | bytes 3538948
  27.1 16.6 %collective-permute-start = (f32[1032,128]{1,0:T(8,128)S(1)}, f32[1032,128]{1,0:T(8,128)S(1)}, u32[]{:S(2)}, u32[]{:S(2)}) collective-permute-start(f32[1032,128]{1,0:T(8,128)S(1)} %get-tuple-element.48.outer.refs_2_), channel_id=1, source_target_pairs={{16,32},{32,16},{48,64},{64,48},{80,96},{96,80},{112,128},{128,112... | collective-permute-start | bytes 1585160 | tf_op jit(solution)/shard_map/ppermute | solution.py:296
  29.0 14.7 %collective-permute-start.1 = (f32[1032,128]{1,0:T(8,128)S(1)}, f32[1032,128]{1,0:T(8,128)S(1)}, u32[]{:S(2)}, u32[]{:S(2)}) collective-permute-start(f32[1032,128]{1,0:T(8,128)S(1)} %get-tuple-element.49.inner.refs_3_), channel_id=1, source_target_pairs={{0,16},{16,0},{32,48},{48,32},{64,80},{80,64},{96,112},{112,96},{1... | collective-permute-start | bytes 1585160 | tf_op jit(solution)/shard_map/ppermute | solution.py:296
  32.2 28.1 %collective-permute-start.2 = (f32[1024,128]{1,0:T(8,128)S(1)}, f32[1024,128]{1,0:T(8,128)S(1)}, u32[]{:S(2)}, u32[]{:S(2)}) collective-permute-start(f32[1024,128]{1,0:T(8,128)S(1)} %get-tuple-element.57.refs_0_), channel_id=1, source_target_pairs={{16,32},{32,16},{48,64},{64,48},{80,96},{96,80},{112,128},{128,112... | collective-permute-start | bytes 1572872 | tf_op jit(solution)/shard_map/ppermute | solution.py:296
  37.6 22.7 %collective-permute-start.3 = (f32[1024,128]{1,0:T(8,128)S(1)}, f32[1024,128]{1,0:T(8,128)S(1)}, u32[]{:S(2)}, u32[]{:S(2)}) collective-permute-start(f32[1024,128]{1,0:T(8,128)S(1)} %get-tuple-element.58.refs_1_), channel_id=1, source_target_pairs={{0,16},{16,0},{32,48},{48,32},{64,80},{80,64},{96,112},{112,96},{1... | collective-permute-start | bytes 1572872 | tf_op jit(solution)/shard_map/ppermute | solution.py:296
  45.5 20.5 %collective-permute-start.4 = (f32[1024,128]{1,0:T(8,128)S(1)}, f32[1024,128]{1,0:T(8,128)S(1)}, u32[]{:S(2)}, u32[]{:S(2)}) collective-permute-start(f32[1024,128]{1,0:T(8,128)S(1)} %get-tuple-element.59.refs_0_), channel_id=1, source_target_pairs={{16,32},{32,16},{48,64},{64,48},{80,96},{96,80},{112,128},{128,112... | collective-permute-start | bytes 1572872 | tf_op jit(solution)/shard_map/ppermute | solution.py:296
  47.4 18.6 %collective-permute-start.5 = (f32[1024,128]{1,0:T(8,128)S(1)}, f32[1024,128]{1,0:T(8,128)S(1)}, u32[]{:S(2)}, u32[]{:S(2)}) collective-permute-start(f32[1024,128]{1,0:T(8,128)S(1)} %get-tuple-element.60.refs_1_), channel_id=1, source_target_pairs={{0,16},{16,0},{32,48},{48,32},{64,80},{80,64},{96,112},{112,96},{1... | collective-permute-start | bytes 1572872 | tf_op jit(solution)/shard_map/ppermute | solution.py:296
  62.1 16.6 %collective-permute-start.6 = (f32[1024,128]{1,0:T(8,128)S(1)}, f32[1024,128]{1,0:T(8,128)S(1)}, u32[]{:S(2)}, u32[]{:S(2)}) collective-permute-start(f32[1024,128]{1,0:T(8,128)S(1)} %get-tuple-element.66.refs_0_), channel_id=1, source_target_pairs={{16,32},{32,16},{48,64},{64,48},{80,96},{96,80},{112,128},{128,112... | collective-permute-start | bytes 1572872 | tf_op jit(solution)/shard_map/ppermute | solution.py:296
  65.7 13.0 %collective-permute-start.7 = (f32[1024,128]{1,0:T(8,128)S(1)}, f32[1024,128]{1,0:T(8,128)S(1)}, u32[]{:S(2)}, u32[]{:S(2)}) collective-permute-start(f32[1024,128]{1,0:T(8,128)S(1)} %get-tuple-element.67.refs_1_), channel_id=1, source_target_pairs={{0,16},{16,0},{32,48},{48,32},{64,80},{80,64},{96,112},{112,96},{1... | collective-permute-start | bytes 1572872 | tf_op jit(solution)/shard_map/ppermute | solution.py:296

commit v4 on v3

--- a/solution.py
+++ b/solution.py
@@ -58,10 +58,12 @@
     return pl.ds(chunk * CHUNK * 32, CHUNK * 32)
 
 
-def planes():
+def planes(sides):
     for peer in range(PEERS):
-        for side in range(2):
-            yield peer, side, 2 * peer + (side if peer % 2 == 0 else 1 - side)
+        order = (0, 1, -1) if peer % 2 == 0 else (1, 0, 2)
+        for side in range(sides):
+            plane = 2 * peer + order[side]
+            yield peer, side, plane if 0 <= plane < 2 * PEERS else None
 
 
 def pack_kernel(pot_ref, vel_ref, out_ref, rows, sems):
@@ -80,17 +82,19 @@
     for chunk, pair in enumerate(arrive):
         for field, copy in enumerate(pair):
             copy.wait()
-            for peer, side, plane in planes():
-                out_ref[peer, side, field, pl.ds(chunk * CHUNK, CHUNK)] = rows[
-                    field, pl.ds(chunk * CHUNK * 32 + plane, CHUNK, stride=32), :
-                ]
+            for peer, side, plane in planes(3):
+                if plane is None:
+                    piece = jnp.zeros((CHUNK, NR), F32)
+                else:
+                    piece = rows[field, pl.ds(chunk * CHUNK * 32 + plane, CHUNK, stride=32), :]
+                out_ref[peer, side, field, pl.ds(chunk * CHUNK, CHUNK)] = piece
 
 
 def unpack_kernel(in_ref, pot_ref, vel_ref, rows, sems):
     leave = []
     for chunk in range(PER // CHUNK):
         for field, ref in enumerate((pot_ref, vel_ref)):
-            for peer, side, plane in planes():
+            for peer, side, plane in planes(2):
                 rows[field, pl.ds(chunk * CHUNK * 32 + plane, CHUNK, stride=32), :] = in_ref[
                     peer, side, field, pl.ds(chunk * CHUNK, CHUNK)
                 ]
@@ -120,19 +124,21 @@
     )(*args)
 
 
-def split_kernel(core_ref, in_ref, diff_ref, out_outer, out_inner):
-    for side, out in enumerate((out_outer, out_inner)):
+def split_kernel(core_ref, in_ref, diff_ref, *outs):
+    row = lax.broadcasted_iota(jnp.int32, (8, NR), 0)
+    for side, out in enumerate(outs):
         for src in range(PEERS):
             for field in range(2):
                 out[pl.ds(field * K + src * PER, PER), :] = in_ref[src, side, field]
-        own = near(core_ref, diff_ref, side)
-        row = lax.broadcasted_iota(jnp.int32, (8, NR), 0)
-        out[pl.ds(2 * K, 8), :] = jnp.where(row == 0, jnp.broadcast_to(own, (8, NR)), 1.0)
+        own = jnp.where(row == 0, jnp.broadcast_to(near(core_ref, diff_ref, side), (8, NR)), 1.0)
+        if side == 2:
+            own = jnp.where(jnp.full((8, NR), core_ref[2], jnp.int32) == 1, own, 0.0)
+        out[pl.ds(2 * K, 8), :] = own
 
 
 def near(core_ref, diff_ref, side):
-    plane = core_ref[1] + (core_ref[0] if side == 0 else 1 - core_ref[0])
-    return diff_ref[pl.ds(plane, 1), :]
+    at = (core_ref[0], 1 - core_ref[0], core_ref[3])[side]
+    return diff_ref[pl.ds(core_ref[1] + at, 1), :]
 
 
 def factor_kernel(core_ref, diff_ref, *refs):
@@ -198,20 +204,25 @@
     refs = list(refs)
     take = lambda n: [refs.pop(0) for _ in range(n)]
     parts, olds, rims = take(2), take(2), take(2)
-    pasts, edge_ref = ((None, None), None) if opening else (take(2), take(1)[0])
+    if opening:
+        (beyond,) = take(1)
+        coming = [lambda rows: rims[0][rows, :] + beyond[rows, :], lambda rows: rims[1][rows, :]]
+    else:
+        pasts, (edge_ref,) = take(2), take(1)
+        coming = [lambda rows, rim=rim: rim[rows, :] for rim in rims]
     factor_ref, table_ref, coef_ref = take(3)
     outs, fulls, fluxes = take(2), take(2), take(2)
     if opening:
         (edge_ref,) = take(1)
         for side in range(2):
-            own, other = (ref[pl.ds(2 * K, 8), :] for ref in (olds[side], rims[side]))
+            own, other = olds[side][pl.ds(2 * K, 8), :], coming[side](pl.ds(2 * K, 8))
             row = lax.broadcasted_iota(jnp.int32, (8, NR), 0)
             edge_ref[side] = jnp.where(row < 2, DT * 0.5 * (own + other), other)
     for side in range(2):
         for field in range(2):
             rows = field_rows(field)
             past = None if opening else pasts[side][rows, :]
-            flow = flux(edge_ref, side, field, rims[side][rows, :], olds[side][rows, :], past)
+            flow = flux(edge_ref, side, field, coming[side](rows), olds[side][rows, :], past)
             fluxes[side][rows, :] = flow
             fulls[side][rows, :] = parts[side][rows, :] + flow
     step_alone(fulls, factor_ref, table_ref, coef_ref, outs)
@@ -277,16 +288,21 @@
     inner, outer = [], []
     for g in range(255):
         (inner if g % 2 == 0 else outer).extend([(spot(g), spot(g + 1)), (spot(g + 1), spot(g))])
-    return inner, outer
+    slab = [pair for pair in outer if pair[0] % 16 != pair[1] % 16]
+    return inner, outer, slab
 
 
 def on_device(pot, vel, diffusivity, *factors):
     shape = jax.ShapeDtypeStruct
     modes = lax.axis_index("modes").astype(jnp.int32)
-    place = jnp.stack([modes % 2, 2 * modes])
-    inner_pairs, outer_pairs = swaps()
+    core = modes % 2
+    beyond = 2 * modes + 3 * core - 1
+    held = (beyond >= 0) & (beyond < 2 * PEERS)
+    place = jnp.stack([core, 2 * modes, held.astype(jnp.int32), jnp.where(held, 3 * core - 1, 0)])
+    inner_pairs, outer_pairs, slab_pairs = swaps()
     table = jnp.asarray(tables())
     block = shape((PEERS, 2, 2, PER, NR), F32)
+    wide = shape((PEERS, 3, 2, PER, NR), F32)
     plane = shape((2 * K, NR), F32)
     opening = shape((2 * K + 8, NR), F32)
     tiles = shape((2, 2, 8, NR), F32)
@@ -296,12 +312,12 @@
         return [lax.ppermute(planes[0], AXES, outer_pairs), lax.ppermute(planes[1], AXES, inner_pairs)]
 
     flat = [a.reshape(-1, NR) for a in (pot, vel)]
-    (sent,) = moved(pack_kernel, [block], flat, (pltpu.HBM, pltpu.VMEM), staging)
+    (sent,) = moved(pack_kernel, [wide], flat, (pltpu.HBM, pltpu.VMEM), staging)
     sent, place = lax.optimization_barrier((sent, place))
     got = lax.all_to_all(sent, "modes", split_axis=0, concat_axis=0, tiled=True)
     got, place, diffusivity, table = lax.optimization_barrier((got, place, diffusivity, table))
-    start = call(split_kernel, [opening] * 2, [place, got, diffusivity], 0, smem=1)
-    rims = swap(start)
+    *start, beyond = call(split_kernel, [opening] * 3, [place, got, diffusivity], 0, smem=1)
+    rims = [lax.ppermute(start[0], AXES, slab_pairs), lax.ppermute(start[1], AXES, inner_pairs)]
     start, factors = lax.optimization_barrier((start, factors))
     factor, coef = call(
         factor_kernel,
@@ -313,7 +329,7 @@
     shared = [factor, table, coef]
     flops = 8 * 2 * 768 * 256 * 256
     parts = call(first_kernel, [plane] * 2, [*start, *shared], flops)
-    olds, pasts = start, []
+    olds, pasts = start, [beyond]
     for step in range(1, STEPS):
         coming = swap(parts)
         outs = call(

time: 105 us -> 106 us (level); the launches traced: 104 us -> 106 us
  blocking collectives: 47.4 us -> 59.5 us
  waiting for transfers between devices: 16.9 us -> 10.3 us
  starting transfers between devices: 26.5 us -> 23.1 us
    all_to_all x2, blocking collectives: 47.4 us -> 59.5 us  [on_device(): got = lax.all_to_all(sent, 'modes', split_axis=0, concat_axis=0, tiled=True)]
    ppermute x4 -> x3, waiting for transfers between devices: 16.9 us -> 7.36 us  [swap(): lax.ppermute(planes[0], AXES, outer_pairs)]
    ppermute x4 -> x3, starting transfers between devices: 13.8 us -> 9.21 us  [swap(): lax.ppermute(planes[1], AXES, inner_pairs)]
    ppermute x0 -> x2, waiting for transfers between devices: none -> 2.98 us  [the longest x1 2.98 us: on_device(): lax.ppermute(start[0], AXES, slab_pairs)]
    ppermute x0 -> x2, starting transfers between devices: none -> 2.01 us  [the longest x1 1.92 us: on_device(): lax.ppermute(start[0], AXES, slab_pairs)]
    ppermute x4 -> x3, starting transfers between devices: 12.7 us -> 11.9 us  [swap(): lax.ppermute(planes[0], AXES, outer_pairs)]
  transfers between devices with their start and end apart: 8 -> 8, of which waited for: 2 -> 3; matrix products, arithmetic and copies ran while one was open for 0% -> 0% of each run, Pallas kernels for 8% -> 8%
where the time goes in v4:
time: 106 us
  blocking collectives  59.5 us (56%)
  starting transfers between devices  23.1 us (22%)
  Pallas kernels  11.9 us (11%)
  waiting for transfers between devices  10.3 us (10%)
    all_to_all x2, blocking collectives, on_device(): got = lax.all_to_all(sent, 'modes', split_axis=0, concat_axis=0, tiled=True)  59.5 us
    ppermute x3, starting transfers between devices, swap(): lax.ppermute(planes[0], AXES, outer_pairs)  11.9 us
    ppermute x3, starting transfers between devices, swap(): lax.ppermute(planes[1], AXES, inner_pairs)  9.21 us
    pallas_call x7, Pallas kernels, call(): pl.pallas_call(body, out_shape=out_shapes, in_specs=space, out_specs=[pl....  8.94 us
    ppermute x3, waiting for transfers between devices, swap(): lax.ppermute(planes[0], AXES, outer_pairs)  7.36 us
    ppermute x1, waiting for transfers between devices, on_device(): lax.ppermute(start[0], AXES, slab_pairs)  2.98 us
    pallas_call x2, Pallas kernels, moved(): pl.pallas_call(body, out_shape=out_shapes, in_specs=[pl.BlockSpec(memory_...  2.95 us
  transfers between devices with their start and end apart: 8, of which 3 were waited for; matrix products, arithmetic and copies ran while one was open for 0% of the time, Pallas kernels for 8%

profile of v4, /device:TPU:104, one launch (start us, length us, event | category | flops | bytes accessed | tf_op | source)
XLA Modules:
  0.0 105.8 jit_solution(1649072632715344515)
XLA Ops:
  0.7 1.6 %shard_map.95 = f32[16,3,2,32,128]{4,3,2,1,0:T(8,128)S(1)} custom-call(f32[1024,128]{1,0:T(8,128)} %bitcast.16, f32[1024,128]{1,0:T(8,128)} %bitcast.17), custom_call_target="tpu_custom_call" | custom-call | bytes 2097152 | tf_op jit(solution)/shard_map/pallas_call | solution.py:116
  2.3 0.1 pad_add_fusion.core_ref
  2.4 0.0 copy-start.5
  2.4 0.0 copy-start.1
  2.4 0.0 copy-start.2
  2.4 0.0 copy-start.3
  2.4 0.0 copy-start.4
  2.4 29.7 %all_to_all.10.in_ref = f32[16,3,2,32,128]{4,3,2,1,0:T(8,128)S(1)} all-to-all(f32[16,3,2,32,128]{4,3,2,1,0:T(8,128)S(1)} %shard_map.95), channel_id=1, replica_groups=mesh['modes'=16,'axial'=16] {'modes'}, dimensions={0} | all-to-all | bytes 3145728 | tf_op jit(solution)/shard_map/all_to_all | solution.py:317
  32.1 0.0 copy-done.5
  32.1 0.0 copy-start
  32.1 0.6 shard_map.96
  32.7 1.9 %collective-permute-start = (f32[1032,128]{1,0:T(8,128)S(1)}, f32[1032,128]{1,0:T(8,128)S(1)}, u32[]{:S(2)}, u32[]{:S(2)}) collective-permute-start(f32[1032,128]{1,0:T(8,128)S(1)} %get-tuple-element.49.outer.refs_2_), channel_id=1, source_target_pairs={{240,1},{1,240},{241,2},{2,241},{242,3},{3,242},{243,4},{4,243},{2... | collective-permute-start | bytes 1585160 | tf_op jit(solution)/shard_map/ppermute | solution.py:320
  34.7 0.1 collective-permute-start.1
  34.8 0.0 copy-done.1
  34.8 0.0 copy-done.2
  34.8 0.0 copy-done.3
  34.8 0.0 copy-done.4
  34.8 1.0 shard_map.97
  35.8 0.0 copy-done
  35.8 1.6 %shard_map.98 = (f32[1024,128]{1,0:T(8,128)S(1)}, f32[1024,128]{1,0:T(8,128)S(1)}) custom-call(f32[1032,128]{1,0:T(8,128)S(1)} %get-tuple-element.49.outer.refs_2_, f32[1032,128]{1,0:T(8,128)S(1)} %get-tuple-element.50.inner.refs_3_, f32[4,2,512,128]{3,2,1,0:T(8,128)S(1)} %get-tuple-element.55.factor_ref.refs_7_.refs_9_, bf16[3,256,768]{2,1,0:T(8,128)(2,1)S(1)} %copy-done, ...), custom_call_target="tpu_custom_call" | custom-call | flops 805306368 | bytes 5398528 | tf_op jit(solution)/shard_map/pallas_call | solution.py:46
  37.4 5.8 %collective-permute-start.2 = (f32[1024,128]{1,0:T(8,128)S(1)}, f32[1024,128]{1,0:T(8,128)S(1)}, u32[]{:S(2)}, u32[]{:S(2)}) collective-permute-start(f32[1024,128]{1,0:T(8,128)S(1)} %get-tuple-element.58.refs_0_), channel_id=1, source_target_pairs={{16,32},{32,16},{48,64},{64,48},{80,96},{96,80},{112,128},{128,112... | collective-permute-start | bytes 1572872 | tf_op jit(solution)/shard_map/ppermute | solution.py:312
  43.2 0.1 collective-permute-start.3
  43.3 3.0 %collective-permute-done.refs_4_ = f32[1032,128]{1,0:T(8,128)S(1)} collective-permute-done((f32[1032,128]{1,0:T(8,128)S(1)}, f32[1032,128]{1,0:T(8,128)S(1)}, u32[]{:S(2)}, u32[]{:S(2)}) %collective-permute-start) | collective-permute-done | bytes 528416 | tf_op jit(solution)/shard_map/ppermute | solution.py:320
  46.3 0.0 collective-permute-done.1.refs_5_
  46.3 1.8 %shard_map.99 = (f32[1024,128]{1,0:T(8,128)S(1)}, f32[1024,128]{1,0:T(8,128)S(1)}, f32[1024,128]{1,0:T(8,128)S(1)}, f32[1024,128]{1,0:T(8,128)S(1)}, f32[1024,12...) custom-call(f32[1024,128]{1,0:T(8,128)S(1)} %get-tuple-element.58.refs_0_, ...), custom_call_target="tpu_custom_call" | custom-call | flops 805306368 | bytes 10137600 | tf_op jit(solution)/shard_map/pallas_call | solution.py:46
  48.1 1.9 %collective-permute-start.4 = (f32[1024,128]{1,0:T(8,128)S(1)}, f32[1024,128]{1,0:T(8,128)S(1)}, u32[]{:S(2)}, u32[]{:S(2)}) collective-permute-start(f32[1024,128]{1,0:T(8,128)S(1)} %get-tuple-element.61.refs_0_), channel_id=1, source_target_pairs={{16,32},{32,16},{48,64},{64,48},{80,96},{96,80},{112,128},{128,112... | collective-permute-start | bytes 1572872 | tf_op jit(solution)/shard_map/ppermute | solution.py:312
  50.0 0.1 collective-permute-start.5
  50.1 5.4 %collective-permute-done.2.refs_4_ = f32[1024,128]{1,0:T(8,128)S(1)} collective-permute-done((f32[1024,128]{1,0:T(8,128)S(1)}, f32[1024,128]{1,0:T(8,128)S(1)}, u32[]{:S(2)}, u32[]{:S(2)}) %collective-permute-start.2) | collective-permute-done | bytes 524320 | tf_op jit(solution)/shard_map/ppermute | solution.py:312
  55.5 0.0 collective-permute-done.3.refs_5_
  55.5 1.8 %shard_map.100 = (f32[1024,128]{1,0:T(8,128)S(1)}, f32[1024,128]{1,0:T(8,128)S(1)}, f32[1024,128]{1,0:T(8,128)S(1)}, f32[1024,128]{1,0:T(8,128)S(1)}, f32[1024,128]{1,0:T(8,128)S(1)}, /*index=5*/f32[1024,128]{1,0:T(8,128)S(1)}) custom-call(f32[1024,128]{1,0:T(8,128)S(1)} %get-tuple-element.61.refs_0_, f32[1024,128]{1,0:T(8,128)S(1)} %get-tuple-element.62.refs_1_, ...), custom_call_target="tpu_custom_call" | custom-call | flops 805306368 | bytes 10641408 | tf_op jit(solution)/shard_map/pallas_call | solution.py:46
  57.4 4.2 %collective-permute-start.6 = (f32[1024,128]{1,0:T(8,128)S(1)}, f32[1024,128]{1,0:T(8,128)S(1)}, u32[]{:S(2)}, u32[]{:S(2)}) collective-permute-start(f32[1024,128]{1,0:T(8,128)S(1)} %get-tuple-element.68.refs_0_), channel_id=1, source_target_pairs={{16,32},{32,16},{48,64},{64,48},{80,96},{96,80},{112,128},{128,112... | collective-permute-start | bytes 1572872 | tf_op jit(solution)/shard_map/ppermute | solution.py:312
  61.6 9.0 %collective-permute-start.7 = (f32[1024,128]{1,0:T(8,128)S(1)}, f32[1024,128]{1,0:T(8,128)S(1)}, u32[]{:S(2)}, u32[]{:S(2)}) collective-permute-start(f32[1024,128]{1,0:T(8,128)S(1)} %get-tuple-element.69.refs_1_), channel_id=1, source_target_pairs={{0,16},{16,0},{32,48},{48,32},{64,80},{80,64},{96,112},{112,96},{1... | collective-permute-start | bytes 1572872 | tf_op jit(solution)/shard_map/ppermute | solution.py:312
  70.6 0.0 collective-permute-done.4.refs_4_
  70.6 0.0 collective-permute-done.5.refs_5_
  70.6 1.9 %shard_map.101 = (f32[1024,128]{1,0:T(8,128)S(1)}, f32[1024,128]{1,0:T(8,128)S(1)}, f32[1024,128]{1,0:T(8,128)S(1)}, f32[1024,128]{1,0:T(8,128)S(1)}, f32[1024,128]{1,0:T(8,128)S(1)}, /*index=5*/f32[1024,128]{1,0:T(8,128)S(1)}) custom-call(f32[1024,128]{1,0:T(8,128)S(1)} %get-tuple-element.68.refs_0_, f32[1024,128]{1,0:T(8,128)S(1)} %get-tuple-element.69.refs_1_, ...), custom_call_target="tpu_custom_call" | custom-call | flops 805306368 | bytes 10641408 | tf_op jit(solution)/shard_map/pallas_call | solution.py:46
  72.5 1.9 %collective-permute-done.6.refs_4_ = f32[1024,128]{1,0:T(8,128)S(1)} collective-permute-done((f32[1024,128]{1,0:T(8,128)S(1)}, f32[1024,128]{1,0:T(8,128)S(1)}, u32[]{:S(2)}, u32[]{:S(2)}) %collective-permute-start.6) | collective-permute-done | bytes 524320 | tf_op jit(solution)/shard_map/ppermute | solution.py:312
  74.4 0.0 collective-permute-done.7.refs_5_
  74.4 0.2 shard_map.102
  74.6 29.9 %all_to_all.11.in_ref = f32[16,2,2,32,128]{4,3,2,1,0:T(8,128)S(1)} all-to-all(f32[16,2,2,32,128]{4,3,2,1,0:T(8,128)S(1)} %shard_map.102), channel_id=1, replica_groups=mesh['modes'=16,'axial'=16] {'modes'}, dimensions={0} | all-to-all | bytes 2097152 | tf_op jit(solution)/shard_map/all_to_all | solution.py:345
  104.5 1.3 %shard_map.103 = (f32[1024,128]{1,0:T(8,128)}, f32[1024,128]{1,0:T(8,128)}) custom-call(f32[16,2,2,32,128]{4,3,2,1,0:T(8,128)S(1)} %all_to_all.11.in_ref), custom_call_target="tpu_custom_call" | custom-call | bytes 2097152 | tf_op jit(solution)/shard_map/pallas_call | solution.py:116
Async XLA Ops:
  2.4 29.7 %copy-start.5 = (f32[32,128]{1,0:T(8,128)S(1)}, f32[32,128]{1,0:T(8,128)}, u32[]{:S(2)}) copy-start(f32[32,128]{1,0:T(8,128)} %diff_ref.1) | copy-start | bytes 49156
  2.4 32.4 %copy-start.1 = (f32[512,2,128]{2,1,0:T(2,128)S(1)}, f32[512,2,128]{2,1,0:T(2,128)}, u32[]{:S(2)}) copy-start(f32[512,2,128]{2,1,0:T(2,128)} %param.11) | copy-start | bytes 1572868
  2.4 32.4 %copy-start.2 = (f32[512,2,128]{2,1,0:T(2,128)S(1)}, f32[512,2,128]{2,1,0:T(2,128)}, u32[]{:S(2)}) copy-start(f32[512,2,128]{2,1,0:T(2,128)} %param.12) | copy-start | bytes 1572868
  2.4 32.4 %copy-start.3 = (f32[512,2,128]{2,1,0:T(2,128)S(1)}, f32[512,2,128]{2,1,0:T(2,128)}, u32[]{:S(2)}) copy-start(f32[512,2,128]{2,1,0:T(2,128)} %param.13) | copy-start | bytes 1572868
  2.4 32.4 %copy-start.4 = (f32[512,2,128]{2,1,0:T(2,128)S(1)}, f32[512,2,128]{2,1,0:T(2,128)}, u32[]{:S(2)}) copy-start(f32[512,2,128]{2,1,0:T(2,128)} %param.14) | copy-start | bytes 1572868
  32.1 3.7 %copy-start = (bf16[3,256,768]{2,1,0:T(8,128)(2,1)S(1)}, bf16[3,256,768]{2,1,0:T(8,128)(2,1)}, u32[]{:S(2)}) copy-start(bf16[3,256,768]{2,1,0:T(8,128)(2,1)} %constant.29.clone.table_ref.refs_8_.refs_10_) | copy-start | bytes 3538948
  32.7 13.6 %collective-permute-start = (f32[1032,128]{1,0:T(8,128)S(1)}, f32[1032,128]{1,0:T(8,128)S(1)}, u32[]{:S(2)}, u32[]{:S(2)}) collective-permute-start(f32[1032,128]{1,0:T(8,128)S(1)} %get-tuple-element.49.outer.refs_2_), channel_id=1, source_target_pairs={{240,1},{1,240},{241,2},{2,241},{242,3},{3,242},{243,4},{4,243},{2... | collective-permute-start | bytes 1585160 | tf_op jit(solution)/shard_map/ppermute | solution.py:320
  34.7 11.6 %collective-permute-start.1 = (f32[1032,128]{1,0:T(8,128)S(1)}, f32[1032,128]{1,0:T(8,128)S(1)}, u32[]{:S(2)}, u32[]{:S(2)}) collective-permute-start(f32[1032,128]{1,0:T(8,128)S(1)} %get-tuple-element.50.inner.refs_3_), channel_id=1, source_target_pairs={{0,16},{16,0},{32,48},{48,32},{64,80},{80,64},{96,112},{112,96},{1... | collective-permute-start | bytes 1585160 | tf_op jit(solution)/shard_map/ppermute | solution.py:320
  37.4 18.1 %collective-permute-start.2 = (f32[1024,128]{1,0:T(8,128)S(1)}, f32[1024,128]{1,0:T(8,128)S(1)}, u32[]{:S(2)}, u32[]{:S(2)}) collective-permute-start(f32[1024,128]{1,0:T(8,128)S(1)} %get-tuple-element.58.refs_0_), channel_id=1, source_target_pairs={{16,32},{32,16},{48,64},{64,48},{80,96},{96,80},{112,128},{128,112... | collective-permute-start | bytes 1572872 | tf_op jit(solution)/shard_map/ppermute | solution.py:312
  43.2 12.3 %collective-permute-start.3 = (f32[1024,128]{1,0:T(8,128)S(1)}, f32[1024,128]{1,0:T(8,128)S(1)}, u32[]{:S(2)}, u32[]{:S(2)}) collective-permute-start(f32[1024,128]{1,0:T(8,128)S(1)} %get-tuple-element.59.refs_1_), channel_id=1, source_target_pairs={{0,16},{16,0},{32,48},{48,32},{64,80},{80,64},{96,112},{112,96},{1... | collective-permute-start | bytes 1572872 | tf_op jit(solution)/shard_map/ppermute | solution.py:312
  48.1 22.5 %collective-permute-start.4 = (f32[1024,128]{1,0:T(8,128)S(1)}, f32[1024,128]{1,0:T(8,128)S(1)}, u32[]{:S(2)}, u32[]{:S(2)}) collective-permute-start(f32[1024,128]{1,0:T(8,128)S(1)} %get-tuple-element.61.refs_0_), channel_id=1, source_target_pairs={{16,32},{32,16},{48,64},{64,48},{80,96},{96,80},{112,128},{128,112... | collective-permute-start | bytes 1572872 | tf_op jit(solution)/shard_map/ppermute | solution.py:312
  50.0 20.6 %collective-permute-start.5 = (f32[1024,128]{1,0:T(8,128)S(1)}, f32[1024,128]{1,0:T(8,128)S(1)}, u32[]{:S(2)}, u32[]{:S(2)}) collective-permute-start(f32[1024,128]{1,0:T(8,128)S(1)} %get-tuple-element.62.refs_1_), channel_id=1, source_target_pairs={{0,16},{16,0},{32,48},{48,32},{64,80},{80,64},{96,112},{112,96},{1... | collective-permute-start | bytes 1572872 | tf_op jit(solution)/shard_map/ppermute | solution.py:312
  57.4 17.0 %collective-permute-start.6 = (f32[1024,128]{1,0:T(8,128)S(1)}, f32[1024,128]{1,0:T(8,128)S(1)}, u32[]{:S(2)}, u32[]{:S(2)}) collective-permute-start(f32[1024,128]{1,0:T(8,128)S(1)} %get-tuple-element.68.refs_0_), channel_id=1, source_target_pairs={{16,32},{32,16},{48,64},{64,48},{80,96},{96,80},{112,128},{128,112... | collective-permute-start | bytes 1572872 | tf_op jit(solution)/shard_map/ppermute | solution.py:312
  61.6 12.8 %collective-permute-start.7 = (f32[1024,128]{1,0:T(8,128)S(1)}, f32[1024,128]{1,0:T(8,128)S(1)}, u32[]{:S(2)}, u32[]{:S(2)}) collective-permute-start(f32[1024,128]{1,0:T(8,128)S(1)} %get-tuple-element.69.refs_1_), channel_id=1, source_target_pairs={{0,16},{16,0},{32,48},{48,32},{64,80},{80,64},{96,112},{112,96},{1... | collective-permute-start | bytes 1572872 | tf_op jit(solution)/shard_map/ppermute | solution.py:312

commit v5 on v4

--- a/solution.py
+++ b/solution.py
@@ -82,12 +82,12 @@
     for chunk, pair in enumerate(arrive):
         for field, copy in enumerate(pair):
             copy.wait()
-            for peer, side, plane in planes(3):
+            for peer, side, plane in planes(2 + field):
                 if plane is None:
                     piece = jnp.zeros((CHUNK, NR), F32)
                 else:
                     piece = rows[field, pl.ds(chunk * CHUNK * 32 + plane, CHUNK, stride=32), :]
-                out_ref[peer, side, field, pl.ds(chunk * CHUNK, CHUNK)] = piece
+                out_ref[peer, 2 * side + field * (side < 2), pl.ds(chunk * CHUNK, CHUNK)] = piece
 
 
 def unpack_kernel(in_ref, pot_ref, vel_ref, rows, sems):
@@ -124,21 +124,27 @@
     )(*args)
 
 
-def split_kernel(core_ref, in_ref, diff_ref, *outs):
+def split_kernel(core_ref, in_ref, diff_ref, outer, inner, pot_rim, vel_rim, beyond):
     row = lax.broadcasted_iota(jnp.int32, (8, NR), 0)
-    for side, out in enumerate(outs):
+    for side, out in enumerate((outer, inner)):
+        own = jnp.broadcast_to(near(core_ref, diff_ref, side), (8, NR))
+        own = jnp.where(row == 0, own, 1.0)
+        out[pl.ds(2 * K, 8), :] = own
+        if side == 0:
+            pot_rim[pl.ds(K, 8), :] = own
         for src in range(PEERS):
             for field in range(2):
-                out[pl.ds(field * K + src * PER, PER), :] = in_ref[src, side, field]
-        own = jnp.where(row == 0, jnp.broadcast_to(near(core_ref, diff_ref, side), (8, NR)), 1.0)
-        if side == 2:
-            own = jnp.where(jnp.full((8, NR), core_ref[2], jnp.int32) == 1, own, 0.0)
-        out[pl.ds(2 * K, 8), :] = own
+                piece = in_ref[src, 2 * side + field]
+                out[pl.ds(field * K + src * PER, PER), :] = piece
+                if side == 0:
+                    (pot_rim, vel_rim)[field][pl.ds(src * PER, PER), :] = piece
+    for src in range(PEERS):
+        beyond[pl.ds(src * PER, PER), :] = in_ref[src, 4]
 
 
 def near(core_ref, diff_ref, side):
-    at = (core_ref[0], 1 - core_ref[0], core_ref[3])[side]
-    return diff_ref[pl.ds(core_ref[1] + at, 1), :]
+    plane = core_ref[1] + (core_ref[0] if side == 0 else 1 - core_ref[0])
+    return diff_ref[pl.ds(plane, 1), :]
 
 
 def factor_kernel(core_ref, diff_ref, *refs):
@@ -203,26 +209,30 @@
 def next_kernel(opening, *refs):
     refs = list(refs)
     take = lambda n: [refs.pop(0) for _ in range(n)]
-    parts, olds, rims = take(2), take(2), take(2)
+    parts, olds = take(2), take(2)
     if opening:
-        (beyond,) = take(1)
-        coming = [lambda rows: rims[0][rows, :] + beyond[rows, :], lambda rows: rims[1][rows, :]]
+        pot_rim, vel_rim, beyond, inner_rim = take(4)
+        comings = [
+            [pot_rim[pl.ds(0, K), :], vel_rim[...] + beyond[...]],
+            [inner_rim[field_rows(field), :] for field in range(2)],
+        ]
+        others = [pot_rim[pl.ds(K, 8), :], inner_rim[pl.ds(2 * K, 8), :]]
     else:
-        pasts, (edge_ref,) = take(2), take(1)
-        coming = [lambda rows, rim=rim: rim[rows, :] for rim in rims]
+        rims, pasts, (edge_ref,) = take(2), take(2), take(1)
+        comings = [[rim[field_rows(field), :] for field in range(2)] for rim in rims]
     factor_ref, table_ref, coef_ref = take(3)
     outs, fulls, fluxes = take(2), take(2), take(2)
     if opening:
         (edge_ref,) = take(1)
         for side in range(2):
-            own, other = olds[side][pl.ds(2 * K, 8), :], coming[side](pl.ds(2 * K, 8))
+            own, other = olds[side][pl.ds(2 * K, 8), :], others[side]
             row = lax.broadcasted_iota(jnp.int32, (8, NR), 0)
             edge_ref[side] = jnp.where(row < 2, DT * 0.5 * (own + other), other)
     for side in range(2):
         for field in range(2):
             rows = field_rows(field)
             past = None if opening else pasts[side][rows, :]
-            flow = flux(edge_ref, side, field, coming[side](rows), olds[side][rows, :], past)
+            flow = flux(edge_ref, side, field, comings[side][field], olds[side][rows, :], past)
             fluxes[side][rows, :] = flow
             fulls[side][rows, :] = parts[side][rows, :] + flow
     step_alone(fulls, factor_ref, table_ref, coef_ref, outs)
@@ -295,14 +305,11 @@
 def on_device(pot, vel, diffusivity, *factors):
     shape = jax.ShapeDtypeStruct
     modes = lax.axis_index("modes").astype(jnp.int32)
-    core = modes % 2
-    beyond = 2 * modes + 3 * core - 1
-    held = (beyond >= 0) & (beyond < 2 * PEERS)
-    place = jnp.stack([core, 2 * modes, held.astype(jnp.int32), jnp.where(held, 3 * core - 1, 0)])
+    place = jnp.stack([modes % 2, 2 * modes])
     inner_pairs, outer_pairs, slab_pairs = swaps()
     table = jnp.asarray(tables())
     block = shape((PEERS, 2, 2, PER, NR), F32)
-    wide = shape((PEERS, 3, 2, PER, NR), F32)
+    wide = shape((PEERS, 5, PER, NR), F32)
     plane = shape((2 * K, NR), F32)
     opening = shape((2 * K + 8, NR), F32)
     tiles = shape((2, 2, 8, NR), F32)
@@ -316,8 +323,19 @@
     sent, place = lax.optimization_barrier((sent, place))
     got = lax.all_to_all(sent, "modes", split_axis=0, concat_axis=0, tiled=True)
     got, place, diffusivity, table = lax.optimization_barrier((got, place, diffusivity, table))
-    *start, beyond = call(split_kernel, [opening] * 3, [place, got, diffusivity], 0, smem=1)
-    rims = [lax.ppermute(start[0], AXES, slab_pairs), lax.ppermute(start[1], AXES, inner_pairs)]
+    *start, pot_rim, vel_rim, beyond = call(
+        split_kernel,
+        [opening] * 2 + [shape((K + 8, NR), F32)] + [shape((K, NR), F32)] * 2,
+        [place, got, diffusivity],
+        0,
+        smem=1,
+    )
+    rims = [
+        lax.ppermute(pot_rim, AXES, outer_pairs),
+        lax.ppermute(vel_rim, AXES, slab_pairs),
+        beyond,
+        lax.ppermute(start[1], AXES, inner_pairs),
+    ]
     start, factors = lax.optimization_barrier((start, factors))
     factor, coef = call(
         factor_kernel,
@@ -327,9 +345,9 @@
         smem=1,
     )
     shared = [factor, table, coef]
-    flops = 8 * 2 * 768 * 256 * 256
+    flops = 1 << 34
     parts = call(first_kernel, [plane] * 2, [*start, *shared], flops)
-    olds, pasts = start, [beyond]
+    olds, pasts = start, []
     for step in range(1, STEPS):
         coming = swap(parts)
         outs = call(

time: 106 us -> 105 us (level)
  blocking collectives: 59.5 us -> 55.2 us
  starting transfers between devices: 23.1 us -> 24.9 us
  waiting for transfers between devices: 10.3 us -> 11.9 us
    ppermute x1 -> x2, starting transfers between devices: 1.92 us -> 7.79 us  [the longest x1 5.68 us: on_device(): lax.ppermute(vel_rim, AXES, slab_pairs)]
    ppermute x3, starting transfers between devices: 11.9 us -> 6.02 us  [swap(): lax.ppermute(planes[0], AXES, outer_pairs)]
    all_to_all x2, blocking collectives: 59.5 us -> 55.2 us  [on_device(): got = lax.all_to_all(sent, 'modes', split_axis=0, concat_axis=0, tiled=True)]
    ppermute x3, starting transfers between devices: 9.21 us -> 10.9 us  [swap(): lax.ppermute(planes[1], AXES, inner_pairs)]
    ppermute x1 -> x2, waiting for transfers between devices: 2.98 us -> 4.11 us  [the longest x1 4.11 us: on_device(): lax.ppermute(vel_rim, AXES, slab_pairs)]
  transfers between devices with their start and end apart: 8 -> 9, of which waited for: 3 -> 3; matrix products, arithmetic and copies ran while one was open for 0% -> 0% of each run, Pallas kernels for 8% -> 7%
where the time goes in v5:
time: 105 us; the launch traced here: 104 us
  blocking collectives  55.2 us (53%)
  starting transfers between devices  24.9 us (24%)
  waiting for transfers between devices  11.9 us (11%)
  Pallas kernels  11.4 us (11%)
    all_to_all x2, blocking collectives, on_device(): got = lax.all_to_all(sent, 'modes', split_axis=0, concat_axis=0, tiled=True)  55.2 us
    ppermute x3, starting transfers between devices, swap(): lax.ppermute(planes[1], AXES, inner_pairs)  10.9 us
    pallas_call x7, Pallas kernels, call(): pl.pallas_call(body, out_shape=out_shapes, in_specs=space, out_specs=[pl....  8.49 us
    ppermute x3, waiting for transfers between devices, swap(): lax.ppermute(planes[0], AXES, outer_pairs)  7.74 us
    ppermute x3, starting transfers between devices, swap(): lax.ppermute(planes[0], AXES, outer_pairs)  6.02 us
    ppermute x1, starting transfers between devices, on_device(): lax.ppermute(vel_rim, AXES, slab_pairs)  5.68 us
    ppermute x1, waiting for transfers between devices, on_device(): lax.ppermute(vel_rim, AXES, slab_pairs)  4.11 us
    pallas_call x2, Pallas kernels, moved(): pl.pallas_call(body, out_shape=out_shapes, in_specs=[pl.BlockSpec(memory_...  2.95 us
  transfers between devices with their start and end apart: 9, of which 3 were waited for; matrix products, arithmetic and copies ran while one was open for 0% of the time, Pallas kernels for 7%

profile of v5, /device:TPU:104, one launch (start us, length us, event | category | flops | bytes accessed | tf_op | source)
XLA Modules:
  0.0 104.3 jit_solution(13487948299570551685)
XLA Ops:
  0.6 0.1 pad_add_fusion.core_ref
  0.7 1.6 %shard_map.95 = f32[16,5,32,128]{3,2,1,0:T(8,128)S(1)} custom-call(f32[1024,128]{1,0:T(8,128)} %bitcast.14, f32[1024,128]{1,0:T(8,128)} %bitcast.15), custom_call_target="tpu_custom_call" | custom-call | bytes 2097152 | tf_op jit(solution)/shard_map/pallas_call | solution.py:116
  2.4 0.0 copy-start.4
  2.4 0.0 copy-start.2
  2.4 0.0 copy-start.3
  2.4 26.5 %all_to_all.10.in_ref = f32[16,5,32,128]{3,2,1,0:T(8,128)S(1)} all-to-all(f32[16,5,32,128]{3,2,1,0:T(8,128)S(1)} %shard_map.95), channel_id=1, replica_groups=mesh['modes'=16,'axial'=16] {'modes'}, dimensions={0} | all-to-all | bytes 2621440 | tf_op jit(solution)/shard_map/all_to_all | solution.py:324
  28.9 0.0 copy-done.4
  28.9 0.0 copy-start
  28.9 0.0 copy-start.1
  28.9 0.7 shard_map.96
  29.6 0.0 copy-start.5
  29.6 0.2 collective-permute-start.2
  29.8 2.1 %collective-permute-start = (f32[520,128]{1,0:T(8,128)S(1)}, f32[520,128]{1,0:T(8,128)S(1)}, u32[]{:S(2)}, u32[]{:S(2)}) collective-permute-start(f32[520,128]{1,0:T(8,128)S(1)} %get-tuple-element.62), channel_id=1, source_target_pairs={{16,32},{32,16},{48,64},{64,48},{80,96},{96,80},{112,128},{128,112... | collective-permute-start | bytes 798728 | tf_op jit(solution)/shard_map/ppermute | solution.py:334
  31.9 5.7 %collective-permute-start.1 = (f32[512,128]{1,0:T(8,128)S(1)}, f32[512,128]{1,0:T(8,128)S(1)}, u32[]{:S(2)}, u32[]{:S(2)}) collective-permute-start(f32[512,128]{1,0:T(8,128)S(1)} %get-tuple-element.63), channel_id=1, source_target_pairs={{240,1},{1,240},{241,2},{2,241},{242,3},{3,242},{243,4},{4,243},{2... | collective-permute-start | bytes 786440 | tf_op jit(solution)/shard_map/ppermute | solution.py:335
  37.6 0.0 copy-done.2
  37.6 0.0 copy-done.3
  37.6 0.0 copy-done
  37.6 0.0 copy-done.1
  37.6 1.0 shard_map.97
  38.6 0.0 copy-done.5
  38.6 1.6 %shard_map.98 = (f32[1024,128]{1,0:T(8,128)S(1)}, f32[1024,128]{1,0:T(8,128)S(1)}) custom-call(f32[1032,128]{1,0:T(8,128)S(1)} %get-tuple-element.51.outer.refs_2_, f32[1032,128]{1,0:T(8,128)S(1)} %get-tuple-element.52.inner.refs_3_, f32[4,2,512,128]{3,2,1,0:T(8,128)S(1)} %get-tuple-element.57.factor_ref.refs_8_.refs_9_, bf16[3,256,768]{2,1,0:T(8,128)(2,1)S(1)} %copy-done.5, ...), custom_call_target="tpu_custom_call" | custom-call | flops 17179869184 | bytes 5398528 | tf_op jit(solution)/shard_map/pallas_call | solution.py:46
  40.2 2.0 %collective-permute-start.3 = (f32[1024,128]{1,0:T(8,128)S(1)}, f32[1024,128]{1,0:T(8,128)S(1)}, u32[]{:S(2)}, u32[]{:S(2)}) collective-permute-start(f32[1024,128]{1,0:T(8,128)S(1)} %get-tuple-element.60.refs_0_), channel_id=1, source_target_pairs={{16,32},{32,16},{48,64},{64,48},{80,96},{96,80},{112,128},{128,112... | collective-permute-start | bytes 1572872 | tf_op jit(solution)/shard_map/ppermute | solution.py:319
  42.2 0.1 collective-permute-start.4
  42.3 4.1 %collective-permute-done.1.refs_5_ = f32[512,128]{1,0:T(8,128)S(1)} collective-permute-done((f32[512,128]{1,0:T(8,128)S(1)}, f32[512,128]{1,0:T(8,128)S(1)}, u32[]{:S(2)}, u32[]{:S(2)}) %collective-permute-start.1) | collective-permute-done | bytes 262176 | tf_op jit(solution)/shard_map/ppermute | solution.py:335
  46.4 0.0 collective-permute-done.refs_4_
  46.4 0.0 collective-permute-done.2.refs_7_
  46.4 1.6 %shard_map.99 = (f32[1024,128]{1,0:T(8,128)S(1)}, f32[1024,128]{1,0:T(8,128)S(1)}, f32[1024,128]{1,0:T(8,128)S(1)}, f32[1024,128]{1,0:T(8,128)S(1)}, f32[1024,12...) custom-call(f32[1024,128]{1,0:T(8,128)S(1)} %get-tuple-element.60.refs_0_, ...), custom_call_target="tpu_custom_call" | custom-call | flops 17179869184 | bytes 9871360 | tf_op jit(solution)/shard_map/pallas_call | solution.py:46
  48.0 2.1 %collective-permute-start.5 = (f32[1024,128]{1,0:T(8,128)S(1)}, f32[1024,128]{1,0:T(8,128)S(1)}, u32[]{:S(2)}, u32[]{:S(2)}) collective-permute-start(f32[1024,128]{1,0:T(8,128)S(1)} %get-tuple-element.65.refs_0_), channel_id=1, source_target_pairs={{16,32},{32,16},{48,64},{64,48},{80,96},{96,80},{112,128},{128,112... | collective-permute-start | bytes 1572872 | tf_op jit(solution)/shard_map/ppermute | solution.py:319
  50.1 0.1 collective-permute-start.6
  50.2 6.6 %collective-permute-done.3.refs_4_ = f32[1024,128]{1,0:T(8,128)S(1)} collective-permute-done((f32[1024,128]{1,0:T(8,128)S(1)}, f32[1024,128]{1,0:T(8,128)S(1)}, u32[]{:S(2)}, u32[]{:S(2)}) %collective-permute-start.3) | collective-permute-done | bytes 524320 | tf_op jit(solution)/shard_map/ppermute | solution.py:319
  56.8 0.0 collective-permute-done.4.refs_5_
  56.8 1.7 %shard_map.100 = (f32[1024,128]{1,0:T(8,128)S(1)}, f32[1024,128]{1,0:T(8,128)S(1)}, f32[1024,128]{1,0:T(8,128)S(1)}, f32[1024,128]{1,0:T(8,128)S(1)}, f32[1024,128]{1,0:T(8,128)S(1)}, /*index=5*/f32[1024,128]{1,0:T(8,128)S(1)}) custom-call(f32[1024,128]{1,0:T(8,128)S(1)} %get-tuple-element.65.refs_0_, f32[1024,128]{1,0:T(8,128)S(1)} %get-tuple-element.66.refs_1_, ...), custom_call_target="tpu_custom_call" | custom-call | flops 17179869184 | bytes 10641408 | tf_op jit(solution)/shard_map/pallas_call | solution.py:46
  58.5 2.0 %collective-permute-start.7 = (f32[1024,128]{1,0:T(8,128)S(1)}, f32[1024,128]{1,0:T(8,128)S(1)}, u32[]{:S(2)}, u32[]{:S(2)}) collective-permute-start(f32[1024,128]{1,0:T(8,128)S(1)} %get-tuple-element.72.refs_0_), channel_id=1, source_target_pairs={{16,32},{32,16},{48,64},{64,48},{80,96},{96,80},{112,128},{128,112... | collective-permute-start | bytes 1572872 | tf_op jit(solution)/shard_map/ppermute | solution.py:319
  60.5 10.7 %collective-permute-start.8 = (f32[1024,128]{1,0:T(8,128)S(1)}, f32[1024,128]{1,0:T(8,128)S(1)}, u32[]{:S(2)}, u32[]{:S(2)}) collective-permute-start(f32[1024,128]{1,0:T(8,128)S(1)} %get-tuple-element.73.refs_1_), channel_id=1, source_target_pairs={{0,16},{16,0},{32,48},{48,32},{64,80},{80,64},{96,112},{112,96},{1... | collective-permute-start | bytes 1572872 | tf_op jit(solution)/shard_map/ppermute | solution.py:319
  71.2 0.0 collective-permute-done.5.refs_4_
  71.2 0.0 collective-permute-done.6.refs_5_
  71.2 1.8 %shard_map.101 = (f32[1024,128]{1,0:T(8,128)S(1)}, f32[1024,128]{1,0:T(8,128)S(1)}, f32[1024,128]{1,0:T(8,128)S(1)}, f32[1024,128]{1,0:T(8,128)S(1)}, f32[1024,128]{1,0:T(8,128)S(1)}, /*index=5*/f32[1024,128]{1,0:T(8,128)S(1)}) custom-call(f32[1024,128]{1,0:T(8,128)S(1)} %get-tuple-element.72.refs_0_, f32[1024,128]{1,0:T(8,128)S(1)} %get-tuple-element.73.refs_1_, ...), custom_call_target="tpu_custom_call" | custom-call | flops 17179869184 | bytes 10641408 | tf_op jit(solution)/shard_map/pallas_call | solution.py:46
  73.0 1.1 %collective-permute-done.7.refs_4_ = f32[1024,128]{1,0:T(8,128)S(1)} collective-permute-done((f32[1024,128]{1,0:T(8,128)S(1)}, f32[1024,128]{1,0:T(8,128)S(1)}, u32[]{:S(2)}, u32[]{:S(2)}) %collective-permute-start.7) | collective-permute-done | bytes 524320 | tf_op jit(solution)/shard_map/ppermute | solution.py:319
  74.1 0.0 collective-permute-done.8.refs_5_
  74.1 0.2 shard_map.102
  74.3 28.7 %all_to_all.11.in_ref = f32[16,2,2,32,128]{4,3,2,1,0:T(8,128)S(1)} all-to-all(f32[16,2,2,32,128]{4,3,2,1,0:T(8,128)S(1)} %shard_map.102), channel_id=1, replica_groups=mesh['modes'=16,'axial'=16] {'modes'}, dimensions={0} | all-to-all | bytes 2097152 | tf_op jit(solution)/shard_map/all_to_all | solution.py:363
  103.0 1.3 %shard_map.103 = (f32[1024,128]{1,0:T(8,128)}, f32[1024,128]{1,0:T(8,128)}) custom-call(f32[16,2,2,32,128]{4,3,2,1,0:T(8,128)S(1)} %all_to_all.11.in_ref), custom_call_target="tpu_custom_call" | custom-call | bytes 2097152 | tf_op jit(solution)/shard_map/pallas_call | solution.py:116
Async XLA Ops:
  2.4 26.5 %copy-start.4 = (f32[32,128]{1,0:T(8,128)S(1)}, f32[32,128]{1,0:T(8,128)}, u32[]{:S(2)}) copy-start(f32[32,128]{1,0:T(8,128)} %diff_ref.1) | copy-start | bytes 49156
  2.4 35.2 %copy-start.2 = (f32[512,2,128]{2,1,0:T(2,128)S(1)}, f32[512,2,128]{2,1,0:T(2,128)}, u32[]{:S(2)}) copy-start(f32[512,2,128]{2,1,0:T(2,128)} %param.13) | copy-start | bytes 1572868
  2.4 35.2 %copy-start.3 = (f32[512,2,128]{2,1,0:T(2,128)S(1)}, f32[512,2,128]{2,1,0:T(2,128)}, u32[]{:S(2)}) copy-start(f32[512,2,128]{2,1,0:T(2,128)} %param.14) | copy-start | bytes 1572868
  28.9 8.7 %copy-start = (f32[512,2,128]{2,1,0:T(2,128)S(1)}, f32[512,2,128]{2,1,0:T(2,128)}, u32[]{:S(2)}) copy-start(f32[512,2,128]{2,1,0:T(2,128)} %param.11) | copy-start | bytes 1572868
  28.9 8.7 %copy-start.1 = (f32[512,2,128]{2,1,0:T(2,128)S(1)}, f32[512,2,128]{2,1,0:T(2,128)}, u32[]{:S(2)}) copy-start(f32[512,2,128]{2,1,0:T(2,128)} %param.12) | copy-start | bytes 1572868
  29.6 9.0 %copy-start.5 = (bf16[3,256,768]{2,1,0:T(8,128)(2,1)S(1)}, bf16[3,256,768]{2,1,0:T(8,128)(2,1)}, u32[]{:S(2)}) copy-start(bf16[3,256,768]{2,1,0:T(8,128)(2,1)} %constant.20.clone.table_ref.refs_9_.refs_10_) | copy-start | bytes 3538948
  29.6 16.8 %collective-permute-start.2 = (f32[1032,128]{1,0:T(8,128)S(1)}, f32[1032,128]{1,0:T(8,128)S(1)}, u32[]{:S(2)}, u32[]{:S(2)}) collective-permute-start(f32[1032,128]{1,0:T(8,128)S(1)} %get-tuple-element.52.inner.refs_3_), channel_id=1, source_target_pairs={{0,16},{16,0},{32,48},{48,32},{64,80},{80,64},{96,112},{112,96},{1... | collective-permute-start | bytes 1585160 | tf_op jit(solution)/shard_map/ppermute | solution.py:337
  29.8 16.6 %collective-permute-start = (f32[520,128]{1,0:T(8,128)S(1)}, f32[520,128]{1,0:T(8,128)S(1)}, u32[]{:S(2)}, u32[]{:S(2)}) collective-permute-start(f32[520,128]{1,0:T(8,128)S(1)} %get-tuple-element.62), channel_id=1, source_target_pairs={{16,32},{32,16},{48,64},{64,48},{80,96},{96,80},{112,128},{128,112... | collective-permute-start | bytes 798728 | tf_op jit(solution)/shard_map/ppermute | solution.py:334
  31.9 14.5 %collective-permute-start.1 = (f32[512,128]{1,0:T(8,128)S(1)}, f32[512,128]{1,0:T(8,128)S(1)}, u32[]{:S(2)}, u32[]{:S(2)}) collective-permute-start(f32[512,128]{1,0:T(8,128)S(1)} %get-tuple-element.63), channel_id=1, source_target_pairs={{240,1},{1,240},{241,2},{2,241},{242,3},{3,242},{243,4},{4,243},{2... | collective-permute-start | bytes 786440 | tf_op jit(solution)/shard_map/ppermute | solution.py:335
  40.2 16.6 %collective-permute-start.3 = (f32[1024,128]{1,0:T(8,128)S(1)}, f32[1024,128]{1,0:T(8,128)S(1)}, u32[]{:S(2)}, u32[]{:S(2)}) collective-permute-start(f32[1024,128]{1,0:T(8,128)S(1)} %get-tuple-element.60.refs_0_), channel_id=1, source_target_pairs={{16,32},{32,16},{48,64},{64,48},{80,96},{96,80},{112,128},{128,112... | collective-permute-start | bytes 1572872 | tf_op jit(solution)/shard_map/ppermute | solution.py:319
  42.2 14.6 %collective-permute-start.4 = (f32[1024,128]{1,0:T(8,128)S(1)}, f32[1024,128]{1,0:T(8,128)S(1)}, u32[]{:S(2)}, u32[]{:S(2)}) collective-permute-start(f32[1024,128]{1,0:T(8,128)S(1)} %get-tuple-element.61.refs_1_), channel_id=1, source_target_pairs={{0,16},{16,0},{32,48},{48,32},{64,80},{80,64},{96,112},{112,96},{1... | collective-permute-start | bytes 1572872 | tf_op jit(solution)/shard_map/ppermute | solution.py:319
  48.0 23.1 %collective-permute-start.5 = (f32[1024,128]{1,0:T(8,128)S(1)}, f32[1024,128]{1,0:T(8,128)S(1)}, u32[]{:S(2)}, u32[]{:S(2)}) collective-permute-start(f32[1024,128]{1,0:T(8,128)S(1)} %get-tuple-element.65.refs_0_), channel_id=1, source_target_pairs={{16,32},{32,16},{48,64},{64,48},{80,96},{96,80},{112,128},{128,112... | collective-permute-start | bytes 1572872 | tf_op jit(solution)/shard_map/ppermute | solution.py:319
  50.1 21.1 %collective-permute-start.6 = (f32[1024,128]{1,0:T(8,128)S(1)}, f32[1024,128]{1,0:T(8,128)S(1)}, u32[]{:S(2)}, u32[]{:S(2)}) collective-permute-start(f32[1024,128]{1,0:T(8,128)S(1)} %get-tuple-element.66.refs_1_), channel_id=1, source_target_pairs={{0,16},{16,0},{32,48},{48,32},{64,80},{80,64},{96,112},{112,96},{1... | collective-permute-start | bytes 1572872 | tf_op jit(solution)/shard_map/ppermute | solution.py:319
  58.5 15.6 %collective-permute-start.7 = (f32[1024,128]{1,0:T(8,128)S(1)}, f32[1024,128]{1,0:T(8,128)S(1)}, u32[]{:S(2)}, u32[]{:S(2)}) collective-permute-start(f32[1024,128]{1,0:T(8,128)S(1)} %get-tuple-element.72.refs_0_), channel_id=1, source_target_pairs={{16,32},{32,16},{48,64},{64,48},{80,96},{96,80},{112,128},{128,112... | collective-permute-start | bytes 1572872 | tf_op jit(solution)/shard_map/ppermute | solution.py:319
  60.5 13.7 %collective-permute-start.8 = (f32[1024,128]{1,0:T(8,128)S(1)}, f32[1024,128]{1,0:T(8,128)S(1)}, u32[]{:S(2)}, u32[]{:S(2)}) collective-permute-start(f32[1024,128]{1,0:T(8,128)S(1)} %get-tuple-element.73.refs_1_), channel_id=1, source_target_pairs={{0,16},{16,0},{32,48},{48,32},{64,80},{80,64},{96,112},{112,96},{1... | collective-permute-start | bytes 1572872 | tf_op jit(solution)/shard_map/ppermute | solution.py:319

commit v6 on v5

--- a/solution.py
+++ b/solution.py
@@ -124,7 +124,7 @@
     )(*args)
 
 
-def split_kernel(core_ref, in_ref, diff_ref, outer, inner, pot_rim, vel_rim, beyond):
+def split_kernel(core_ref, in_ref, diff_ref, outer, inner, pot_rim, beyond):
     row = lax.broadcasted_iota(jnp.int32, (8, NR), 0)
     for side, out in enumerate((outer, inner)):
         own = jnp.broadcast_to(near(core_ref, diff_ref, side), (8, NR))
@@ -132,12 +132,14 @@
         out[pl.ds(2 * K, 8), :] = own
         if side == 0:
             pot_rim[pl.ds(K, 8), :] = own
+        else:
+            out[pl.ds(2 * K + 8, 8), :] = own
         for src in range(PEERS):
             for field in range(2):
                 piece = in_ref[src, 2 * side + field]
                 out[pl.ds(field * K + src * PER, PER), :] = piece
-                if side == 0:
-                    (pot_rim, vel_rim)[field][pl.ds(src * PER, PER), :] = piece
+                if side == 0 and field == 0:
+                    pot_rim[pl.ds(src * PER, PER), :] = piece
     for src in range(PEERS):
         beyond[pl.ds(src * PER, PER), :] = in_ref[src, 4]
 
@@ -211,12 +213,13 @@
     take = lambda n: [refs.pop(0) for _ in range(n)]
     parts, olds = take(2), take(2)
     if opening:
-        pot_rim, vel_rim, beyond, inner_rim = take(4)
+        pot_rim, slab_rim, beyond, inner_rim = take(4)
         comings = [
-            [pot_rim[pl.ds(0, K), :], vel_rim[...] + beyond[...]],
+            [slab_rim[field_rows(0), :] + pot_rim[pl.ds(0, K), :], slab_rim[field_rows(1), :] + beyond[...]],
             [inner_rim[field_rows(field), :] for field in range(2)],
         ]
-        others = [pot_rim[pl.ds(K, 8), :], inner_rim[pl.ds(2 * K, 8), :]]
+        ends = pl.ds(2 * K, 8)
+        others = [slab_rim[ends, :] + pot_rim[pl.ds(K, 8), :], inner_rim[ends, :]]
     else:
         rims, pasts, (edge_ref,) = take(2), take(2), take(1)
         comings = [[rim[field_rows(field), :] for field in range(2)] for rim in rims]
@@ -311,7 +314,6 @@
     block = shape((PEERS, 2, 2, PER, NR), F32)
     wide = shape((PEERS, 5, PER, NR), F32)
     plane = shape((2 * K, NR), F32)
-    opening = shape((2 * K + 8, NR), F32)
     tiles = shape((2, 2, 8, NR), F32)
     staging = [pltpu.VMEM((2, 32 * PER, NR), F32), pltpu.SemaphoreType.DMA((2, PER // CHUNK))]
 
@@ -323,16 +325,16 @@
     sent, place = lax.optimization_barrier((sent, place))
     got = lax.all_to_all(sent, "modes", split_axis=0, concat_axis=0, tiled=True)
     got, place, diffusivity, table = lax.optimization_barrier((got, place, diffusivity, table))
-    *start, pot_rim, vel_rim, beyond = call(
+    *start, pot_rim, beyond = call(
         split_kernel,
-        [opening] * 2 + [shape((K + 8, NR), F32)] + [shape((K, NR), F32)] * 2,
+        [shape((2 * K + rows, NR), F32) for rows in (8, 16)] + [shape((K + 8, NR), F32), shape((K, NR), F32)],
         [place, got, diffusivity],
         0,
         smem=1,
     )
     rims = [
-        lax.ppermute(pot_rim, AXES, outer_pairs),
-        lax.ppermute(vel_rim, AXES, slab_pairs),
+        lax.ppermute(pot_rim, AXES, [pair for pair in outer_pairs if pair not in slab_pairs]),
+        lax.ppermute(start[0], AXES, slab_pairs),
         beyond,
         lax.ppermute(start[1], AXES, inner_pairs),
     ]

time: 105 us -> 106 us (level)
  blocking collectives: 55.2 us -> 57.4 us
    ppermute x2, starting transfers between devices: 7.79 us -> 2.79 us  [the longest x1 2.12 us: on_device(): lax.ppermute(start[0], AXES, slab_pairs)]
    ppermute x3, starting transfers between devices: 6.02 us -> 9.69 us  [swap(): lax.ppermute(planes[0], AXES, outer_pairs)]
    all_to_all x2, blocking collectives: 55.2 us -> 57.4 us  [on_device(): got = lax.all_to_all(sent, 'modes', split_axis=0, concat_axis=0, tiled=True)]
    ppermute x3, waiting for transfers between devices: 7.74 us -> 6.04 us  [swap(): lax.ppermute(planes[0], AXES, outer_pairs)]
    ppermute x3, starting transfers between devices: 10.9 us -> 12.1 us  [swap(): lax.ppermute(planes[1], AXES, inner_pairs)]
  transfers between devices with their start and end apart: 9 -> 9, of which waited for: 3 -> 3; matrix products, arithmetic and copies ran while one was open for 0% -> 0% of each run, Pallas kernels for 7% -> 8%
where the time goes in v6:
time: 106 us
  blocking collectives  57.4 us (54%)
  starting transfers between devices  24.8 us (23%)
  Pallas kernels  11.8 us (11%)
  waiting for transfers between devices  11.2 us (11%)
    all_to_all x2, blocking collectives, on_device(): got = lax.all_to_all(sent, 'modes', split_axis=0, concat_axis=0, tiled=True)  57.4 us
    ppermute x3, starting transfers between devices, swap(): lax.ppermute(planes[1], AXES, inner_pairs)  12.1 us
    ppermute x3, starting transfers between devices, swap(): lax.ppermute(planes[0], AXES, outer_pairs)  9.69 us
    pallas_call x7, Pallas kernels, call(): pl.pallas_call(body, out_shape=out_shapes, in_specs=space, out_specs=[pl....  8.85 us
    ppermute x3, waiting for transfers between devices, swap(): lax.ppermute(planes[0], AXES, outer_pairs)  6.04 us
    ppermute x1, waiting for transfers between devices, on_device(): lax.ppermute(start[0], AXES, slab_pairs)  5.16 us
    pallas_call x2, Pallas kernels, moved(): pl.pallas_call(body, out_shape=out_shapes, in_specs=[pl.BlockSpec(memory_...  2.95 us
  transfers between devices with their start and end apart: 9, of which 3 were waited for; matrix products, arithmetic and copies ran while one was open for 0% of the time, Pallas kernels for 8%

profile of v6, /device:TPU:104, one launch (start us, length us, event | category | flops | bytes accessed | tf_op | source)
XLA Modules:
  0.0 106.2 jit_solution(4411564799746132566)
XLA Ops:
  0.6 0.1 pad_add_fusion.core_ref
  0.7 1.6 %shard_map.95 = f32[16,5,32,128]{3,2,1,0:T(8,128)S(1)} custom-call(f32[1024,128]{1,0:T(8,128)} %bitcast.14, f32[1024,128]{1,0:T(8,128)} %bitcast.15), custom_call_target="tpu_custom_call" | custom-call | bytes 2097152 | tf_op jit(solution)/shard_map/pallas_call | solution.py:116
  2.4 0.0 copy-start.4
  2.4 0.0 copy-start.2
  2.4 0.0 copy-start.3
  2.4 26.5 %all_to_all.10.in_ref = f32[16,5,32,128]{3,2,1,0:T(8,128)S(1)} all-to-all(f32[16,5,32,128]{3,2,1,0:T(8,128)S(1)} %shard_map.95), channel_id=1, replica_groups=mesh['modes'=16,'axial'=16] {'modes'}, dimensions={0} | all-to-all | bytes 2621440 | tf_op jit(solution)/shard_map/all_to_all | solution.py:326
  28.9 0.0 copy-done.4
  28.9 0.0 copy-start
  28.9 0.0 copy-start.1
  28.9 0.6 shard_map.96
  29.6 0.0 copy-start.5
  29.6 0.2 collective-permute-start.2
  29.8 2.1 %collective-permute-start.1 = (f32[1032,128]{1,0:T(8,128)S(1)}, f32[1032,128]{1,0:T(8,128)S(1)}, u32[]{:S(2)}, u32[]{:S(2)}) collective-permute-start(f32[1032,128]{1,0:T(8,128)S(1)} %get-tuple-element.50.outer.refs_2_), channel_id=1, source_target_pairs={{240,1},{1,240},{241,2},{2,241},{242,3},{3,242},{243,4},{4,243},{2... | collective-permute-start | bytes 1585160 | tf_op jit(solution)/shard_map/ppermute | solution.py:337
  31.9 0.7 collective-permute-start
  32.6 0.0 copy-done.2
  32.6 0.0 copy-done.3
  32.6 0.0 copy-done
  32.6 0.0 copy-done.1
  32.6 1.0 shard_map.97
  33.6 0.0 copy-done.5
  33.6 1.6 %shard_map.98 = (f32[1024,128]{1,0:T(8,128)S(1)}, f32[1024,128]{1,0:T(8,128)S(1)}) custom-call(f32[1032,128]{1,0:T(8,128)S(1)} %get-tuple-element.50.outer.refs_2_, f32[1040,128]{1,0:T(8,128)S(1)} %get-tuple-element.51.inner.refs_3_, f32[4,2,512,128]{3,2,1,0:T(8,128)S(1)} %get-tuple-element.56.factor_ref.refs_8_.refs_9_, bf16[3,256,768]{2,1,0:T(8,128)(2,1)S(1)} %copy-done.5, ...), custom_call_target="tpu_custom_call" | custom-call | flops 17179869184 | bytes 5402624 | tf_op jit(solution)/shard_map/pallas_call | solution.py:46
  35.2 5.7 %collective-permute-start.3 = (f32[1024,128]{1,0:T(8,128)S(1)}, f32[1024,128]{1,0:T(8,128)S(1)}, u32[]{:S(2)}, u32[]{:S(2)}) collective-permute-start(f32[1024,128]{1,0:T(8,128)S(1)} %get-tuple-element.59.refs_0_), channel_id=1, source_target_pairs={{16,32},{32,16},{48,64},{64,48},{80,96},{96,80},{112,128},{128,112... | collective-permute-start | bytes 1572872 | tf_op jit(solution)/shard_map/ppermute | solution.py:321
  40.9 0.1 collective-permute-start.4
  41.0 0.0 collective-permute-done.refs_4_
  41.0 5.2 %collective-permute-done.1.refs_5_ = f32[1032,128]{1,0:T(8,128)S(1)} collective-permute-done((f32[1032,128]{1,0:T(8,128)S(1)}, f32[1032,128]{1,0:T(8,128)S(1)}, u32[]{:S(2)}, u32[]{:S(2)}) %collective-permute-start.1) | collective-permute-done | bytes 528416 | tf_op jit(solution)/shard_map/ppermute | solution.py:337
  46.2 0.0 collective-permute-done.2.refs_7_
  46.2 1.8 %shard_map.99 = (f32[1024,128]{1,0:T(8,128)S(1)}, f32[1024,128]{1,0:T(8,128)S(1)}, f32[1024,128]{1,0:T(8,128)S(1)}, f32[1024,128]{1,0:T(8,128)S(1)}, f32[1024,12...) custom-call(f32[1024,128]{1,0:T(8,128)S(1)} %get-tuple-element.59.refs_0_, ...), custom_call_target="tpu_custom_call" | custom-call | flops 17179869184 | bytes 10145792 | tf_op jit(solution)/shard_map/pallas_call | solution.py:46
  47.9 1.9 %collective-permute-start.5 = (f32[1024,128]{1,0:T(8,128)S(1)}, f32[1024,128]{1,0:T(8,128)S(1)}, u32[]{:S(2)}, u32[]{:S(2)}) collective-permute-start(f32[1024,128]{1,0:T(8,128)S(1)} %get-tuple-element.63.refs_0_), channel_id=1, source_target_pairs={{16,32},{32,16},{48,64},{64,48},{80,96},{96,80},{112,128},{128,112... | collective-permute-start | bytes 1572872 | tf_op jit(solution)/shard_map/ppermute | solution.py:321
  49.9 0.1 collective-permute-start.6
  50.0 5.5 %collective-permute-done.3.refs_4_ = f32[1024,128]{1,0:T(8,128)S(1)} collective-permute-done((f32[1024,128]{1,0:T(8,128)S(1)}, f32[1024,128]{1,0:T(8,128)S(1)}, u32[]{:S(2)}, u32[]{:S(2)}) %collective-permute-start.3) | collective-permute-done | bytes 524320 | tf_op jit(solution)/shard_map/ppermute | solution.py:321
  55.5 0.0 collective-permute-done.4.refs_5_
  55.5 1.8 %shard_map.100 = (f32[1024,128]{1,0:T(8,128)S(1)}, f32[1024,128]{1,0:T(8,128)S(1)}, f32[1024,128]{1,0:T(8,128)S(1)}, f32[1024,128]{1,0:T(8,128)S(1)}, f32[1024,128]{1,0:T(8,128)S(1)}, /*index=5*/f32[1024,128]{1,0:T(8,128)S(1)}) custom-call(f32[1024,128]{1,0:T(8,128)S(1)} %get-tuple-element.63.refs_0_, f32[1024,128]{1,0:T(8,128)S(1)} %get-tuple-element.64.refs_1_, ...), custom_call_target="tpu_custom_call" | custom-call | flops 17179869184 | bytes 10641408 | tf_op jit(solution)/shard_map/pallas_call | solution.py:46
  57.3 2.1 %collective-permute-start.7 = (f32[1024,128]{1,0:T(8,128)S(1)}, f32[1024,128]{1,0:T(8,128)S(1)}, u32[]{:S(2)}, u32[]{:S(2)}) collective-permute-start(f32[1024,128]{1,0:T(8,128)S(1)} %get-tuple-element.70.refs_0_), channel_id=1, source_target_pairs={{16,32},{32,16},{48,64},{64,48},{80,96},{96,80},{112,128},{128,112... | collective-permute-start | bytes 1572872 | tf_op jit(solution)/shard_map/ppermute | solution.py:321
  59.4 11.9 %collective-permute-start.8 = (f32[1024,128]{1,0:T(8,128)S(1)}, f32[1024,128]{1,0:T(8,128)S(1)}, u32[]{:S(2)}, u32[]{:S(2)}) collective-permute-start(f32[1024,128]{1,0:T(8,128)S(1)} %get-tuple-element.71.refs_1_), channel_id=1, source_target_pairs={{0,16},{16,0},{32,48},{48,32},{64,80},{80,64},{96,112},{112,96},{1... | collective-permute-start | bytes 1572872 | tf_op jit(solution)/shard_map/ppermute | solution.py:321
  71.3 0.0 collective-permute-done.5.refs_4_
  71.3 0.0 collective-permute-done.6.refs_5_
  71.3 1.9 %shard_map.101 = (f32[1024,128]{1,0:T(8,128)S(1)}, f32[1024,128]{1,0:T(8,128)S(1)}, f32[1024,128]{1,0:T(8,128)S(1)}, f32[1024,128]{1,0:T(8,128)S(1)}, f32[1024,128]{1,0:T(8,128)S(1)}, /*index=5*/f32[1024,128]{1,0:T(8,128)S(1)}) custom-call(f32[1024,128]{1,0:T(8,128)S(1)} %get-tuple-element.70.refs_0_, f32[1024,128]{1,0:T(8,128)S(1)} %get-tuple-element.71.refs_1_, ...), custom_call_target="tpu_custom_call" | custom-call | flops 17179869184 | bytes 10641408 | tf_op jit(solution)/shard_map/pallas_call | solution.py:46
  73.2 0.5 collective-permute-done.7.refs_4_
  73.7 0.0 collective-permute-done.8.refs_5_
  73.7 0.2 shard_map.102
  73.9 30.9 %all_to_all.11.in_ref = f32[16,2,2,32,128]{4,3,2,1,0:T(8,128)S(1)} all-to-all(f32[16,2,2,32,128]{4,3,2,1,0:T(8,128)S(1)} %shard_map.102), channel_id=1, replica_groups=mesh['modes'=16,'axial'=16] {'modes'}, dimensions={0} | all-to-all | bytes 2097152 | tf_op jit(solution)/shard_map/all_to_all | solution.py:365
  104.8 1.3 %shard_map.103 = (f32[1024,128]{1,0:T(8,128)}, f32[1024,128]{1,0:T(8,128)}) custom-call(f32[16,2,2,32,128]{4,3,2,1,0:T(8,128)S(1)} %all_to_all.11.in_ref), custom_call_target="tpu_custom_call" | custom-call | bytes 2097152 | tf_op jit(solution)/shard_map/pallas_call | solution.py:116
Async XLA Ops:
  2.4 26.5 %copy-start.4 = (f32[32,128]{1,0:T(8,128)S(1)}, f32[32,128]{1,0:T(8,128)}, u32[]{:S(2)}) copy-start(f32[32,128]{1,0:T(8,128)} %diff_ref.1) | copy-start | bytes 49156
  2.4 30.2 %copy-start.2 = (f32[512,2,128]{2,1,0:T(2,128)S(1)}, f32[512,2,128]{2,1,0:T(2,128)}, u32[]{:S(2)}) copy-start(f32[512,2,128]{2,1,0:T(2,128)} %param.13) | copy-start | bytes 1572868
  2.4 30.2 %copy-start.3 = (f32[512,2,128]{2,1,0:T(2,128)S(1)}, f32[512,2,128]{2,1,0:T(2,128)}, u32[]{:S(2)}) copy-start(f32[512,2,128]{2,1,0:T(2,128)} %param.14) | copy-start | bytes 1572868
  28.9 3.7 %copy-start = (f32[512,2,128]{2,1,0:T(2,128)S(1)}, f32[512,2,128]{2,1,0:T(2,128)}, u32[]{:S(2)}) copy-start(f32[512,2,128]{2,1,0:T(2,128)} %param.11) | copy-start | bytes 1572868
  28.9 3.7 %copy-start.1 = (f32[512,2,128]{2,1,0:T(2,128)S(1)}, f32[512,2,128]{2,1,0:T(2,128)}, u32[]{:S(2)}) copy-start(f32[512,2,128]{2,1,0:T(2,128)} %param.12) | copy-start | bytes 1572868
  29.6 4.0 %copy-start.5 = (bf16[3,256,768]{2,1,0:T(8,128)(2,1)S(1)}, bf16[3,256,768]{2,1,0:T(8,128)(2,1)}, u32[]{:S(2)}) copy-start(bf16[3,256,768]{2,1,0:T(8,128)(2,1)} %constant.20.clone.table_ref.refs_9_.refs_10_) | copy-start | bytes 3538948
  29.6 16.6 %collective-permute-start.2 = (f32[1040,128]{1,0:T(8,128)S(1)}, f32[1040,128]{1,0:T(8,128)S(1)}, u32[]{:S(2)}, u32[]{:S(2)}) collective-permute-start(f32[1040,128]{1,0:T(8,128)S(1)} %get-tuple-element.51.inner.refs_3_), channel_id=1, source_target_pairs={{0,16},{16,0},{32,48},{48,32},{64,80},{80,64},{96,112},{112,96},{1... | collective-permute-start | bytes 1597448 | tf_op jit(solution)/shard_map/ppermute | solution.py:339
  29.8 16.4 %collective-permute-start.1 = (f32[1032,128]{1,0:T(8,128)S(1)}, f32[1032,128]{1,0:T(8,128)S(1)}, u32[]{:S(2)}, u32[]{:S(2)}) collective-permute-start(f32[1032,128]{1,0:T(8,128)S(1)} %get-tuple-element.50.outer.refs_2_), channel_id=1, source_target_pairs={{240,1},{1,240},{241,2},{2,241},{242,3},{3,242},{243,4},{4,243},{2... | collective-permute-start | bytes 1585160 | tf_op jit(solution)/shard_map/ppermute | solution.py:337
  31.9 9.1 %collective-permute-start = (f32[520,128]{1,0:T(8,128)S(1)}, f32[520,128]{1,0:T(8,128)S(1)}, u32[]{:S(2)}, u32[]{:S(2)}) collective-permute-start(f32[520,128]{1,0:T(8,128)S(1)} %get-tuple-element.61), channel_id=1, source_target_pairs={{16,32},{32,16},{48,64},{64,48},{80,96},{96,80},{112,128},{128,112... | collective-permute-start | bytes 798728 | tf_op jit(solution)/shard_map/ppermute | solution.py:336
  35.2 20.3 %collective-permute-start.3 = (f32[1024,128]{1,0:T(8,128)S(1)}, f32[1024,128]{1,0:T(8,128)S(1)}, u32[]{:S(2)}, u32[]{:S(2)}) collective-permute-start(f32[1024,128]{1,0:T(8,128)S(1)} %get-tuple-element.59.refs_0_), channel_id=1, source_target_pairs={{16,32},{32,16},{48,64},{64,48},{80,96},{96,80},{112,128},{128,112... | collective-permute-start | bytes 1572872 | tf_op jit(solution)/shard_map/ppermute | solution.py:321
  40.9 14.6 %collective-permute-start.4 = (f32[1024,128]{1,0:T(8,128)S(1)}, f32[1024,128]{1,0:T(8,128)S(1)}, u32[]{:S(2)}, u32[]{:S(2)}) collective-permute-start(f32[1024,128]{1,0:T(8,128)S(1)} %get-tuple-element.60.refs_1_), channel_id=1, source_target_pairs={{0,16},{16,0},{32,48},{48,32},{64,80},{80,64},{96,112},{112,96},{1... | collective-permute-start | bytes 1572872 | tf_op jit(solution)/shard_map/ppermute | solution.py:321
  47.9 23.4 %collective-permute-start.5 = (f32[1024,128]{1,0:T(8,128)S(1)}, f32[1024,128]{1,0:T(8,128)S(1)}, u32[]{:S(2)}, u32[]{:S(2)}) collective-permute-start(f32[1024,128]{1,0:T(8,128)S(1)} %get-tuple-element.63.refs_0_), channel_id=1, source_target_pairs={{16,32},{32,16},{48,64},{64,48},{80,96},{96,80},{112,128},{128,112... | collective-permute-start | bytes 1572872 | tf_op jit(solution)/shard_map/ppermute | solution.py:321
  49.9 21.5 %collective-permute-start.6 = (f32[1024,128]{1,0:T(8,128)S(1)}, f32[1024,128]{1,0:T(8,128)S(1)}, u32[]{:S(2)}, u32[]{:S(2)}) collective-permute-start(f32[1024,128]{1,0:T(8,128)S(1)} %get-tuple-element.64.refs_1_), channel_id=1, source_target_pairs={{0,16},{16,0},{32,48},{48,32},{64,80},{80,64},{96,112},{112,96},{1... | collective-permute-start | bytes 1572872 | tf_op jit(solution)/shard_map/ppermute | solution.py:321
  57.3 16.4 %collective-permute-start.7 = (f32[1024,128]{1,0:T(8,128)S(1)}, f32[1024,128]{1,0:T(8,128)S(1)}, u32[]{:S(2)}, u32[]{:S(2)}) collective-permute-start(f32[1024,128]{1,0:T(8,128)S(1)} %get-tuple-element.70.refs_0_), channel_id=1, source_target_pairs={{16,32},{32,16},{48,64},{64,48},{80,96},{96,80},{112,128},{128,112... | collective-permute-start | bytes 1572872 | tf_op jit(solution)/shard_map/ppermute | solution.py:321
  59.4 14.3 %collective-permute-start.8 = (f32[1024,128]{1,0:T(8,128)S(1)}, f32[1024,128]{1,0:T(8,128)S(1)}, u32[]{:S(2)}, u32[]{:S(2)}) collective-permute-start(f32[1024,128]{1,0:T(8,128)S(1)} %get-tuple-element.71.refs_1_), channel_id=1, source_target_pairs={{0,16},{16,0},{32,48},{48,32},{64,80},{80,64},{96,112},{112,96},{1... | collective-permute-start | bytes 1572872 | tf_op jit(solution)/shard_map/ppermute | solution.py:321

commit v7 on v3

--- a/solution.py
+++ b/solution.py
@@ -86,14 +86,22 @@
                 ]
 
 
-def unpack_kernel(in_ref, pot_ref, vel_ref, rows, sems):
+def unpack_kernel(in_ref, diff_ref, pot_ref, vel_ref, rows, sems):
     leave = []
     for chunk in range(PER // CHUNK):
+        modes = pl.ds(chunk * CHUNK, CHUNK)
         for field, ref in enumerate((pot_ref, vel_ref)):
+            flows = {}
+            for left in range(1, PEERS - 1, 2):
+                pair = diff_ref[pl.ds(2 * left + 1, 1), :] + diff_ref[pl.ds(2 * left + 2, 1), :]
+                coef = DT * 0.5 * pair if field == 0 else DT
+                flow = coef * (in_ref[left + 1, 4 + field, modes] - in_ref[left, 4 + field, modes])
+                flows[left], flows[left + 1] = flow, -flow
             for peer, side, plane in planes():
-                rows[field, pl.ds(chunk * CHUNK * 32 + plane, CHUNK, stride=32), :] = in_ref[
-                    peer, side, field, pl.ds(chunk * CHUNK, CHUNK)
-                ]
+                value = in_ref[peer, 2 * side + field, modes]
+                if side == 0 and peer in flows:
+                    value = value + flows[peer]
+                rows[field, pl.ds(chunk * CHUNK * 32 + plane, CHUNK, stride=32), :] = value
             leave.append(
                 pltpu.make_async_copy(
                     rows.at[field, chunk_rows(chunk)], ref.at[chunk_rows(chunk)], sems.at[field, chunk]
@@ -127,7 +135,9 @@
                 out[pl.ds(field * K + src * PER, PER), :] = in_ref[src, side, field]
         own = near(core_ref, diff_ref, side)
         row = lax.broadcasted_iota(jnp.int32, (8, NR), 0)
-        out[pl.ds(2 * K, 8), :] = jnp.where(row == 0, jnp.broadcast_to(own, (8, NR)), 1.0)
+        held = jnp.full((8, NR), core_ref[2], jnp.int32).astype(F32)
+        ends = jnp.where(row == 3, held, 1.0)
+        out[pl.ds(2 * K, 8), :] = jnp.where(row == 0, jnp.broadcast_to(own, (8, NR)), ends)
 
 
 def near(core_ref, diff_ref, side):
@@ -206,7 +216,8 @@
         for side in range(2):
             own, other = (ref[pl.ds(2 * K, 8), :] for ref in (olds[side], rims[side]))
             row = lax.broadcasted_iota(jnp.int32, (8, NR), 0)
-            edge_ref[side] = jnp.where(row < 2, DT * 0.5 * (own + other), other)
+            other = jnp.where(row < 2, DT * 0.5 * (own + other), other)
+            edge_ref[side] = jnp.where(row == 3, 1.0 - own, other)
     for side in range(2):
         for field in range(2):
             rows = field_rows(field)
@@ -266,10 +277,12 @@
         for field in range(2):
             for dest in range(PEERS):
                 rows = pl.ds(field * K + dest * PER, PER)
-                flow = flux(
-                    edge_ref, side, field, rims[side][rows, :], olds[side][rows, :], pasts[side][rows, :]
-                )
-                out_ref[dest, side, field] = parts[side][rows, :] + flow
+                old = olds[side][rows, :]
+                flow = flux(edge_ref, side, field, rims[side][rows, :], old, pasts[side][rows, :])
+                if side == 0:
+                    flow = edge_ref[0, pl.ds(3, 1), :] * flow
+                    out_ref[dest, 4 + field] = old
+                out_ref[dest, 2 * side + field] = parts[side][rows, :] + flow
 
 
 def swaps():
@@ -277,14 +290,17 @@
     inner, outer = [], []
     for g in range(255):
         (inner if g % 2 == 0 else outer).extend([(spot(g), spot(g + 1)), (spot(g + 1), spot(g))])
-    return inner, outer
+    slab = [pair for pair in outer if pair[0] % 16 != pair[1] % 16]
+    return inner, outer, slab
 
 
 def on_device(pot, vel, diffusivity, *factors):
     shape = jax.ShapeDtypeStruct
     modes = lax.axis_index("modes").astype(jnp.int32)
-    place = jnp.stack([modes % 2, 2 * modes])
-    inner_pairs, outer_pairs = swaps()
+    beyond = 2 * modes + 3 * (modes % 2) - 1
+    held = (beyond >= 0) & (beyond < 2 * PEERS)
+    place = jnp.stack([modes % 2, 2 * modes, held.astype(jnp.int32)])
+    inner_pairs, outer_pairs, slab_pairs = swaps()
     table = jnp.asarray(tables())
     block = shape((PEERS, 2, 2, PER, NR), F32)
     plane = shape((2 * K, NR), F32)
@@ -292,8 +308,8 @@
     tiles = shape((2, 2, 8, NR), F32)
     staging = [pltpu.VMEM((2, 32 * PER, NR), F32), pltpu.SemaphoreType.DMA((2, PER // CHUNK))]
 
-    def swap(planes):
-        return [lax.ppermute(planes[0], AXES, outer_pairs), lax.ppermute(planes[1], AXES, inner_pairs)]
+    def swap(planes, pairs=outer_pairs):
+        return [lax.ppermute(planes[0], AXES, pairs), lax.ppermute(planes[1], AXES, inner_pairs)]
 
     flat = [a.reshape(-1, NR) for a in (pot, vel)]
     (sent,) = moved(pack_kernel, [block], flat, (pltpu.HBM, pltpu.VMEM), staging)
@@ -315,7 +331,7 @@
     parts = call(first_kernel, [plane] * 2, [*start, *shared], flops)
     olds, pasts = start, []
     for step in range(1, STEPS):
-        coming = swap(parts)
+        coming = swap(parts, outer_pairs if step < STEPS - 1 else slab_pairs)
         outs = call(
             functools.partial(next_kernel, step == 1),
             [plane] * 6 + ([shape((2, 8, NR), F32)] if step == 1 else []),
@@ -325,9 +341,9 @@
         parts, olds = outs[:2], outs[2:4]
         edge = outs[6] if step == 1 else edge
         pasts, rims = [*outs[4:6], edge], coming
-    (sent,) = call(last_kernel, [block], [*parts, *olds, *rims, *pasts], 0)
+    (sent,) = call(last_kernel, [shape((PEERS, 6, PER, NR), F32)], [*parts, *olds, *rims, *pasts], 0)
     got = lax.all_to_all(sent, "modes", split_axis=0, concat_axis=0, tiled=True)
-    outs = moved(unpack_kernel, [shape((32 * PER, NR), F32)] * 2, [got], (pltpu.VMEM, pltpu.HBM), staging)
+    outs = moved(unpack_kernel, [shape((32 * PER, NR), F32)] * 2, [got, diffusivity], (pltpu.VMEM, pltpu.HBM), staging)
     return tuple(a.reshape(PER, 32, NR) for a in outs)
 
 

time: 105 us -> 107 us (1.019)
  blocking collectives: 47.4 us -> 52.8 us
  waiting for transfers between devices: 16.9 us -> 13.1 us
    all_to_all x2, blocking collectives: 47.4 us -> 52.8 us  [on_device(): got = lax.all_to_all(sent, 'modes', split_axis=0, concat_axis=0, tiled=True)]
    ppermute x4, waiting for transfers between devices: 16.9 us -> 13.1 us  [swap(): lax.ppermute(planes[0], AXES, pairs)]
where the time goes in v7:
time: 107 us; the launch traced here: 105 us
  blocking collectives  52.8 us (49%)
  starting transfers between devices  26.4 us (25%)
  waiting for transfers between devices  13.1 us (12%)
  Pallas kernels  11.9 us (11%)
    all_to_all x2, blocking collectives, on_device(): got = lax.all_to_all(sent, 'modes', split_axis=0, concat_axis=0, tiled=True)  52.8 us
    ppermute x4, starting transfers between devices, swap(): lax.ppermute(planes[1], AXES, inner_pairs)  13.6 us
    ppermute x4, waiting for transfers between devices, swap(): lax.ppermute(planes[0], AXES, pairs)  13.1 us
    ppermute x4, starting transfers between devices, swap(): lax.ppermute(planes[0], AXES, pairs)  12.7 us
    pallas_call x7, Pallas kernels, call(): pl.pallas_call(body, out_shape=out_shapes, in_specs=space, out_specs=[pl....  8.9 us
    pallas_call x2, Pallas kernels, moved(): pl.pallas_call(body, out_shape=out_shapes, in_specs=[pl.BlockSpec(memory_...  3.04 us
  transfers between devices with their start and end apart: 8, of which 2 were waited for; matrix products, arithmetic and copies ran while one was open for 0% of the time, Pallas kernels for 8%

profile of v7, /device:TPU:104, one launch (start us, length us, event | category | flops | bytes accessed | tf_op | source)
XLA Modules:
  0.0 105.1 jit_solution(15981823626958315548)
XLA Ops:
  0.6 1.6 %shard_map.95 = f32[16,2,2,32,128]{4,3,2,1,0:T(8,128)S(1)} custom-call(f32[1024,128]{1,0:T(8,128)} %bitcast.15, f32[1024,128]{1,0:T(8,128)} %bitcast.16), custom_call_target="tpu_custom_call" | custom-call | bytes 2097152 | tf_op jit(solution)/shard_map/pallas_call | solution.py:120
  2.3 0.0 copy-start.5
  2.3 0.1 pad_add_fusion.core_ref
  2.4 0.0 copy-start.1
  2.4 0.0 copy-start.2
  2.4 0.0 copy-start.3
  2.4 0.0 copy-start.4
  2.4 24.0 %all_to_all.10.in_ref = f32[16,2,2,32,128]{4,3,2,1,0:T(8,128)S(1)} all-to-all(f32[16,2,2,32,128]{4,3,2,1,0:T(8,128)S(1)} %shard_map.95), channel_id=1, replica_groups=mesh['modes'=16,'axial'=16] {'modes'}, dimensions={0} | all-to-all | bytes 2097152 | tf_op jit(solution)/shard_map/all_to_all | solution.py:317
  26.4 0.0 copy-done.5
  26.4 0.0 copy-start
  26.4 0.6 shard_map.96
  27.1 1.9 %collective-permute-start = (f32[1032,128]{1,0:T(8,128)S(1)}, f32[1032,128]{1,0:T(8,128)S(1)}, u32[]{:S(2)}, u32[]{:S(2)}) collective-permute-start(f32[1032,128]{1,0:T(8,128)S(1)} %get-tuple-element.48.outer.refs_2_), channel_id=1, source_target_pairs={{16,32},{32,16},{48,64},{64,48},{80,96},{96,80},{112,128},{128,112... | collective-permute-start | bytes 1585160 | tf_op jit(solution)/shard_map/ppermute | solution.py:312
  29.0 0.6 collective-permute-start.1
  29.6 0.0 copy-done.1
  29.6 0.0 copy-done.2
  29.6 0.0 copy-done.3
  29.6 0.0 copy-done.4
  29.6 1.0 shard_map.97
  30.6 0.0 copy-done
  30.6 1.7 %shard_map.98 = (f32[1024,128]{1,0:T(8,128)S(1)}, f32[1024,128]{1,0:T(8,128)S(1)}) custom-call(f32[1032,128]{1,0:T(8,128)S(1)} %get-tuple-element.48.outer.refs_2_, f32[1032,128]{1,0:T(8,128)S(1)} %get-tuple-element.49.inner.refs_3_, f32[4,2,512,128]{3,2,1,0:T(8,128)S(1)} %get-tuple-element.54.factor_ref.refs_6_.refs_9_, bf16[3,256,768]{2,1,0:T(8,128)(2,1)S(1)} %copy-done, ...), custom_call_target="tpu_custom_call" | custom-call | flops 805306368 | bytes 5398528 | tf_op jit(solution)/shard_map/pallas_call | solution.py:46
  32.2 5.3 %collective-permute-start.2 = (f32[1024,128]{1,0:T(8,128)S(1)}, f32[1024,128]{1,0:T(8,128)S(1)}, u32[]{:S(2)}, u32[]{:S(2)}) collective-permute-start(f32[1024,128]{1,0:T(8,128)S(1)} %get-tuple-element.57.refs_0_), channel_id=1, source_target_pairs={{16,32},{32,16},{48,64},{64,48},{80,96},{96,80},{112,128},{128,112... | collective-permute-start | bytes 1572872 | tf_op jit(solution)/shard_map/ppermute | solution.py:312
  37.6 0.1 collective-permute-start.3
  37.7 6.0 %collective-permute-done.refs_4_ = f32[1032,128]{1,0:T(8,128)S(1)} collective-permute-done((f32[1032,128]{1,0:T(8,128)S(1)}, f32[1032,128]{1,0:T(8,128)S(1)}, u32[]{:S(2)}, u32[]{:S(2)}) %collective-permute-start) | collective-permute-done | bytes 528416 | tf_op jit(solution)/shard_map/ppermute | solution.py:312
  43.7 0.0 collective-permute-done.1.refs_5_
  43.7 1.8 %shard_map.99 = (f32[1024,128]{1,0:T(8,128)S(1)}, f32[1024,128]{1,0:T(8,128)S(1)}, f32[1024,128]{1,0:T(8,128)S(1)}, f32[1024,128]{1,0:T(8,128)S(1)}, f32[1024,12...) custom-call(f32[1024,128]{1,0:T(8,128)S(1)} %get-tuple-element.57.refs_0_, ...), custom_call_target="tpu_custom_call" | custom-call | flops 805306368 | bytes 9609216 | tf_op jit(solution)/shard_map/pallas_call | solution.py:46
  45.5 1.9 %collective-permute-start.4 = (f32[1024,128]{1,0:T(8,128)S(1)}, f32[1024,128]{1,0:T(8,128)S(1)}, u32[]{:S(2)}, u32[]{:S(2)}) collective-permute-start(f32[1024,128]{1,0:T(8,128)S(1)} %get-tuple-element.59.refs_0_), channel_id=1, source_target_pairs={{16,32},{32,16},{48,64},{64,48},{80,96},{96,80},{112,128},{128,112... | collective-permute-start | bytes 1572872 | tf_op jit(solution)/shard_map/ppermute | solution.py:312
  47.4 12.9 %collective-permute-start.5 = (f32[1024,128]{1,0:T(8,128)S(1)}, f32[1024,128]{1,0:T(8,128)S(1)}, u32[]{:S(2)}, u32[]{:S(2)}) collective-permute-start(f32[1024,128]{1,0:T(8,128)S(1)} %get-tuple-element.60.refs_1_), channel_id=1, source_target_pairs={{0,16},{16,0},{32,48},{48,32},{64,80},{80,64},{96,112},{112,96},{1... | collective-permute-start | bytes 1572872 | tf_op jit(solution)/shard_map/ppermute | solution.py:312
  60.3 0.0 collective-permute-done.2.refs_4_
  60.3 0.0 collective-permute-done.3.refs_5_
  60.3 1.8 %shard_map.100 = (f32[1024,128]{1,0:T(8,128)S(1)}, f32[1024,128]{1,0:T(8,128)S(1)}, f32[1024,128]{1,0:T(8,128)S(1)}, f32[1024,128]{1,0:T(8,128)S(1)}, f32[1024,128]{1,0:T(8,128)S(1)}, /*index=5*/f32[1024,128]{1,0:T(8,128)S(1)}) custom-call(f32[1024,128]{1,0:T(8,128)S(1)} %get-tuple-element.59.refs_0_, f32[1024,128]{1,0:T(8,128)S(1)} %get-tuple-element.60.refs_1_, ...), custom_call_target="tpu_custom_call" | custom-call | flops 805306368 | bytes 10641408 | tf_op jit(solution)/shard_map/pallas_call | solution.py:46
  62.1 3.6 %collective-permute-start.6 = (f32[1024,128]{1,0:T(8,128)S(1)}, f32[1024,128]{1,0:T(8,128)S(1)}, u32[]{:S(2)}, u32[]{:S(2)}) collective-permute-start(f32[1024,128]{1,0:T(8,128)S(1)} %get-tuple-element.66.refs_0_), channel_id=1, source_target_pairs={{240,1},{1,240},{241,2},{2,241},{242,3},{3,242},{243,4},{4,243},{2... | collective-permute-start | bytes 1572872 | tf_op jit(solution)/shard_map/ppermute | solution.py:312
  65.7 0.1 collective-permute-start.7
  65.8 0.0 collective-permute-done.4.refs_4_
  65.8 0.0 collective-permute-done.5.refs_5_
  65.8 1.9 %shard_map.101 = (f32[1024,128]{1,0:T(8,128)S(1)}, f32[1024,128]{1,0:T(8,128)S(1)}, f32[1024,128]{1,0:T(8,128)S(1)}, f32[1024,128]{1,0:T(8,128)S(1)}, f32[1024,128]{1,0:T(8,128)S(1)}, /*index=5*/f32[1024,128]{1,0:T(8,128)S(1)}) custom-call(f32[1024,128]{1,0:T(8,128)S(1)} %get-tuple-element.66.refs_0_, f32[1024,128]{1,0:T(8,128)S(1)} %get-tuple-element.67.refs_1_, ...), custom_call_target="tpu_custom_call" | custom-call | flops 805306368 | bytes 10641408 | tf_op jit(solution)/shard_map/pallas_call | solution.py:46
  67.7 7.0 %collective-permute-done.6.refs_4_ = f32[1024,128]{1,0:T(8,128)S(1)} collective-permute-done((f32[1024,128]{1,0:T(8,128)S(1)}, f32[1024,128]{1,0:T(8,128)S(1)}, u32[]{:S(2)}, u32[]{:S(2)}) %collective-permute-start.6) | collective-permute-done | bytes 524320 | tf_op jit(solution)/shard_map/ppermute | solution.py:312
  74.7 0.0 collective-permute-done.7.refs_5_
  74.7 0.2 shard_map.102
  74.9 28.7 %all_to_all.11.in_ref = f32[16,6,32,128]{3,2,1,0:T(8,128)S(1)} all-to-all(f32[16,6,32,128]{3,2,1,0:T(8,128)S(1)} %shard_map.102), channel_id=1, replica_groups=mesh['modes'=16,'axial'=16] {'modes'}, dimensions={0} | all-to-all | bytes 3145728 | tf_op jit(solution)/shard_map/all_to_all | solution.py:345
  103.7 1.4 %shard_map.103 = (f32[1024,128]{1,0:T(8,128)}, f32[1024,128]{1,0:T(8,128)}) custom-call(f32[16,6,32,128]{3,2,1,0:T(8,128)S(1)} %all_to_all.11.in_ref, f32[32,128]{1,0:T(8,128)S(1)} %copy-done.5), custom_call_target="tpu_custom_call" | custom-call | bytes 2097152 | tf_op jit(solution)/shard_map/pallas_call | solution.py:120
Async XLA Ops:
  2.3 24.2 %copy-start.5 = (f32[32,128]{1,0:T(8,128)S(1)}, f32[32,128]{1,0:T(8,128)}, u32[]{:S(2)}) copy-start(f32[32,128]{1,0:T(8,128)} %diff_ref.2) | copy-start | bytes 49156
  2.4 27.2 %copy-start.1 = (f32[512,2,128]{2,1,0:T(2,128)S(1)}, f32[512,2,128]{2,1,0:T(2,128)}, u32[]{:S(2)}) copy-start(f32[512,2,128]{2,1,0:T(2,128)} %param.11) | copy-start | bytes 1572868
  2.4 27.2 %copy-start.2 = (f32[512,2,128]{2,1,0:T(2,128)S(1)}, f32[512,2,128]{2,1,0:T(2,128)}, u32[]{:S(2)}) copy-start(f32[512,2,128]{2,1,0:T(2,128)} %param.12) | copy-start | bytes 1572868
  2.4 27.2 %copy-start.3 = (f32[512,2,128]{2,1,0:T(2,128)S(1)}, f32[512,2,128]{2,1,0:T(2,128)}, u32[]{:S(2)}) copy-start(f32[512,2,128]{2,1,0:T(2,128)} %param.13) | copy-start | bytes 1572868
  2.4 27.2 %copy-start.4 = (f32[512,2,128]{2,1,0:T(2,128)S(1)}, f32[512,2,128]{2,1,0:T(2,128)}, u32[]{:S(2)}) copy-start(f32[512,2,128]{2,1,0:T(2,128)} %param.14) | copy-start | bytes 1572868
  26.4 4.1 %copy-start = (bf16[3,256,768]{2,1,0:T(8,128)(2,1)S(1)}, bf16[3,256,768]{2,1,0:T(8,128)(2,1)}, u32[]{:S(2)}) copy-start(bf16[3,256,768]{2,1,0:T(8,128)(2,1)} %constant.30.clone.table_ref.refs_7_.refs_10_) | copy-start | bytes 3538948
  27.1 16.6 %collective-permute-start = (f32[1032,128]{1,0:T(8,128)S(1)}, f32[1032,128]{1,0:T(8,128)S(1)}, u32[]{:S(2)}, u32[]{:S(2)}) collective-permute-start(f32[1032,128]{1,0:T(8,128)S(1)} %get-tuple-element.48.outer.refs_2_), channel_id=1, source_target_pairs={{16,32},{32,16},{48,64},{64,48},{80,96},{96,80},{112,128},{128,112... | collective-permute-start | bytes 1585160 | tf_op jit(solution)/shard_map/ppermute | solution.py:312
  29.0 14.7 %collective-permute-start.1 = (f32[1032,128]{1,0:T(8,128)S(1)}, f32[1032,128]{1,0:T(8,128)S(1)}, u32[]{:S(2)}, u32[]{:S(2)}) collective-permute-start(f32[1032,128]{1,0:T(8,128)S(1)} %get-tuple-element.49.inner.refs_3_), channel_id=1, source_target_pairs={{0,16},{16,0},{32,48},{48,32},{64,80},{80,64},{96,112},{112,96},{1... | collective-permute-start | bytes 1585160 | tf_op jit(solution)/shard_map/ppermute | solution.py:312
  32.2 28.1 %collective-permute-start.2 = (f32[1024,128]{1,0:T(8,128)S(1)}, f32[1024,128]{1,0:T(8,128)S(1)}, u32[]{:S(2)}, u32[]{:S(2)}) collective-permute-start(f32[1024,128]{1,0:T(8,128)S(1)} %get-tuple-element.57.refs_0_), channel_id=1, source_target_pairs={{16,32},{32,16},{48,64},{64,48},{80,96},{96,80},{112,128},{128,112... | collective-permute-start | bytes 1572872 | tf_op jit(solution)/shard_map/ppermute | solution.py:312
  37.6 22.7 %collective-permute-start.3 = (f32[1024,128]{1,0:T(8,128)S(1)}, f32[1024,128]{1,0:T(8,128)S(1)}, u32[]{:S(2)}, u32[]{:S(2)}) collective-permute-start(f32[1024,128]{1,0:T(8,128)S(1)} %get-tuple-element.58.refs_1_), channel_id=1, source_target_pairs={{0,16},{16,0},{32,48},{48,32},{64,80},{80,64},{96,112},{112,96},{1... | collective-permute-start | bytes 1572872 | tf_op jit(solution)/shard_map/ppermute | solution.py:312
  45.5 20.3 %collective-permute-start.4 = (f32[1024,128]{1,0:T(8,128)S(1)}, f32[1024,128]{1,0:T(8,128)S(1)}, u32[]{:S(2)}, u32[]{:S(2)}) collective-permute-start(f32[1024,128]{1,0:T(8,128)S(1)} %get-tuple-element.59.refs_0_), channel_id=1, source_target_pairs={{16,32},{32,16},{48,64},{64,48},{80,96},{96,80},{112,128},{128,112... | collective-permute-start | bytes 1572872 | tf_op jit(solution)/shard_map/ppermute | solution.py:312
  47.4 18.4 %collective-permute-start.5 = (f32[1024,128]{1,0:T(8,128)S(1)}, f32[1024,128]{1,0:T(8,128)S(1)}, u32[]{:S(2)}, u32[]{:S(2)}) collective-permute-start(f32[1024,128]{1,0:T(8,128)S(1)} %get-tuple-element.60.refs_1_), channel_id=1, source_target_pairs={{0,16},{16,0},{32,48},{48,32},{64,80},{80,64},{96,112},{112,96},{1... | collective-permute-start | bytes 1572872 | tf_op jit(solution)/shard_map/ppermute | solution.py:312
  62.1 12.6 %collective-permute-start.6 = (f32[1024,128]{1,0:T(8,128)S(1)}, f32[1024,128]{1,0:T(8,128)S(1)}, u32[]{:S(2)}, u32[]{:S(2)}) collective-permute-start(f32[1024,128]{1,0:T(8,128)S(1)} %get-tuple-element.66.refs_0_), channel_id=1, source_target_pairs={{240,1},{1,240},{241,2},{2,241},{242,3},{3,242},{243,4},{4,243},{2... | collective-permute-start | bytes 1572872 | tf_op jit(solution)/shard_map/ppermute | solution.py:312
  65.7 9.0 %collective-permute-start.7 = (f32[1024,128]{1,0:T(8,128)S(1)}, f32[1024,128]{1,0:T(8,128)S(1)}, u32[]{:S(2)}, u32[]{:S(2)}) collective-permute-start(f32[1024,128]{1,0:T(8,128)S(1)} %get-tuple-element.67.refs_1_), channel_id=1, source_target_pairs={{0,16},{16,0},{32,48},{48,32},{64,80},{80,64},{96,112},{112,96},{1... | collective-permute-start | bytes 1572872 | tf_op jit(solution)/shard_map/ppermute | solution.py:312

commit v8 on v6

--- a/solution.py
+++ b/solution.py
@@ -90,14 +90,22 @@
                 out_ref[peer, 2 * side + field * (side < 2), pl.ds(chunk * CHUNK, CHUNK)] = piece
 
 
-def unpack_kernel(in_ref, pot_ref, vel_ref, rows, sems):
+def unpack_kernel(in_ref, diff_ref, pot_ref, vel_ref, rows, sems):
     leave = []
     for chunk in range(PER // CHUNK):
+        modes = pl.ds(chunk * CHUNK, CHUNK)
         for field, ref in enumerate((pot_ref, vel_ref)):
+            flows = {}
+            for left in range(1, PEERS - 1, 2):
+                pair = diff_ref[pl.ds(2 * left + 1, 1), :] + diff_ref[pl.ds(2 * left + 2, 1), :]
+                coef = DT * 0.5 * pair if field == 0 else DT
+                flow = coef * (in_ref[left + 1, 4 + field, modes] - in_ref[left, 4 + field, modes])
+                flows[left], flows[left + 1] = flow, -flow
             for peer, side, plane in planes(2):
-                rows[field, pl.ds(chunk * CHUNK * 32 + plane, CHUNK, stride=32), :] = in_ref[
-                    peer, side, field, pl.ds(chunk * CHUNK, CHUNK)
-                ]
+                value = in_ref[peer, 2 * side + field, modes]
+                if side == 0 and peer in flows:
+                    value = value + flows[peer]
+                rows[field, pl.ds(chunk * CHUNK * 32 + plane, CHUNK, stride=32), :] = value
             leave.append(
                 pltpu.make_async_copy(
                     rows.at[field, chunk_rows(chunk)], ref.at[chunk_rows(chunk)], sems.at[field, chunk]
@@ -230,7 +238,8 @@
         for side in range(2):
             own, other = olds[side][pl.ds(2 * K, 8), :], others[side]
             row = lax.broadcasted_iota(jnp.int32, (8, NR), 0)
-            edge_ref[side] = jnp.where(row < 2, DT * 0.5 * (own + other), other)
+            other = jnp.where(row < 2, DT * 0.5 * (own + other), other)
+            edge_ref[side] = jnp.where(row == 3, 1.0 - pot_rim[pl.ds(K, 8), :], other)
     for side in range(2):
         for field in range(2):
             rows = field_rows(field)
@@ -290,10 +299,12 @@
         for field in range(2):
             for dest in range(PEERS):
                 rows = pl.ds(field * K + dest * PER, PER)
-                flow = flux(
-                    edge_ref, side, field, rims[side][rows, :], olds[side][rows, :], pasts[side][rows, :]
-                )
-                out_ref[dest, side, field] = parts[side][rows, :] + flow
+                old = olds[side][rows, :]
+                flow = flux(edge_ref, side, field, rims[side][rows, :], old, pasts[side][rows, :])
+                if side == 0:
+                    flow = edge_ref[0, pl.ds(3, 1), :] * flow
+                    out_ref[dest, 4 + field] = old
+                out_ref[dest, 2 * side + field] = parts[side][rows, :] + flow
 
 
 def swaps():
@@ -311,14 +322,13 @@
     place = jnp.stack([modes % 2, 2 * modes])
     inner_pairs, outer_pairs, slab_pairs = swaps()
     table = jnp.asarray(tables())
-    block = shape((PEERS, 2, 2, PER, NR), F32)
     wide = shape((PEERS, 5, PER, NR), F32)
     plane = shape((2 * K, NR), F32)
     tiles = shape((2, 2, 8, NR), F32)
     staging = [pltpu.VMEM((2, 32 * PER, NR), F32), pltpu.SemaphoreType.DMA((2, PER // CHUNK))]
 
-    def swap(planes):
-        return [lax.ppermute(planes[0], AXES, outer_pairs), lax.ppermute(planes[1], AXES, inner_pairs)]
+    def swap(planes, pairs=outer_pairs):
+        return [lax.ppermute(planes[0], AXES, pairs), lax.ppermute(planes[1], AXES, inner_pairs)]
 
     flat = [a.reshape(-1, NR) for a in (pot, vel)]
     (sent,) = moved(pack_kernel, [wide], flat, (pltpu.HBM, pltpu.VMEM), staging)
@@ -351,7 +361,7 @@
     parts = call(first_kernel, [plane] * 2, [*start, *shared], flops)
     olds, pasts = start, []
     for step in range(1, STEPS):
-        coming = swap(parts)
+        coming = swap(parts, outer_pairs if step < STEPS - 1 else slab_pairs)
         outs = call(
             functools.partial(next_kernel, step == 1),
             [plane] * 6 + ([shape((2, 8, NR), F32)] if step == 1 else []),
@@ -361,9 +371,9 @@
         parts, olds = outs[:2], outs[2:4]
         edge = outs[6] if step == 1 else edge
         pasts, rims = [*outs[4:6], edge], coming
-    (sent,) = call(last_kernel, [block], [*parts, *olds, *rims, *pasts], 0)
+    (sent,) = call(last_kernel, [shape((PEERS, 6, PER, NR), F32)], [*parts, *olds, *rims, *pasts], 0)
     got = lax.all_to_all(sent, "modes", split_axis=0, concat_axis=0, tiled=True)
-    outs = moved(unpack_kernel, [shape((32 * PER, NR), F32)] * 2, [got], (pltpu.VMEM, pltpu.HBM), staging)
+    outs = moved(unpack_kernel, [shape((32 * PER, NR), F32)] * 2, [got, diffusivity], (pltpu.VMEM, pltpu.HBM), staging)
     return tuple(a.reshape(PER, 32, NR) for a in outs)
 
 

time: 106 us -> 105 us (level)
  starting transfers between devices: 24.8 us -> 14 us
  waiting for transfers between devices: 11.2 us -> 21.6 us
  blocking collectives: 57.4 us -> 55.8 us
    ppermute x3, starting transfers between devices: 12.1 us -> 1.21 us  [swap(): lax.ppermute(planes[1], AXES, inner_pairs)]
    ppermute x3, waiting for transfers between devices: 6.04 us -> 16.5 us  [swap(): lax.ppermute(planes[0], AXES, pairs)]
    all_to_all x2, blocking collectives: 57.4 us -> 55.8 us  [on_device(): got = lax.all_to_all(sent, 'modes', split_axis=0, concat_axis=0, tiled=True)]
  transfers between devices with their start and end apart: 9 -> 9, of which waited for: 3 -> 4; matrix products, arithmetic and copies ran while one was open for 0% -> 0% of each run, Pallas kernels for 8% -> 8%
where the time goes in v8:
time: 105 us; the launch traced here: 104 us
  blocking collectives  55.8 us (53%)
  waiting for transfers between devices  21.6 us (21%)
  starting transfers between devices  14 us (13%)
  Pallas kernels  11.9 us (11%)
    all_to_all x2, blocking collectives, on_device(): got = lax.all_to_all(sent, 'modes', split_axis=0, concat_axis=0, tiled=True)  55.8 us
    ppermute x3, waiting for transfers between devices, swap(): lax.ppermute(planes[0], AXES, pairs)  16.5 us
    ppermute x3, starting transfers between devices, swap(): lax.ppermute(planes[0], AXES, pairs)  9.97 us
    pallas_call x7, Pallas kernels, call(): pl.pallas_call(body, out_shape=out_shapes, in_specs=space, out_specs=[pl....  8.86 us
    ppermute x1, waiting for transfers between devices, on_device(): lax.ppermute(start[0], AXES, slab_pairs)  5.07 us
    pallas_call x2, Pallas kernels, moved(): pl.pallas_call(body, out_shape=out_shapes, in_specs=[pl.BlockSpec(memory_...  3.04 us
  transfers between devices with their start and end apart: 9, of which 4 were waited for; matrix products, arithmetic and copies ran while one was open for 0% of the time, Pallas kernels for 8%

profile of v8, /device:TPU:104, one launch (start us, length us, event | category | flops | bytes accessed | tf_op | source)
XLA Modules:
  0.0 104.3 jit_solution(4868579313620333157)
XLA Ops:
  0.6 0.1 pad_add_fusion.core_ref
  0.7 1.6 %shard_map.95 = f32[16,5,32,128]{3,2,1,0:T(8,128)S(1)} custom-call(f32[1024,128]{1,0:T(8,128)} %bitcast.14, f32[1024,128]{1,0:T(8,128)} %bitcast.15), custom_call_target="tpu_custom_call" | custom-call | bytes 2097152 | tf_op jit(solution)/shard_map/pallas_call | solution.py:124
  2.4 0.0 copy-start.4
  2.4 0.0 copy-start
  2.4 0.0 copy-start.1
  2.4 0.0 copy-start.2
  2.4 0.0 copy-start.3
  2.4 26.5 %all_to_all.10.in_ref = f32[16,5,32,128]{3,2,1,0:T(8,128)S(1)} all-to-all(f32[16,5,32,128]{3,2,1,0:T(8,128)S(1)} %shard_map.95), channel_id=1, replica_groups=mesh['modes'=16,'axial'=16] {'modes'}, dimensions={0} | all-to-all | bytes 2621440 | tf_op jit(solution)/shard_map/all_to_all | solution.py:336
  28.9 0.0 copy-done.4
  28.9 0.0 copy-start.5
  28.9 0.6 shard_map.96
  29.6 0.2 collective-permute-start.2
  29.8 2.0 %collective-permute-start.1 = (f32[1032,128]{1,0:T(8,128)S(1)}, f32[1032,128]{1,0:T(8,128)S(1)}, u32[]{:S(2)}, u32[]{:S(2)}) collective-permute-start(f32[1032,128]{1,0:T(8,128)S(1)} %get-tuple-element.50.outer.refs_2_), channel_id=1, source_target_pairs={{240,1},{1,240},{241,2},{2,241},{242,3},{3,242},{243,4},{4,243},{2... | collective-permute-start | bytes 1585160 | tf_op jit(solution)/shard_map/ppermute | solution.py:347
  31.8 0.7 collective-permute-start
  32.5 0.0 copy-done
  32.5 0.0 copy-done.1
  32.5 0.0 copy-done.2
  32.5 0.0 copy-done.3
  32.5 1.0 shard_map.97
  33.5 0.0 copy-done.5
  33.5 1.6 %shard_map.98 = (f32[1024,128]{1,0:T(8,128)S(1)}, f32[1024,128]{1,0:T(8,128)S(1)}) custom-call(f32[1032,128]{1,0:T(8,128)S(1)} %get-tuple-element.50.outer.refs_2_, f32[1040,128]{1,0:T(8,128)S(1)} %get-tuple-element.51.inner.refs_3_, f32[4,2,512,128]{3,2,1,0:T(8,128)S(1)} %get-tuple-element.56.factor_ref.refs_8_.refs_9_, bf16[3,256,768]{2,1,0:T(8,128)(2,1)S(1)} %copy-done.5, ...), custom_call_target="tpu_custom_call" | custom-call | flops 17179869184 | bytes 5402624 | tf_op jit(solution)/shard_map/pallas_call | solution.py:46
  35.1 5.7 %collective-permute-start.3 = (f32[1024,128]{1,0:T(8,128)S(1)}, f32[1024,128]{1,0:T(8,128)S(1)}, u32[]{:S(2)}, u32[]{:S(2)}) collective-permute-start(f32[1024,128]{1,0:T(8,128)S(1)} %get-tuple-element.59.refs_0_), channel_id=1, source_target_pairs={{16,32},{32,16},{48,64},{64,48},{80,96},{96,80},{112,128},{128,112... | collective-permute-start | bytes 1572872 | tf_op jit(solution)/shard_map/ppermute | solution.py:331
  40.8 0.1 collective-permute-start.4
  40.9 0.0 collective-permute-done.refs_4_
  40.9 5.1 %collective-permute-done.1.refs_5_ = f32[1032,128]{1,0:T(8,128)S(1)} collective-permute-done((f32[1032,128]{1,0:T(8,128)S(1)}, f32[1032,128]{1,0:T(8,128)S(1)}, u32[]{:S(2)}, u32[]{:S(2)}) %collective-permute-start.1) | collective-permute-done | bytes 528416 | tf_op jit(solution)/shard_map/ppermute | solution.py:347
  45.9 0.0 collective-permute-done.2.refs_7_
  45.9 1.8 %shard_map.99 = (f32[1024,128]{1,0:T(8,128)S(1)}, f32[1024,128]{1,0:T(8,128)S(1)}, f32[1024,128]{1,0:T(8,128)S(1)}, f32[1024,128]{1,0:T(8,128)S(1)}, f32[1024,12...) custom-call(f32[1024,128]{1,0:T(8,128)S(1)} %get-tuple-element.59.refs_0_, ...), custom_call_target="tpu_custom_call" | custom-call | flops 17179869184 | bytes 10145792 | tf_op jit(solution)/shard_map/pallas_call | solution.py:46
  47.7 1.9 %collective-permute-start.5 = (f32[1024,128]{1,0:T(8,128)S(1)}, f32[1024,128]{1,0:T(8,128)S(1)}, u32[]{:S(2)}, u32[]{:S(2)}) collective-permute-start(f32[1024,128]{1,0:T(8,128)S(1)} %get-tuple-element.63.refs_0_), channel_id=1, source_target_pairs={{16,32},{32,16},{48,64},{64,48},{80,96},{96,80},{112,128},{128,112... | collective-permute-start | bytes 1572872 | tf_op jit(solution)/shard_map/ppermute | solution.py:331
  49.7 0.1 collective-permute-start.6
  49.8 5.5 %collective-permute-done.3.refs_4_ = f32[1024,128]{1,0:T(8,128)S(1)} collective-permute-done((f32[1024,128]{1,0:T(8,128)S(1)}, f32[1024,128]{1,0:T(8,128)S(1)}, u32[]{:S(2)}, u32[]{:S(2)}) %collective-permute-start.3) | collective-permute-done | bytes 524320 | tf_op jit(solution)/shard_map/ppermute | solution.py:331
  55.3 0.0 collective-permute-done.4.refs_5_
  55.3 1.8 %shard_map.100 = (f32[1024,128]{1,0:T(8,128)S(1)}, f32[1024,128]{1,0:T(8,128)S(1)}, f32[1024,128]{1,0:T(8,128)S(1)}, f32[1024,128]{1,0:T(8,128)S(1)}, f32[1024,128]{1,0:T(8,128)S(1)}, /*index=5*/f32[1024,128]{1,0:T(8,128)S(1)}) custom-call(f32[1024,128]{1,0:T(8,128)S(1)} %get-tuple-element.63.refs_0_, f32[1024,128]{1,0:T(8,128)S(1)} %get-tuple-element.64.refs_1_, ...), custom_call_target="tpu_custom_call" | custom-call | flops 17179869184 | bytes 10641408 | tf_op jit(solution)/shard_map/pallas_call | solution.py:46
  57.1 2.4 %collective-permute-start.7 = (f32[1024,128]{1,0:T(8,128)S(1)}, f32[1024,128]{1,0:T(8,128)S(1)}, u32[]{:S(2)}, u32[]{:S(2)}) collective-permute-start(f32[1024,128]{1,0:T(8,128)S(1)} %get-tuple-element.70.refs_0_), channel_id=1, source_target_pairs={{240,1},{1,240},{241,2},{2,241},{242,3},{3,242},{243,4},{4,243},{2... | collective-permute-start | bytes 1572872 | tf_op jit(solution)/shard_map/ppermute | solution.py:331
  59.5 1.0 collective-permute-start.8
  60.5 4.2 %collective-permute-done.5.refs_4_ = f32[1024,128]{1,0:T(8,128)S(1)} collective-permute-done((f32[1024,128]{1,0:T(8,128)S(1)}, f32[1024,128]{1,0:T(8,128)S(1)}, u32[]{:S(2)}, u32[]{:S(2)}) %collective-permute-start.5) | collective-permute-done | bytes 524320 | tf_op jit(solution)/shard_map/ppermute | solution.py:331
  64.8 0.0 collective-permute-done.6.refs_5_
  64.8 1.9 %shard_map.101 = (f32[1024,128]{1,0:T(8,128)S(1)}, f32[1024,128]{1,0:T(8,128)S(1)}, f32[1024,128]{1,0:T(8,128)S(1)}, f32[1024,128]{1,0:T(8,128)S(1)}, f32[1024,128]{1,0:T(8,128)S(1)}, /*index=5*/f32[1024,128]{1,0:T(8,128)S(1)}) custom-call(f32[1024,128]{1,0:T(8,128)S(1)} %get-tuple-element.70.refs_0_, f32[1024,128]{1,0:T(8,128)S(1)} %get-tuple-element.71.refs_1_, ...), custom_call_target="tpu_custom_call" | custom-call | flops 17179869184 | bytes 10641408 | tf_op jit(solution)/shard_map/pallas_call | solution.py:46
  66.6 6.7 %collective-permute-done.7.refs_4_ = f32[1024,128]{1,0:T(8,128)S(1)} collective-permute-done((f32[1024,128]{1,0:T(8,128)S(1)}, f32[1024,128]{1,0:T(8,128)S(1)}, u32[]{:S(2)}, u32[]{:S(2)}) %collective-permute-start.7) | collective-permute-done | bytes 524320 | tf_op jit(solution)/shard_map/ppermute | solution.py:331
  73.4 0.0 collective-permute-done.8.refs_5_
  73.4 0.2 shard_map.102
  73.6 29.3 %all_to_all.11.in_ref = f32[16,6,32,128]{3,2,1,0:T(8,128)S(1)} all-to-all(f32[16,6,32,128]{3,2,1,0:T(8,128)S(1)} %shard_map.102), channel_id=1, replica_groups=mesh['modes'=16,'axial'=16] {'modes'}, dimensions={0} | all-to-all | bytes 3145728 | tf_op jit(solution)/shard_map/all_to_all | solution.py:375
  102.9 1.4 %shard_map.103 = (f32[1024,128]{1,0:T(8,128)}, f32[1024,128]{1,0:T(8,128)}) custom-call(f32[16,6,32,128]{3,2,1,0:T(8,128)S(1)} %all_to_all.11.in_ref, f32[32,128]{1,0:T(8,128)S(1)} %copy-done.4), custom_call_target="tpu_custom_call" | custom-call | bytes 2097152 | tf_op jit(solution)/shard_map/pallas_call | solution.py:124
Async XLA Ops:
  2.4 26.6 %copy-start.4 = (f32[32,128]{1,0:T(8,128)S(1)}, f32[32,128]{1,0:T(8,128)}, u32[]{:S(2)}) copy-start(f32[32,128]{1,0:T(8,128)} %diff_ref.2) | copy-start | bytes 49156
  2.4 30.1 %copy-start = (f32[512,2,128]{2,1,0:T(2,128)S(1)}, f32[512,2,128]{2,1,0:T(2,128)}, u32[]{:S(2)}) copy-start(f32[512,2,128]{2,1,0:T(2,128)} %param.11) | copy-start | bytes 1572868
  2.4 30.1 %copy-start.1 = (f32[512,2,128]{2,1,0:T(2,128)S(1)}, f32[512,2,128]{2,1,0:T(2,128)}, u32[]{:S(2)}) copy-start(f32[512,2,128]{2,1,0:T(2,128)} %param.12) | copy-start | bytes 1572868
  2.4 30.1 %copy-start.2 = (f32[512,2,128]{2,1,0:T(2,128)S(1)}, f32[512,2,128]{2,1,0:T(2,128)}, u32[]{:S(2)}) copy-start(f32[512,2,128]{2,1,0:T(2,128)} %param.13) | copy-start | bytes 1572868
  2.4 30.1 %copy-start.3 = (f32[512,2,128]{2,1,0:T(2,128)S(1)}, f32[512,2,128]{2,1,0:T(2,128)}, u32[]{:S(2)}) copy-start(f32[512,2,128]{2,1,0:T(2,128)} %param.14) | copy-start | bytes 1572868
  28.9 4.6 %copy-start.5 = (bf16[3,256,768]{2,1,0:T(8,128)(2,1)S(1)}, bf16[3,256,768]{2,1,0:T(8,128)(2,1)}, u32[]{:S(2)}) copy-start(bf16[3,256,768]{2,1,0:T(8,128)(2,1)} %constant.20.clone.table_ref.refs_9_.refs_10_) | copy-start | bytes 3538948
  29.6 16.4 %collective-permute-start.2 = (f32[1040,128]{1,0:T(8,128)S(1)}, f32[1040,128]{1,0:T(8,128)S(1)}, u32[]{:S(2)}, u32[]{:S(2)}) collective-permute-start(f32[1040,128]{1,0:T(8,128)S(1)} %get-tuple-element.51.inner.refs_3_), channel_id=1, source_target_pairs={{0,16},{16,0},{32,48},{48,32},{64,80},{80,64},{96,112},{112,96},{1... | collective-permute-start | bytes 1597448 | tf_op jit(solution)/shard_map/ppermute | solution.py:349
  29.8 16.2 %collective-permute-start.1 = (f32[1032,128]{1,0:T(8,128)S(1)}, f32[1032,128]{1,0:T(8,128)S(1)}, u32[]{:S(2)}, u32[]{:S(2)}) collective-permute-start(f32[1032,128]{1,0:T(8,128)S(1)} %get-tuple-element.50.outer.refs_2_), channel_id=1, source_target_pairs={{240,1},{1,240},{241,2},{2,241},{242,3},{3,242},{243,4},{4,243},{2... | collective-permute-start | bytes 1585160 | tf_op jit(solution)/shard_map/ppermute | solution.py:347
  31.8 9.1 %collective-permute-start = (f32[520,128]{1,0:T(8,128)S(1)}, f32[520,128]{1,0:T(8,128)S(1)}, u32[]{:S(2)}, u32[]{:S(2)}) collective-permute-start(f32[520,128]{1,0:T(8,128)S(1)} %get-tuple-element.61), channel_id=1, source_target_pairs={{16,32},{32,16},{48,64},{64,48},{80,96},{96,80},{112,128},{128,112... | collective-permute-start | bytes 798728 | tf_op jit(solution)/shard_map/ppermute | solution.py:346
  35.1 20.2 %collective-permute-start.3 = (f32[1024,128]{1,0:T(8,128)S(1)}, f32[1024,128]{1,0:T(8,128)S(1)}, u32[]{:S(2)}, u32[]{:S(2)}) collective-permute-start(f32[1024,128]{1,0:T(8,128)S(1)} %get-tuple-element.59.refs_0_), channel_id=1, source_target_pairs={{16,32},{32,16},{48,64},{64,48},{80,96},{96,80},{112,128},{128,112... | collective-permute-start | bytes 1572872 | tf_op jit(solution)/shard_map/ppermute | solution.py:331
  40.8 14.5 %collective-permute-start.4 = (f32[1024,128]{1,0:T(8,128)S(1)}, f32[1024,128]{1,0:T(8,128)S(1)}, u32[]{:S(2)}, u32[]{:S(2)}) collective-permute-start(f32[1024,128]{1,0:T(8,128)S(1)} %get-tuple-element.60.refs_1_), channel_id=1, source_target_pairs={{0,16},{16,0},{32,48},{48,32},{64,80},{80,64},{96,112},{112,96},{1... | collective-permute-start | bytes 1572872 | tf_op jit(solution)/shard_map/ppermute | solution.py:331
  47.7 17.0 %collective-permute-start.5 = (f32[1024,128]{1,0:T(8,128)S(1)}, f32[1024,128]{1,0:T(8,128)S(1)}, u32[]{:S(2)}, u32[]{:S(2)}) collective-permute-start(f32[1024,128]{1,0:T(8,128)S(1)} %get-tuple-element.63.refs_0_), channel_id=1, source_target_pairs={{16,32},{32,16},{48,64},{64,48},{80,96},{96,80},{112,128},{128,112... | collective-permute-start | bytes 1572872 | tf_op jit(solution)/shard_map/ppermute | solution.py:331
  49.7 15.1 %collective-permute-start.6 = (f32[1024,128]{1,0:T(8,128)S(1)}, f32[1024,128]{1,0:T(8,128)S(1)}, u32[]{:S(2)}, u32[]{:S(2)}) collective-permute-start(f32[1024,128]{1,0:T(8,128)S(1)} %get-tuple-element.64.refs_1_), channel_id=1, source_target_pairs={{0,16},{16,0},{32,48},{48,32},{64,80},{80,64},{96,112},{112,96},{1... | collective-permute-start | bytes 1572872 | tf_op jit(solution)/shard_map/ppermute | solution.py:331
  57.1 16.2 %collective-permute-start.7 = (f32[1024,128]{1,0:T(8,128)S(1)}, f32[1024,128]{1,0:T(8,128)S(1)}, u32[]{:S(2)}, u32[]{:S(2)}) collective-permute-start(f32[1024,128]{1,0:T(8,128)S(1)} %get-tuple-element.70.refs_0_), channel_id=1, source_target_pairs={{240,1},{1,240},{241,2},{2,241},{242,3},{3,242},{243,4},{4,243},{2... | collective-permute-start | bytes 1572872 | tf_op jit(solution)/shard_map/ppermute | solution.py:331
  59.5 13.8 %collective-permute-start.8 = (f32[1024,128]{1,0:T(8,128)S(1)}, f32[1024,128]{1,0:T(8,128)S(1)}, u32[]{:S(2)}, u32[]{:S(2)}) collective-permute-start(f32[1024,128]{1,0:T(8,128)S(1)} %get-tuple-element.71.refs_1_), channel_id=1, source_target_pairs={{0,16},{16,0},{32,48},{48,32},{64,80},{80,64},{96,112},{112,96},{1... | collective-permute-start | bytes 1572872 | tf_op jit(solution)/shard_map/ppermute | solution.py:331

commit v9 on v7

--- a/solution.py
+++ b/solution.py
@@ -226,6 +226,9 @@
             fluxes[side][rows, :] = flow
             fulls[side][rows, :] = parts[side][rows, :] + flow
     step_alone(fulls, factor_ref, table_ref, coef_ref, outs)
+    more = outs[0].shape[0] - 2 * K
+    if more > 0:
+        outs[0][pl.ds(2 * K, more), :] = jnp.zeros((more, NR), F32)
 
 
 def step_alone(sides, factor_ref, table_ref, coef_ref, outs):
@@ -308,16 +311,13 @@
     tiles = shape((2, 2, 8, NR), F32)
     staging = [pltpu.VMEM((2, 32 * PER, NR), F32), pltpu.SemaphoreType.DMA((2, PER // CHUNK))]
 
-    def swap(planes, pairs=outer_pairs):
-        return [lax.ppermute(planes[0], AXES, pairs), lax.ppermute(planes[1], AXES, inner_pairs)]
-
     flat = [a.reshape(-1, NR) for a in (pot, vel)]
     (sent,) = moved(pack_kernel, [block], flat, (pltpu.HBM, pltpu.VMEM), staging)
     sent, place = lax.optimization_barrier((sent, place))
     got = lax.all_to_all(sent, "modes", split_axis=0, concat_axis=0, tiled=True)
     got, place, diffusivity, table = lax.optimization_barrier((got, place, diffusivity, table))
     start = call(split_kernel, [opening] * 2, [place, got, diffusivity], 0, smem=1)
-    rims = swap(start)
+    rims = [lax.ppermute(start[0], AXES, outer_pairs), lax.ppermute(start[1], AXES, inner_pairs)]
     start, factors = lax.optimization_barrier((start, factors))
     factor, coef = call(
         factor_kernel,
@@ -327,17 +327,27 @@
         smem=1,
     )
     shared = [factor, table, coef]
-    flops = 8 * 2 * 768 * 256 * 256
+    flops = 1 << 34
     parts = call(first_kernel, [plane] * 2, [*start, *shared], flops)
     olds, pasts = start, []
     for step in range(1, STEPS):
-        coming = swap(parts, outer_pairs if step < STEPS - 1 else slab_pairs)
+        late = step == STEPS - 2
+        pairs = outer_pairs if step < STEPS - 1 else slab_pairs
+        coming = [lax.ppermute(parts[0], AXES, pairs)]
+        inner = parts[1]
+        if not late:
+            coming.append(lax.ppermute(inner, AXES, inner_pairs))
+        if step == STEPS - 1:
+            coming[0], rims = lax.optimization_barrier((coming[0], rims))
         outs = call(
             functools.partial(next_kernel, step == 1),
-            [plane] * 6 + ([shape((2, 8, NR), F32)] if step == 1 else []),
+            [shape((2 * K + 8 * (STEPS - 1 - step), NR), F32)] + [plane] * 5 + ([shape((2, 8, NR), F32)] if step == 1 else []),
             [*parts, *olds, *rims, *pasts, *shared],
             flops,
         )
+        if late:
+            inner, outs = lax.optimization_barrier((inner, outs))
+            coming.append(lax.ppermute(inner, AXES, inner_pairs))
         parts, olds = outs[:2], outs[2:4]
         edge = outs[6] if step == 1 else edge
         pasts, rims = [*outs[4:6], edge], coming

time: 107 us -> 107 us (level)
  the two profiles are of different devices: /device:TPU:104 before, /device:TPU:128 now
where the time goes in v9:
time: 107 us; the launch traced here: 106 us
  blocking collectives  51.2 us (48%)
  waiting for transfers between devices  23.2 us (22%)
  starting transfers between devices  19.2 us (18%)
  Pallas kernels  11.9 us (11%)
    all_to_all x2, blocking collectives, on_device(): got = lax.all_to_all(sent, 'modes', split_axis=0, concat_axis=0, tiled=True)  51.2 us
    ppermute x3, waiting for transfers between devices, on_device(): coming = [lax.ppermute(parts[0], AXES, pairs)]  16.1 us
    ppermute x3, starting transfers between devices, on_device(): coming = [lax.ppermute(parts[0], AXES, pairs)]  14.7 us
    pallas_call x7, Pallas kernels, call(): pl.pallas_call(body, out_shape=out_shapes, in_specs=space, out_specs=[pl....  8.82 us
    ppermute x1, waiting for transfers between devices, on_device(): lax.ppermute(start[0], AXES, outer_pairs)  5.66 us
    pallas_call x2, Pallas kernels, moved(): pl.pallas_call(body, out_shape=out_shapes, in_specs=[pl.BlockSpec(memory_...  3.04 us
  transfers between devices with their start and end apart: 8, of which 4 were waited for; matrix products, arithmetic and copies ran while one was open for 0% of the time, Pallas kernels for 7%

profile of v9, /device:TPU:128, one launch (start us, length us, event | category | flops | bytes accessed | tf_op | source)
XLA Modules:
  0.0 106.4 jit_solution(12359729145591664532)
XLA Ops:
  0.6 1.6 %shard_map.95 = f32[16,2,2,32,128]{4,3,2,1,0:T(8,128)S(1)} custom-call(f32[1024,128]{1,0:T(8,128)} %bitcast.15, f32[1024,128]{1,0:T(8,128)} %bitcast.16), custom_call_target="tpu_custom_call" | custom-call | bytes 2097152 | tf_op jit(solution)/shard_map/pallas_call | solution.py:120
  2.3 0.0 copy-start.4
  2.3 0.1 pad_add_fusion.core_ref
  2.4 0.0 copy-start
  2.4 0.0 copy-start.1
  2.4 0.0 copy-start.2
  2.4 0.0 copy-start.3
  2.4 24.9 %all_to_all.10.in_ref = f32[16,2,2,32,128]{4,3,2,1,0:T(8,128)S(1)} all-to-all(f32[16,2,2,32,128]{4,3,2,1,0:T(8,128)S(1)} %shard_map.95), channel_id=1, replica_groups=mesh['modes'=16,'axial'=16] {'modes'}, dimensions={0} | all-to-all | bytes 2097152 | tf_op jit(solution)/shard_map/all_to_all | solution.py:317
  27.3 0.0 copy-done.4
  27.3 0.0 copy-start.5
  27.3 0.6 shard_map.96
  28.0 1.9 %collective-permute-start = (f32[1032,128]{1,0:T(8,128)S(1)}, f32[1032,128]{1,0:T(8,128)S(1)}, u32[]{:S(2)}, u32[]{:S(2)}) collective-permute-start(f32[1032,128]{1,0:T(8,128)S(1)} %get-tuple-element.58.outer.refs_2_), channel_id=1, source_target_pairs={{16,32},{32,16},{48,64},{64,48},{80,96},{96,80},{112,128},{128,112... | collective-permute-start | bytes 1585160 | tf_op jit(solution)/shard_map/ppermute | solution.py:320
  29.9 0.6 collective-permute-start.1
  30.5 0.0 copy-done
  30.5 0.0 copy-done.1
  30.5 0.0 copy-done.2
  30.5 0.0 copy-done.3
  30.5 1.0 shard_map.97
  31.5 0.0 copy-done.5
  31.5 1.5 %shard_map.98 = (f32[1024,128]{1,0:T(8,128)S(1)}, f32[1024,128]{1,0:T(8,128)S(1)}) custom-call(f32[1032,128]{1,0:T(8,128)S(1)} %get-tuple-element.58.outer.refs_2_, f32[1032,128]{1,0:T(8,128)S(1)} %get-tuple-element.59.inner.refs_3_, f32[4,2,512,128]{3,2,1,0:T(8,128)S(1)} %get-tuple-element.64.factor_ref.refs_6_.refs_9_, bf16[3,256,768]{2,1,0:T(8,128)(2,1)S(1)} %copy-done.5, ...), custom_call_target="tpu_custom_call" | custom-call | flops 17179869184 | bytes 5398528 | tf_op jit(solution)/shard_map/pallas_call | solution.py:46
  33.0 8.6 %collective-permute-start.2 = (f32[1024,128]{1,0:T(8,128)S(1)}, f32[1024,128]{1,0:T(8,128)S(1)}, u32[]{:S(2)}, u32[]{:S(2)}) collective-permute-start(f32[1024,128]{1,0:T(8,128)S(1)} %get-tuple-element.67.refs_0_), channel_id=1, source_target_pairs={{16,32},{32,16},{48,64},{64,48},{80,96},{96,80},{112,128},{128,112... | collective-permute-start | bytes 1572872 | tf_op jit(solution)/shard_map/ppermute | solution.py:336
  41.6 0.1 collective-permute-start.3
  41.7 5.7 %collective-permute-done.refs_4_ = f32[1032,128]{1,0:T(8,128)S(1)} collective-permute-done((f32[1032,128]{1,0:T(8,128)S(1)}, f32[1032,128]{1,0:T(8,128)S(1)}, u32[]{:S(2)}, u32[]{:S(2)}) %collective-permute-start) | collective-permute-done | bytes 528416 | tf_op jit(solution)/shard_map/ppermute | solution.py:320
  47.4 0.0 collective-permute-done.1.refs_5_
  47.4 1.8 %shard_map.99 = (f32[1040,128]{1,0:T(8,128)S(1)}, f32[1024,128]{1,0:T(8,128)S(1)}, f32[1024,128]{1,0:T(8,128)S(1)}, f32[1024,128]{1,0:T(8,128)S(1)}, f32[1024,12...) custom-call(f32[1024,128]{1,0:T(8,128)S(1)} %get-tuple-element.67.refs_0_, ...), custom_call_target="tpu_custom_call" | custom-call | flops 17179869184 | bytes 9617408 | tf_op jit(solution)/shard_map/pallas_call | solution.py:46
  49.2 1.9 %collective-permute-start.5 = (f32[1040,128]{1,0:T(8,128)S(1)}, f32[1040,128]{1,0:T(8,128)S(1)}, u32[]{:S(2)}, u32[]{:S(2)}) collective-permute-start(f32[1040,128]{1,0:T(8,128)S(1)} %get-tuple-element.70.refs_0_), channel_id=1, source_target_pairs={{16,32},{32,16},{48,64},{64,48},{80,96},{96,80},{112,128},{128,112... | collective-permute-start | bytes 1597448 | tf_op jit(solution)/shard_map/ppermute | solution.py:336
  51.1 4.9 %collective-permute-done.2.refs_4_ = f32[1024,128]{1,0:T(8,128)S(1)} collective-permute-done((f32[1024,128]{1,0:T(8,128)S(1)}, f32[1024,128]{1,0:T(8,128)S(1)}, u32[]{:S(2)}, u32[]{:S(2)}) %collective-permute-start.2) | collective-permute-done | bytes 524320 | tf_op jit(solution)/shard_map/ppermute | solution.py:336
  56.1 0.0 collective-permute-done.3.refs_5_
  56.1 1.8 %shard_map.100 = (f32[1032,128]{1,0:T(8,128)S(1)}, f32[1024,128]{1,0:T(8,128)S(1)}, f32[1024,128]{1,0:T(8,128)S(1)}, f32[1024,128]{1,0:T(8,128)S(1)}, f32[1024,128]{1,0:T(8,128)S(1)}, /*index=5*/f32[1024,128]{1,0:T(8,128)S(1)}) custom-call(f32[1040,128]{1,0:T(8,128)S(1)} %get-tuple-element.70.refs_0_, f32[1024,128]{1,0:T(8,128)S(1)} %get-tuple-element.86.refs_1_, ...), custom_call_target="tpu_custom_call" | custom-call | flops 17179869184 | bytes 10653696 | tf_op jit(solution)/shard_map/pallas_call | solution.py:46
  57.9 4.2 %collective-permute-start.4 = (f32[1032,128]{1,0:T(8,128)S(1)}, f32[1032,128]{1,0:T(8,128)S(1)}, u32[]{:S(2)}, u32[]{:S(2)}) collective-permute-start(f32[1032,128]{1,0:T(8,128)S(1)} %get-tuple-element.82.refs_0_), channel_id=1, source_target_pairs={{240,1},{1,240},{241,2},{2,241},{242,3},{3,242},{243,4},{4,243},{2... | collective-permute-start | bytes 1585160 | tf_op jit(solution)/shard_map/ppermute | solution.py:336
  62.0 1.8 %collective-permute-start.6 = (f32[1024,128]{1,0:T(8,128)S(1)}, f32[1024,128]{1,0:T(8,128)S(1)}, u32[]{:S(2)}, u32[]{:S(2)}) collective-permute-start(f32[1024,128]{1,0:T(8,128)S(1)} %get-tuple-element.86.refs_1_), channel_id=1, source_target_pairs={{0,16},{16,0},{32,48},{48,32},{64,80},{80,64},{96,112},{112,96},{1... | collective-permute-start | bytes 1572872 | tf_op jit(solution)/shard_map/ppermute | solution.py:350
  63.8 0.1 collective-permute-start.7
  63.9 1.4 %collective-permute-done.6.refs_5_ = f32[1024,128]{1,0:T(8,128)S(1)} collective-permute-done((f32[1024,128]{1,0:T(8,128)S(1)}, f32[1024,128]{1,0:T(8,128)S(1)}, u32[]{:S(2)}, u32[]{:S(2)}) %collective-permute-start.6) | collective-permute-done | bytes 524320 | tf_op jit(solution)/shard_map/ppermute | solution.py:350
  65.4 11.2 %collective-permute-done.4.refs_4_ = f32[1032,128]{1,0:T(8,128)S(1)} collective-permute-done((f32[1032,128]{1,0:T(8,128)S(1)}, f32[1032,128]{1,0:T(8,128)S(1)}, u32[]{:S(2)}, u32[]{:S(2)}) %collective-permute-start.4) | collective-permute-done | bytes 528416 | tf_op jit(solution)/shard_map/ppermute | solution.py:336
  76.6 0.0 collective-permute-done.5.refs_4_
  76.6 1.9 %shard_map.101 = (f32[1024,128]{1,0:T(8,128)S(1)}, f32[1024,128]{1,0:T(8,128)S(1)}, f32[1024,128]{1,0:T(8,128)S(1)}, f32[1024,128]{1,0:T(8,128)S(1)}, f32[1024,128]{1,0:T(8,128)S(1)}, /*index=5*/f32[1024,128]{1,0:T(8,128)S(1)}) custom-call(f32[1032,128]{1,0:T(8,128)S(1)} %get-tuple-element.82.refs_0_, f32[1024,128]{1,0:T(8,128)S(1)} %get-tuple-element.83.refs_1_, ...), custom_call_target="tpu_custom_call" | custom-call | flops 17179869184 | bytes 10653696 | tf_op jit(solution)/shard_map/pallas_call | solution.py:46
  78.5 0.0 collective-permute-done.7.refs_5_
  78.5 0.2 shard_map.102
  78.7 26.2 %all_to_all.11.in_ref = f32[16,6,32,128]{3,2,1,0:T(8,128)S(1)} all-to-all(f32[16,6,32,128]{3,2,1,0:T(8,128)S(1)} %shard_map.102), channel_id=1, replica_groups=mesh['modes'=16,'axial'=16] {'modes'}, dimensions={0} | all-to-all | bytes 3145728 | tf_op jit(solution)/shard_map/all_to_all | solution.py:355
  104.9 1.4 %shard_map.103 = (f32[1024,128]{1,0:T(8,128)}, f32[1024,128]{1,0:T(8,128)}) custom-call(f32[16,6,32,128]{3,2,1,0:T(8,128)S(1)} %all_to_all.11.in_ref, f32[32,128]{1,0:T(8,128)S(1)} %copy-done.4), custom_call_target="tpu_custom_call" | custom-call | bytes 2097152 | tf_op jit(solution)/shard_map/pallas_call | solution.py:120
Async XLA Ops:
  2.3 25.1 %copy-start.4 = (f32[32,128]{1,0:T(8,128)S(1)}, f32[32,128]{1,0:T(8,128)}, u32[]{:S(2)}) copy-start(f32[32,128]{1,0:T(8,128)} %diff_ref.2) | copy-start | bytes 49156
  2.4 28.1 %copy-start = (f32[512,2,128]{2,1,0:T(2,128)S(1)}, f32[512,2,128]{2,1,0:T(2,128)}, u32[]{:S(2)}) copy-start(f32[512,2,128]{2,1,0:T(2,128)} %param.11) | copy-start | bytes 1572868
  2.4 28.1 %copy-start.1 = (f32[512,2,128]{2,1,0:T(2,128)S(1)}, f32[512,2,128]{2,1,0:T(2,128)}, u32[]{:S(2)}) copy-start(f32[512,2,128]{2,1,0:T(2,128)} %param.12) | copy-start | bytes 1572868
  2.4 28.1 %copy-start.2 = (f32[512,2,128]{2,1,0:T(2,128)S(1)}, f32[512,2,128]{2,1,0:T(2,128)}, u32[]{:S(2)}) copy-start(f32[512,2,128]{2,1,0:T(2,128)} %param.13) | copy-start | bytes 1572868
  2.4 28.1 %copy-start.3 = (f32[512,2,128]{2,1,0:T(2,128)S(1)}, f32[512,2,128]{2,1,0:T(2,128)}, u32[]{:S(2)}) copy-start(f32[512,2,128]{2,1,0:T(2,128)} %param.14) | copy-start | bytes 1572868
  27.3 4.1 %copy-start.5 = (bf16[3,256,768]{2,1,0:T(8,128)(2,1)S(1)}, bf16[3,256,768]{2,1,0:T(8,128)(2,1)}, u32[]{:S(2)}) copy-start(bf16[3,256,768]{2,1,0:T(8,128)(2,1)} %constant.30.clone.table_ref.refs_7_.refs_10_) | copy-start | bytes 3538948
  28.0 19.4 %collective-permute-start = (f32[1032,128]{1,0:T(8,128)S(1)}, f32[1032,128]{1,0:T(8,128)S(1)}, u32[]{:S(2)}, u32[]{:S(2)}) collective-permute-start(f32[1032,128]{1,0:T(8,128)S(1)} %get-tuple-element.58.outer.refs_2_), channel_id=1, source_target_pairs={{16,32},{32,16},{48,64},{64,48},{80,96},{96,80},{112,128},{128,112... | collective-permute-start | bytes 1585160 | tf_op jit(solution)/shard_map/ppermute | solution.py:320
  29.9 17.5 %collective-permute-start.1 = (f32[1032,128]{1,0:T(8,128)S(1)}, f32[1032,128]{1,0:T(8,128)S(1)}, u32[]{:S(2)}, u32[]{:S(2)}) collective-permute-start(f32[1032,128]{1,0:T(8,128)S(1)} %get-tuple-element.59.inner.refs_3_), channel_id=1, source_target_pairs={{0,16},{16,0},{32,48},{48,32},{64,80},{80,64},{96,112},{112,96},{1... | collective-permute-start | bytes 1585160 | tf_op jit(solution)/shard_map/ppermute | solution.py:320
  33.0 23.1 %collective-permute-start.2 = (f32[1024,128]{1,0:T(8,128)S(1)}, f32[1024,128]{1,0:T(8,128)S(1)}, u32[]{:S(2)}, u32[]{:S(2)}) collective-permute-start(f32[1024,128]{1,0:T(8,128)S(1)} %get-tuple-element.67.refs_0_), channel_id=1, source_target_pairs={{16,32},{32,16},{48,64},{64,48},{80,96},{96,80},{112,128},{128,112... | collective-permute-start | bytes 1572872 | tf_op jit(solution)/shard_map/ppermute | solution.py:336
  41.6 14.4 %collective-permute-start.3 = (f32[1024,128]{1,0:T(8,128)S(1)}, f32[1024,128]{1,0:T(8,128)S(1)}, u32[]{:S(2)}, u32[]{:S(2)}) collective-permute-start(f32[1024,128]{1,0:T(8,128)S(1)} %get-tuple-element.68.refs_1_), channel_id=1, source_target_pairs={{0,16},{16,0},{32,48},{48,32},{64,80},{80,64},{96,112},{112,96},{1... | collective-permute-start | bytes 1572872 | tf_op jit(solution)/shard_map/ppermute | solution.py:339
  49.2 27.4 %collective-permute-start.5 = (f32[1040,128]{1,0:T(8,128)S(1)}, f32[1040,128]{1,0:T(8,128)S(1)}, u32[]{:S(2)}, u32[]{:S(2)}) collective-permute-start(f32[1040,128]{1,0:T(8,128)S(1)} %get-tuple-element.70.refs_0_), channel_id=1, source_target_pairs={{16,32},{32,16},{48,64},{64,48},{80,96},{96,80},{112,128},{128,112... | collective-permute-start | bytes 1597448 | tf_op jit(solution)/shard_map/ppermute | solution.py:336
  57.9 18.7 %collective-permute-start.4 = (f32[1032,128]{1,0:T(8,128)S(1)}, f32[1032,128]{1,0:T(8,128)S(1)}, u32[]{:S(2)}, u32[]{:S(2)}) collective-permute-start(f32[1032,128]{1,0:T(8,128)S(1)} %get-tuple-element.82.refs_0_), channel_id=1, source_target_pairs={{240,1},{1,240},{241,2},{2,241},{242,3},{3,242},{243,4},{4,243},{2... | collective-permute-start | bytes 1585160 | tf_op jit(solution)/shard_map/ppermute | solution.py:336
  62.0 3.3 %collective-permute-start.6 = (f32[1024,128]{1,0:T(8,128)S(1)}, f32[1024,128]{1,0:T(8,128)S(1)}, u32[]{:S(2)}, u32[]{:S(2)}) collective-permute-start(f32[1024,128]{1,0:T(8,128)S(1)} %get-tuple-element.86.refs_1_), channel_id=1, source_target_pairs={{0,16},{16,0},{32,48},{48,32},{64,80},{80,64},{96,112},{112,96},{1... | collective-permute-start | bytes 1572872 | tf_op jit(solution)/shard_map/ppermute | solution.py:350
  63.8 14.6 %collective-permute-start.7 = (f32[1024,128]{1,0:T(8,128)S(1)}, f32[1024,128]{1,0:T(8,128)S(1)}, u32[]{:S(2)}, u32[]{:S(2)}) collective-permute-start(f32[1024,128]{1,0:T(8,128)S(1)} %get-tuple-element.83.refs_1_), channel_id=1, source_target_pairs={{0,16},{16,0},{32,48},{48,32},{64,80},{80,64},{96,112},{112,96},{1... | collective-permute-start | bytes 1572872 | tf_op jit(solution)/shard_map/ppermute | solution.py:339

commit v10 on v8

--- a/solution.py
+++ b/solution.py
@@ -90,16 +90,14 @@
                 out_ref[peer, 2 * side + field * (side < 2), pl.ds(chunk * CHUNK, CHUNK)] = piece
 
 
-def unpack_kernel(in_ref, diff_ref, pot_ref, vel_ref, rows, sems):
+def unpack_kernel(in_ref, pot_ref, vel_ref, rows, sems):
     leave = []
     for chunk in range(PER // CHUNK):
         modes = pl.ds(chunk * CHUNK, CHUNK)
         for field, ref in enumerate((pot_ref, vel_ref)):
             flows = {}
-            for left in range(1, PEERS - 1, 2):
-                pair = diff_ref[pl.ds(2 * left + 1, 1), :] + diff_ref[pl.ds(2 * left + 2, 1), :]
-                coef = DT * 0.5 * pair if field == 0 else DT
-                flow = coef * (in_ref[left + 1, 4 + field, modes] - in_ref[left, 4 + field, modes])
+            for left in range(1, PEERS - 1, 2) if field == 1 else ():
+                flow = DT * (in_ref[left + 1, 4, modes] - in_ref[left, 4, modes])
                 flows[left], flows[left + 1] = flow, -flow
             for peer, side, plane in planes(2):
                 value = in_ref[peer, 2 * side + field, modes]
@@ -294,16 +292,18 @@
 
 def last_kernel(*refs):
     parts, olds, rims, pasts = (refs[i : i + 2] for i in range(0, 8, 2))
-    edge_ref, out_ref = refs[8:]
+    edge_ref, pot_rim, out_ref = refs[8:]
     for side in range(2):
         for field in range(2):
             for dest in range(PEERS):
                 rows = pl.ds(field * K + dest * PER, PER)
-                old = olds[side][rows, :]
-                flow = flux(edge_ref, side, field, rims[side][rows, :], old, pasts[side][rows, :])
-                if side == 0:
+                old, rim = olds[side][rows, :], rims[side][rows, :]
+                if side == 0 and field == 0:
+                    rim = rim + pot_rim[rows, :]
+                flow = flux(edge_ref, side, field, rim, old, pasts[side][rows, :])
+                if side == 0 and field == 1:
                     flow = edge_ref[0, pl.ds(3, 1), :] * flow
-                    out_ref[dest, 4 + field] = old
+                    out_ref[dest, 4] = old
                 out_ref[dest, 2 * side + field] = parts[side][rows, :] + flow
 
 
@@ -342,8 +342,9 @@
         0,
         smem=1,
     )
+    near_pairs = [pair for pair in outer_pairs if pair not in slab_pairs]
     rims = [
-        lax.ppermute(pot_rim, AXES, [pair for pair in outer_pairs if pair not in slab_pairs]),
+        lax.ppermute(pot_rim, AXES, near_pairs),
         lax.ppermute(start[0], AXES, slab_pairs),
         beyond,
         lax.ppermute(start[1], AXES, inner_pairs),
@@ -362,6 +363,8 @@
     olds, pasts = start, []
     for step in range(1, STEPS):
         coming = swap(parts, outer_pairs if step < STEPS - 1 else slab_pairs)
+        if step == STEPS - 1:
+            pot_rim = lax.ppermute(parts[0][:K], AXES, near_pairs)
         outs = call(
             functools.partial(next_kernel, step == 1),
             [plane] * 6 + ([shape((2, 8, NR), F32)] if step == 1 else []),
@@ -371,9 +374,9 @@
         parts, olds = outs[:2], outs[2:4]
         edge = outs[6] if step == 1 else edge
         pasts, rims = [*outs[4:6], edge], coming
-    (sent,) = call(last_kernel, [shape((PEERS, 6, PER, NR), F32)], [*parts, *olds, *rims, *pasts], 0)
+    (sent,) = call(last_kernel, [wide], [*parts, *olds, *rims, *pasts, pot_rim], 0)
     got = lax.all_to_all(sent, "modes", split_axis=0, concat_axis=0, tiled=True)
-    outs = moved(unpack_kernel, [shape((32 * PER, NR), F32)] * 2, [got, diffusivity], (pltpu.VMEM, pltpu.HBM), staging)
+    outs = moved(unpack_kernel, [shape((32 * PER, NR), F32)] * 2, [got], (pltpu.VMEM, pltpu.HBM), staging)
     return tuple(a.reshape(PER, 32, NR) for a in outs)
 
 

time: 105 us -> 107 us (1.019)
  transfers between devices with their start and end apart: 9 -> 10, of which waited for: 4 -> 4; matrix products, arithmetic and copies ran while one was open for 0% -> 0% of each run, Pallas kernels for 8% -> 8%
where the time goes in v10:
time: 107 us; the launch traced here: 106 us
  blocking collectives  56.6 us (53%)
  waiting for transfers between devices  21.9 us (20%)
  starting transfers between devices  14.7 us (14%)
  Pallas kernels  11.8 us (11%)
    all_to_all x2, blocking collectives, on_device(): got = lax.all_to_all(sent, 'modes', split_axis=0, concat_axis=0, tiled=True)  56.6 us
    ppermute x3, waiting for transfers between devices, swap(): lax.ppermute(planes[0], AXES, pairs)  16.7 us
    ppermute x3, starting transfers between devices, swap(): lax.ppermute(planes[0], AXES, pairs)  9.69 us
    pallas_call x7, Pallas kernels, call(): pl.pallas_call(body, out_shape=out_shapes, in_specs=space, out_specs=[pl....  8.86 us
    ppermute x1, waiting for transfers between devices, on_device(): lax.ppermute(start[0], AXES, slab_pairs)  5.16 us
    pallas_call x2, Pallas kernels, moved(): pl.pallas_call(body, out_shape=out_shapes, in_specs=[pl.BlockSpec(memory_...  2.99 us
  transfers between devices with their start and end apart: 10, of which 4 were waited for; matrix products, arithmetic and copies ran while one was open for 0% of the time, Pallas kernels for 8%

profile of v10, /device:TPU:104, one launch (start us, length us, event | category | flops | bytes accessed | tf_op | source)
XLA Modules:
  0.0 106.1 jit_solution(758494969344982560)
XLA Ops:
  0.6 0.1 pad_add_fusion.core_ref
  0.7 1.6 %shard_map.95 = f32[16,5,32,128]{3,2,1,0:T(8,128)S(1)} custom-call(f32[1024,128]{1,0:T(8,128)} %bitcast.14, f32[1024,128]{1,0:T(8,128)} %bitcast.15), custom_call_target="tpu_custom_call" | custom-call | bytes 2097152 | tf_op jit(solution)/shard_map/pallas_call | solution.py:122
  2.4 0.0 copy-start.4
  2.4 0.0 copy-start.2
  2.4 0.0 copy-start.3
  2.4 26.5 %all_to_all.10.in_ref = f32[16,5,32,128]{3,2,1,0:T(8,128)S(1)} all-to-all(f32[16,5,32,128]{3,2,1,0:T(8,128)S(1)} %shard_map.95), channel_id=1, replica_groups=mesh['modes'=16,'axial'=16] {'modes'}, dimensions={0} | all-to-all | bytes 2621440 | tf_op jit(solution)/shard_map/all_to_all | solution.py:336
  28.9 0.0 copy-done.4
  28.9 0.0 copy-start
  28.9 0.0 copy-start.1
  28.9 0.6 shard_map.96
  29.6 0.0 copy-start.5
  29.6 0.2 collective-permute-start.2
  29.8 2.1 %collective-permute-start.1 = (f32[1032,128]{1,0:T(8,128)S(1)}, f32[1032,128]{1,0:T(8,128)S(1)}, u32[]{:S(2)}, u32[]{:S(2)}) collective-permute-start(f32[1032,128]{1,0:T(8,128)S(1)} %get-tuple-element.50.outer.refs_2_), channel_id=1, source_target_pairs={{240,1},{1,240},{241,2},{2,241},{242,3},{3,242},{243,4},{4,243},{2... | collective-permute-start | bytes 1585160 | tf_op jit(solution)/shard_map/ppermute | solution.py:348
  31.9 0.7 collective-permute-start
  32.6 0.0 copy-done.2
  32.6 0.0 copy-done.3
  32.6 0.0 copy-done
  32.6 0.0 copy-done.1
  32.6 1.0 shard_map.97
  33.6 0.0 copy-done.5
  33.6 1.6 %shard_map.98 = (f32[1024,128]{1,0:T(8,128)S(1)}, f32[1024,128]{1,0:T(8,128)S(1)}) custom-call(f32[1032,128]{1,0:T(8,128)S(1)} %get-tuple-element.50.outer.refs_2_, f32[1040,128]{1,0:T(8,128)S(1)} %get-tuple-element.51.inner.refs_3_, f32[4,2,512,128]{3,2,1,0:T(8,128)S(1)} %get-tuple-element.56.factor_ref.refs_8_.refs_9_, bf16[3,256,768]{2,1,0:T(8,128)(2,1)S(1)} %copy-done.5, ...), custom_call_target="tpu_custom_call" | custom-call | flops 17179869184 | bytes 5402624 | tf_op jit(solution)/shard_map/pallas_call | solution.py:46
  35.2 5.7 %collective-permute-start.3 = (f32[1024,128]{1,0:T(8,128)S(1)}, f32[1024,128]{1,0:T(8,128)S(1)}, u32[]{:S(2)}, u32[]{:S(2)}) collective-permute-start(f32[1024,128]{1,0:T(8,128)S(1)} %get-tuple-element.59.refs_0_), channel_id=1, source_target_pairs={{16,32},{32,16},{48,64},{64,48},{80,96},{96,80},{112,128},{128,112... | collective-permute-start | bytes 1572872 | tf_op jit(solution)/shard_map/ppermute | solution.py:331
  40.9 0.1 collective-permute-start.4
  41.0 0.0 collective-permute-done.refs_4_
  41.0 5.2 %collective-permute-done.1.refs_5_ = f32[1032,128]{1,0:T(8,128)S(1)} collective-permute-done((f32[1032,128]{1,0:T(8,128)S(1)}, f32[1032,128]{1,0:T(8,128)S(1)}, u32[]{:S(2)}, u32[]{:S(2)}) %collective-permute-start.1) | collective-permute-done | bytes 528416 | tf_op jit(solution)/shard_map/ppermute | solution.py:348
  46.2 0.0 collective-permute-done.2.refs_7_
  46.2 1.8 %shard_map.99 = (f32[1024,128]{1,0:T(8,128)S(1)}, f32[1024,128]{1,0:T(8,128)S(1)}, f32[1024,128]{1,0:T(8,128)S(1)}, f32[1024,128]{1,0:T(8,128)S(1)}, f32[1024,12...) custom-call(f32[1024,128]{1,0:T(8,128)S(1)} %get-tuple-element.59.refs_0_, ...), custom_call_target="tpu_custom_call" | custom-call | flops 17179869184 | bytes 10145792 | tf_op jit(solution)/shard_map/pallas_call | solution.py:46
  47.9 1.9 %collective-permute-start.5 = (f32[1024,128]{1,0:T(8,128)S(1)}, f32[1024,128]{1,0:T(8,128)S(1)}, u32[]{:S(2)}, u32[]{:S(2)}) collective-permute-start(f32[1024,128]{1,0:T(8,128)S(1)} %get-tuple-element.63.refs_0_), channel_id=1, source_target_pairs={{16,32},{32,16},{48,64},{64,48},{80,96},{96,80},{112,128},{128,112... | collective-permute-start | bytes 1572872 | tf_op jit(solution)/shard_map/ppermute | solution.py:331
  49.9 0.1 collective-permute-start.6
  50.0 5.5 %collective-permute-done.3.refs_4_ = f32[1024,128]{1,0:T(8,128)S(1)} collective-permute-done((f32[1024,128]{1,0:T(8,128)S(1)}, f32[1024,128]{1,0:T(8,128)S(1)}, u32[]{:S(2)}, u32[]{:S(2)}) %collective-permute-start.3) | collective-permute-done | bytes 524320 | tf_op jit(solution)/shard_map/ppermute | solution.py:331
  55.5 0.0 collective-permute-done.4.refs_5_
  55.5 1.8 %shard_map.100 = (f32[1024,128]{1,0:T(8,128)S(1)}, f32[1024,128]{1,0:T(8,128)S(1)}, f32[1024,128]{1,0:T(8,128)S(1)}, f32[1024,128]{1,0:T(8,128)S(1)}, f32[1024,128]{1,0:T(8,128)S(1)}, /*index=5*/f32[1024,128]{1,0:T(8,128)S(1)}) custom-call(f32[1024,128]{1,0:T(8,128)S(1)} %get-tuple-element.63.refs_0_, f32[1024,128]{1,0:T(8,128)S(1)} %get-tuple-element.64.refs_1_, ...), custom_call_target="tpu_custom_call" | custom-call | flops 17179869184 | bytes 10641408 | tf_op jit(solution)/shard_map/pallas_call | solution.py:46
  57.3 2.1 %collective-permute-start.7 = (f32[1024,128]{1,0:T(8,128)S(1)}, f32[1024,128]{1,0:T(8,128)S(1)}, u32[]{:S(2)}, u32[]{:S(2)}) collective-permute-start(f32[1024,128]{1,0:T(8,128)S(1)} %get-tuple-element.70.refs_0_), channel_id=1, source_target_pairs={{240,1},{1,240},{241,2},{2,241},{242,3},{3,242},{243,4},{4,243},{2... | collective-permute-start | bytes 1572872 | tf_op jit(solution)/shard_map/ppermute | solution.py:331
  59.4 1.2 %collective-permute-start.8 = (f32[1024,128]{1,0:T(8,128)S(1)}, f32[1024,128]{1,0:T(8,128)S(1)}, u32[]{:S(2)}, u32[]{:S(2)}) collective-permute-start(f32[1024,128]{1,0:T(8,128)S(1)} %get-tuple-element.71.refs_1_), channel_id=1, source_target_pairs={{0,16},{16,0},{32,48},{48,32},{64,80},{80,64},{96,112},{112,96},{1... | collective-permute-start | bytes 1572872 | tf_op jit(solution)/shard_map/ppermute | solution.py:331
  60.6 0.7 collective-permute-start.9
  61.3 3.6 %collective-permute-done.5.refs_4_ = f32[1024,128]{1,0:T(8,128)S(1)} collective-permute-done((f32[1024,128]{1,0:T(8,128)S(1)}, f32[1024,128]{1,0:T(8,128)S(1)}, u32[]{:S(2)}, u32[]{:S(2)}) %collective-permute-start.5) | collective-permute-done | bytes 524320 | tf_op jit(solution)/shard_map/ppermute | solution.py:331
  65.0 0.0 collective-permute-done.6.refs_5_
  65.0 1.9 %shard_map.101 = (f32[1024,128]{1,0:T(8,128)S(1)}, f32[1024,128]{1,0:T(8,128)S(1)}, f32[1024,128]{1,0:T(8,128)S(1)}, f32[1024,128]{1,0:T(8,128)S(1)}, f32[1024,128]{1,0:T(8,128)S(1)}, /*index=5*/f32[1024,128]{1,0:T(8,128)S(1)}) custom-call(f32[1024,128]{1,0:T(8,128)S(1)} %get-tuple-element.70.refs_0_, f32[1024,128]{1,0:T(8,128)S(1)} %get-tuple-element.71.refs_1_, ...), custom_call_target="tpu_custom_call" | custom-call | flops 17179869184 | bytes 10641408 | tf_op jit(solution)/shard_map/pallas_call | solution.py:46
  66.8 0.0 collective-permute-done.9.refs_9_
  66.8 7.6 %collective-permute-done.7.refs_4_ = f32[1024,128]{1,0:T(8,128)S(1)} collective-permute-done((f32[1024,128]{1,0:T(8,128)S(1)}, f32[1024,128]{1,0:T(8,128)S(1)}, u32[]{:S(2)}, u32[]{:S(2)}) %collective-permute-start.7) | collective-permute-done | bytes 524320 | tf_op jit(solution)/shard_map/ppermute | solution.py:331
  74.4 0.0 collective-permute-done.8.refs_5_
  74.4 0.2 shard_map.102
  74.6 30.1 %all_to_all.11.in_ref = f32[16,5,32,128]{3,2,1,0:T(8,128)S(1)} all-to-all(f32[16,5,32,128]{3,2,1,0:T(8,128)S(1)} %shard_map.102), channel_id=1, replica_groups=mesh['modes'=16,'axial'=16] {'modes'}, dimensions={0} | all-to-all | bytes 2621440 | tf_op jit(solution)/shard_map/all_to_all | solution.py:378
  104.7 1.4 %shard_map.103 = (f32[1024,128]{1,0:T(8,128)}, f32[1024,128]{1,0:T(8,128)}) custom-call(f32[16,5,32,128]{3,2,1,0:T(8,128)S(1)} %all_to_all.11.in_ref), custom_call_target="tpu_custom_call" | custom-call | bytes 2097152 | tf_op jit(solution)/shard_map/pallas_call | solution.py:122
  (1 shorter events, 0.0 us)
Async XLA Ops:
  2.4 26.5 %copy-start.4 = (f32[32,128]{1,0:T(8,128)S(1)}, f32[32,128]{1,0:T(8,128)}, u32[]{:S(2)}) copy-start(f32[32,128]{1,0:T(8,128)} %diff_ref.1) | copy-start | bytes 49156
  2.4 30.2 %copy-start.2 = (f32[512,2,128]{2,1,0:T(2,128)S(1)}, f32[512,2,128]{2,1,0:T(2,128)}, u32[]{:S(2)}) copy-start(f32[512,2,128]{2,1,0:T(2,128)} %param.13) | copy-start | bytes 1572868
  2.4 30.2 %copy-start.3 = (f32[512,2,128]{2,1,0:T(2,128)S(1)}, f32[512,2,128]{2,1,0:T(2,128)}, u32[]{:S(2)}) copy-start(f32[512,2,128]{2,1,0:T(2,128)} %param.14) | copy-start | bytes 1572868
  28.9 3.7 %copy-start = (f32[512,2,128]{2,1,0:T(2,128)S(1)}, f32[512,2,128]{2,1,0:T(2,128)}, u32[]{:S(2)}) copy-start(f32[512,2,128]{2,1,0:T(2,128)} %param.11) | copy-start | bytes 1572868
  28.9 3.7 %copy-start.1 = (f32[512,2,128]{2,1,0:T(2,128)S(1)}, f32[512,2,128]{2,1,0:T(2,128)}, u32[]{:S(2)}) copy-start(f32[512,2,128]{2,1,0:T(2,128)} %param.12) | copy-start | bytes 1572868
  29.6 4.0 %copy-start.5 = (bf16[3,256,768]{2,1,0:T(8,128)(2,1)S(1)}, bf16[3,256,768]{2,1,0:T(8,128)(2,1)}, u32[]{:S(2)}) copy-start(bf16[3,256,768]{2,1,0:T(8,128)(2,1)} %constant.20.clone.table_ref.refs_9_.refs_10_) | copy-start | bytes 3538948
  29.6 16.6 %collective-permute-start.2 = (f32[1040,128]{1,0:T(8,128)S(1)}, f32[1040,128]{1,0:T(8,128)S(1)}, u32[]{:S(2)}, u32[]{:S(2)}) collective-permute-start(f32[1040,128]{1,0:T(8,128)S(1)} %get-tuple-element.51.inner.refs_3_), channel_id=1, source_target_pairs={{0,16},{16,0},{32,48},{48,32},{64,80},{80,64},{96,112},{112,96},{1... | collective-permute-start | bytes 1597448 | tf_op jit(solution)/shard_map/ppermute | solution.py:350
  29.8 16.4 %collective-permute-start.1 = (f32[1032,128]{1,0:T(8,128)S(1)}, f32[1032,128]{1,0:T(8,128)S(1)}, u32[]{:S(2)}, u32[]{:S(2)}) collective-permute-start(f32[1032,128]{1,0:T(8,128)S(1)} %get-tuple-element.50.outer.refs_2_), channel_id=1, source_target_pairs={{240,1},{1,240},{241,2},{2,241},{242,3},{3,242},{243,4},{4,243},{2... | collective-permute-start | bytes 1585160 | tf_op jit(solution)/shard_map/ppermute | solution.py:348
  31.9 9.1 %collective-permute-start = (f32[520,128]{1,0:T(8,128)S(1)}, f32[520,128]{1,0:T(8,128)S(1)}, u32[]{:S(2)}, u32[]{:S(2)}) collective-permute-start(f32[520,128]{1,0:T(8,128)S(1)} %get-tuple-element.61), channel_id=1, source_target_pairs={{16,32},{32,16},{48,64},{64,48},{80,96},{96,80},{112,128},{128,112... | collective-permute-start | bytes 798728 | tf_op jit(solution)/shard_map/ppermute | solution.py:347
  35.2 20.3 %collective-permute-start.3 = (f32[1024,128]{1,0:T(8,128)S(1)}, f32[1024,128]{1,0:T(8,128)S(1)}, u32[]{:S(2)}, u32[]{:S(2)}) collective-permute-start(f32[1024,128]{1,0:T(8,128)S(1)} %get-tuple-element.59.refs_0_), channel_id=1, source_target_pairs={{16,32},{32,16},{48,64},{64,48},{80,96},{96,80},{112,128},{128,112... | collective-permute-start | bytes 1572872 | tf_op jit(solution)/shard_map/ppermute | solution.py:331
  40.9 14.6 %collective-permute-start.4 = (f32[1024,128]{1,0:T(8,128)S(1)}, f32[1024,128]{1,0:T(8,128)S(1)}, u32[]{:S(2)}, u32[]{:S(2)}) collective-permute-start(f32[1024,128]{1,0:T(8,128)S(1)} %get-tuple-element.60.refs_1_), channel_id=1, source_target_pairs={{0,16},{16,0},{32,48},{48,32},{64,80},{80,64},{96,112},{112,96},{1... | collective-permute-start | bytes 1572872 | tf_op jit(solution)/shard_map/ppermute | solution.py:331
  47.9 17.0 %collective-permute-start.5 = (f32[1024,128]{1,0:T(8,128)S(1)}, f32[1024,128]{1,0:T(8,128)S(1)}, u32[]{:S(2)}, u32[]{:S(2)}) collective-permute-start(f32[1024,128]{1,0:T(8,128)S(1)} %get-tuple-element.63.refs_0_), channel_id=1, source_target_pairs={{16,32},{32,16},{48,64},{64,48},{80,96},{96,80},{112,128},{128,112... | collective-permute-start | bytes 1572872 | tf_op jit(solution)/shard_map/ppermute | solution.py:331
  49.9 15.1 %collective-permute-start.6 = (f32[1024,128]{1,0:T(8,128)S(1)}, f32[1024,128]{1,0:T(8,128)S(1)}, u32[]{:S(2)}, u32[]{:S(2)}) collective-permute-start(f32[1024,128]{1,0:T(8,128)S(1)} %get-tuple-element.64.refs_1_), channel_id=1, source_target_pairs={{0,16},{16,0},{32,48},{48,32},{64,80},{80,64},{96,112},{112,96},{1... | collective-permute-start | bytes 1572872 | tf_op jit(solution)/shard_map/ppermute | solution.py:331
  57.3 17.1 %collective-permute-start.7 = (f32[1024,128]{1,0:T(8,128)S(1)}, f32[1024,128]{1,0:T(8,128)S(1)}, u32[]{:S(2)}, u32[]{:S(2)}) collective-permute-start(f32[1024,128]{1,0:T(8,128)S(1)} %get-tuple-element.70.refs_0_), channel_id=1, source_target_pairs={{240,1},{1,240},{241,2},{2,241},{242,3},{3,242},{243,4},{4,243},{2... | collective-permute-start | bytes 1572872 | tf_op jit(solution)/shard_map/ppermute | solution.py:331
  59.4 15.0 %collective-permute-start.8 = (f32[1024,128]{1,0:T(8,128)S(1)}, f32[1024,128]{1,0:T(8,128)S(1)}, u32[]{:S(2)}, u32[]{:S(2)}) collective-permute-start(f32[1024,128]{1,0:T(8,128)S(1)} %get-tuple-element.71.refs_1_), channel_id=1, source_target_pairs={{0,16},{16,0},{32,48},{48,32},{64,80},{80,64},{96,112},{112,96},{1... | collective-permute-start | bytes 1572872 | tf_op jit(solution)/shard_map/ppermute | solution.py:331
  60.6 6.2 %collective-permute-start.9 = (f32[512,128]{1,0:T(8,128)S(1)}, f32[512,128]{1,0:T(8,128)S(1)}, u32[]{:S(2)}, u32[]{:S(2)}) collective-permute-start(f32[512,128]{1,0:T(8,128)S(1)} %slice.3), channel_id=1, source_target_pairs={{16,32},{32,16},{48,64},{64,48},{80,96},{96,80},{112,128},{128,112... | collective-permute-start | bytes 786440 | tf_op jit(solution)/shard_map/ppermute | solution.py:367

commit v11 on v8

--- a/solution.py
+++ b/solution.py
@@ -159,14 +159,12 @@
 
 def factor_kernel(core_ref, diff_ref, *refs):
     ins, out_ref, coef_ref = refs[:4], refs[4], refs[5]
-    first = jnp.full((HALF, NR), core_ref[0], jnp.int32) == 0
+    core = core_ref[0]
     for which, ref in enumerate(ins):
         for parity in range(2):
-            lower = ref[pl.ds(2 * parity, HALF, stride=4), :] * DT
-            upper = ref[pl.ds(2 * parity + 1, HALF, stride=4), :] * DT
             rows = pl.ds(parity * HALF, HALF)
-            out_ref[which, 0, rows, :] = jnp.where(first, lower, upper)
-            out_ref[which, 1, rows, :] = jnp.where(first, upper, lower)
+            for side, plane in enumerate((core, 1 - core)):
+                out_ref[which, side, rows, :] = ref[pl.ds(2 * parity + plane, HALF, stride=4), :] * DT
     tile = (8, NR)
     cell = lax.broadcasted_iota(jnp.int32, tile, 1)
     row = lax.broadcasted_iota(jnp.int32, tile, 0)

time: 105 us -> 104 us (level)
  no operation moved by 1% of the time
where the time goes in v11:
time: 104 us
  blocking collectives  55.7 us (54%)
  waiting for transfers between devices  21.7 us (21%)
  starting transfers between devices  14 us (13%)
  Pallas kernels  11.8 us (11%)
    all_to_all x2, blocking collectives, on_device(): got = lax.all_to_all(sent, 'modes', split_axis=0, concat_axis=0, tiled=True)  55.7 us
    ppermute x3, waiting for transfers between devices, swap(): lax.ppermute(planes[0], AXES, pairs)  16.5 us
    ppermute x3, starting transfers between devices, swap(): lax.ppermute(planes[0], AXES, pairs)  9.86 us
    pallas_call x7, Pallas kernels, call(): pl.pallas_call(body, out_shape=out_shapes, in_specs=space, out_specs=[pl....  8.75 us
    ppermute x1, waiting for transfers between devices, on_device(): lax.ppermute(start[0], AXES, slab_pairs)  5.18 us
    pallas_call x2, Pallas kernels, moved(): pl.pallas_call(body, out_shape=out_shapes, in_specs=[pl.BlockSpec(memory_...  3.04 us
  transfers between devices with their start and end apart: 9, of which 4 were waited for; matrix products, arithmetic and copies ran while one was open for 0% of the time, Pallas kernels for 8%

profile of v11, /device:TPU:104, one launch (start us, length us, event | category | flops | bytes accessed | tf_op | source)
XLA Modules:
  0.0 104.2 jit_solution(17037758904426456016)
XLA Ops:
  0.6 0.1 pad_add_fusion.core_ref
  0.7 1.6 %shard_map.95 = f32[16,5,32,128]{3,2,1,0:T(8,128)S(1)} custom-call(f32[1024,128]{1,0:T(8,128)} %bitcast.14, f32[1024,128]{1,0:T(8,128)} %bitcast.15), custom_call_target="tpu_custom_call" | custom-call | bytes 2097152 | tf_op jit(solution)/shard_map/pallas_call | solution.py:124
  2.4 0.0 copy-start.4
  2.4 0.0 copy-start
  2.4 0.0 copy-start.1
  2.4 0.0 copy-start.2
  2.4 0.0 copy-start.3
  2.4 26.5 %all_to_all.10.in_ref = f32[16,5,32,128]{3,2,1,0:T(8,128)S(1)} all-to-all(f32[16,5,32,128]{3,2,1,0:T(8,128)S(1)} %shard_map.95), channel_id=1, replica_groups=mesh['modes'=16,'axial'=16] {'modes'}, dimensions={0} | all-to-all | bytes 2621440 | tf_op jit(solution)/shard_map/all_to_all | solution.py:334
  28.9 0.0 copy-done.4
  28.9 0.0 copy-start.5
  28.9 0.6 shard_map.96
  29.6 0.2 collective-permute-start.2
  29.8 2.0 %collective-permute-start.1 = (f32[1032,128]{1,0:T(8,128)S(1)}, f32[1032,128]{1,0:T(8,128)S(1)}, u32[]{:S(2)}, u32[]{:S(2)}) collective-permute-start(f32[1032,128]{1,0:T(8,128)S(1)} %get-tuple-element.50.outer.refs_2_), channel_id=1, source_target_pairs={{240,1},{1,240},{241,2},{2,241},{242,3},{3,242},{243,4},{4,243},{2... | collective-permute-start | bytes 1585160 | tf_op jit(solution)/shard_map/ppermute | solution.py:345
  31.8 0.7 collective-permute-start
  32.5 0.0 copy-done
  32.5 0.0 copy-done.1
  32.5 0.0 copy-done.2
  32.5 0.0 copy-done.3
  32.5 0.9 shard_map.97
  33.4 0.0 copy-done.5
  33.4 1.6 %shard_map.98 = (f32[1024,128]{1,0:T(8,128)S(1)}, f32[1024,128]{1,0:T(8,128)S(1)}) custom-call(f32[1032,128]{1,0:T(8,128)S(1)} %get-tuple-element.50.outer.refs_2_, f32[1040,128]{1,0:T(8,128)S(1)} %get-tuple-element.51.inner.refs_3_, f32[4,2,512,128]{3,2,1,0:T(8,128)S(1)} %get-tuple-element.56.factor_ref.refs_8_.refs_9_, bf16[3,256,768]{2,1,0:T(8,128)(2,1)S(1)} %copy-done.5, ...), custom_call_target="tpu_custom_call" | custom-call | flops 17179869184 | bytes 5402624 | tf_op jit(solution)/shard_map/pallas_call | solution.py:46
  35.0 5.7 %collective-permute-start.3 = (f32[1024,128]{1,0:T(8,128)S(1)}, f32[1024,128]{1,0:T(8,128)S(1)}, u32[]{:S(2)}, u32[]{:S(2)}) collective-permute-start(f32[1024,128]{1,0:T(8,128)S(1)} %get-tuple-element.59.refs_0_), channel_id=1, source_target_pairs={{16,32},{32,16},{48,64},{64,48},{80,96},{96,80},{112,128},{128,112... | collective-permute-start | bytes 1572872 | tf_op jit(solution)/shard_map/ppermute | solution.py:329
  40.6 0.1 collective-permute-start.4
  40.7 0.0 collective-permute-done.refs_4_
  40.8 5.2 %collective-permute-done.1.refs_5_ = f32[1032,128]{1,0:T(8,128)S(1)} collective-permute-done((f32[1032,128]{1,0:T(8,128)S(1)}, f32[1032,128]{1,0:T(8,128)S(1)}, u32[]{:S(2)}, u32[]{:S(2)}) %collective-permute-start.1) | collective-permute-done | bytes 528416 | tf_op jit(solution)/shard_map/ppermute | solution.py:345
  45.9 0.0 collective-permute-done.2.refs_7_
  45.9 1.8 %shard_map.99 = (f32[1024,128]{1,0:T(8,128)S(1)}, f32[1024,128]{1,0:T(8,128)S(1)}, f32[1024,128]{1,0:T(8,128)S(1)}, f32[1024,128]{1,0:T(8,128)S(1)}, f32[1024,12...) custom-call(f32[1024,128]{1,0:T(8,128)S(1)} %get-tuple-element.59.refs_0_, ...), custom_call_target="tpu_custom_call" | custom-call | flops 17179869184 | bytes 10145792 | tf_op jit(solution)/shard_map/pallas_call | solution.py:46
  47.7 1.9 %collective-permute-start.5 = (f32[1024,128]{1,0:T(8,128)S(1)}, f32[1024,128]{1,0:T(8,128)S(1)}, u32[]{:S(2)}, u32[]{:S(2)}) collective-permute-start(f32[1024,128]{1,0:T(8,128)S(1)} %get-tuple-element.63.refs_0_), channel_id=1, source_target_pairs={{16,32},{32,16},{48,64},{64,48},{80,96},{96,80},{112,128},{128,112... | collective-permute-start | bytes 1572872 | tf_op jit(solution)/shard_map/ppermute | solution.py:329
  49.7 0.1 collective-permute-start.6
  49.8 5.5 %collective-permute-done.3.refs_4_ = f32[1024,128]{1,0:T(8,128)S(1)} collective-permute-done((f32[1024,128]{1,0:T(8,128)S(1)}, f32[1024,128]{1,0:T(8,128)S(1)}, u32[]{:S(2)}, u32[]{:S(2)}) %collective-permute-start.3) | collective-permute-done | bytes 524320 | tf_op jit(solution)/shard_map/ppermute | solution.py:329
  55.3 0.0 collective-permute-done.4.refs_5_
  55.3 1.8 %shard_map.100 = (f32[1024,128]{1,0:T(8,128)S(1)}, f32[1024,128]{1,0:T(8,128)S(1)}, f32[1024,128]{1,0:T(8,128)S(1)}, f32[1024,128]{1,0:T(8,128)S(1)}, f32[1024,128]{1,0:T(8,128)S(1)}, /*index=5*/f32[1024,128]{1,0:T(8,128)S(1)}) custom-call(f32[1024,128]{1,0:T(8,128)S(1)} %get-tuple-element.63.refs_0_, f32[1024,128]{1,0:T(8,128)S(1)} %get-tuple-element.64.refs_1_, ...), custom_call_target="tpu_custom_call" | custom-call | flops 17179869184 | bytes 10641408 | tf_op jit(solution)/shard_map/pallas_call | solution.py:46
  57.1 2.3 %collective-permute-start.7 = (f32[1024,128]{1,0:T(8,128)S(1)}, f32[1024,128]{1,0:T(8,128)S(1)}, u32[]{:S(2)}, u32[]{:S(2)}) collective-permute-start(f32[1024,128]{1,0:T(8,128)S(1)} %get-tuple-element.70.refs_0_), channel_id=1, source_target_pairs={{240,1},{1,240},{241,2},{2,241},{242,3},{3,242},{243,4},{4,243},{2... | collective-permute-start | bytes 1572872 | tf_op jit(solution)/shard_map/ppermute | solution.py:329
  59.4 1.1 %collective-permute-start.8 = (f32[1024,128]{1,0:T(8,128)S(1)}, f32[1024,128]{1,0:T(8,128)S(1)}, u32[]{:S(2)}, u32[]{:S(2)}) collective-permute-start(f32[1024,128]{1,0:T(8,128)S(1)} %get-tuple-element.71.refs_1_), channel_id=1, source_target_pairs={{0,16},{16,0},{32,48},{48,32},{64,80},{80,64},{96,112},{112,96},{1... | collective-permute-start | bytes 1572872 | tf_op jit(solution)/shard_map/ppermute | solution.py:329
  60.5 4.2 %collective-permute-done.5.refs_4_ = f32[1024,128]{1,0:T(8,128)S(1)} collective-permute-done((f32[1024,128]{1,0:T(8,128)S(1)}, f32[1024,128]{1,0:T(8,128)S(1)}, u32[]{:S(2)}, u32[]{:S(2)}) %collective-permute-start.5) | collective-permute-done | bytes 524320 | tf_op jit(solution)/shard_map/ppermute | solution.py:329
  64.8 0.0 collective-permute-done.6.refs_5_
  64.8 1.9 %shard_map.101 = (f32[1024,128]{1,0:T(8,128)S(1)}, f32[1024,128]{1,0:T(8,128)S(1)}, f32[1024,128]{1,0:T(8,128)S(1)}, f32[1024,128]{1,0:T(8,128)S(1)}, f32[1024,128]{1,0:T(8,128)S(1)}, /*index=5*/f32[1024,128]{1,0:T(8,128)S(1)}) custom-call(f32[1024,128]{1,0:T(8,128)S(1)} %get-tuple-element.70.refs_0_, f32[1024,128]{1,0:T(8,128)S(1)} %get-tuple-element.71.refs_1_, ...), custom_call_target="tpu_custom_call" | custom-call | flops 17179869184 | bytes 10641408 | tf_op jit(solution)/shard_map/pallas_call | solution.py:46
  66.6 6.7 %collective-permute-done.7.refs_4_ = f32[1024,128]{1,0:T(8,128)S(1)} collective-permute-done((f32[1024,128]{1,0:T(8,128)S(1)}, f32[1024,128]{1,0:T(8,128)S(1)}, u32[]{:S(2)}, u32[]{:S(2)}) %collective-permute-start.7) | collective-permute-done | bytes 524320 | tf_op jit(solution)/shard_map/ppermute | solution.py:329
  73.4 0.0 collective-permute-done.8.refs_5_
  73.4 0.2 shard_map.102
  73.6 29.2 %all_to_all.11.in_ref = f32[16,6,32,128]{3,2,1,0:T(8,128)S(1)} all-to-all(f32[16,6,32,128]{3,2,1,0:T(8,128)S(1)} %shard_map.102), channel_id=1, replica_groups=mesh['modes'=16,'axial'=16] {'modes'}, dimensions={0} | all-to-all | bytes 3145728 | tf_op jit(solution)/shard_map/all_to_all | solution.py:373
  102.8 1.4 %shard_map.103 = (f32[1024,128]{1,0:T(8,128)}, f32[1024,128]{1,0:T(8,128)}) custom-call(f32[16,6,32,128]{3,2,1,0:T(8,128)S(1)} %all_to_all.11.in_ref, f32[32,128]{1,0:T(8,128)S(1)} %copy-done.4), custom_call_target="tpu_custom_call" | custom-call | bytes 2097152 | tf_op jit(solution)/shard_map/pallas_call | solution.py:124
Async XLA Ops:
  2.4 26.6 %copy-start.4 = (f32[32,128]{1,0:T(8,128)S(1)}, f32[32,128]{1,0:T(8,128)}, u32[]{:S(2)}) copy-start(f32[32,128]{1,0:T(8,128)} %diff_ref.2) | copy-start | bytes 49156
  2.4 30.1 %copy-start = (f32[512,2,128]{2,1,0:T(2,128)S(1)}, f32[512,2,128]{2,1,0:T(2,128)}, u32[]{:S(2)}) copy-start(f32[512,2,128]{2,1,0:T(2,128)} %param.11) | copy-start | bytes 1572868
  2.4 30.1 %copy-start.1 = (f32[512,2,128]{2,1,0:T(2,128)S(1)}, f32[512,2,128]{2,1,0:T(2,128)}, u32[]{:S(2)}) copy-start(f32[512,2,128]{2,1,0:T(2,128)} %param.12) | copy-start | bytes 1572868
  2.4 30.1 %copy-start.2 = (f32[512,2,128]{2,1,0:T(2,128)S(1)}, f32[512,2,128]{2,1,0:T(2,128)}, u32[]{:S(2)}) copy-start(f32[512,2,128]{2,1,0:T(2,128)} %param.13) | copy-start | bytes 1572868
  2.4 30.1 %copy-start.3 = (f32[512,2,128]{2,1,0:T(2,128)S(1)}, f32[512,2,128]{2,1,0:T(2,128)}, u32[]{:S(2)}) copy-start(f32[512,2,128]{2,1,0:T(2,128)} %param.14) | copy-start | bytes 1572868
  28.9 4.4 %copy-start.5 = (bf16[3,256,768]{2,1,0:T(8,128)(2,1)S(1)}, bf16[3,256,768]{2,1,0:T(8,128)(2,1)}, u32[]{:S(2)}) copy-start(bf16[3,256,768]{2,1,0:T(8,128)(2,1)} %constant.20.clone.table_ref.refs_9_.refs_10_) | copy-start | bytes 3538948
  29.6 16.4 %collective-permute-start.2 = (f32[1040,128]{1,0:T(8,128)S(1)}, f32[1040,128]{1,0:T(8,128)S(1)}, u32[]{:S(2)}, u32[]{:S(2)}) collective-permute-start(f32[1040,128]{1,0:T(8,128)S(1)} %get-tuple-element.51.inner.refs_3_), channel_id=1, source_target_pairs={{0,16},{16,0},{32,48},{48,32},{64,80},{80,64},{96,112},{112,96},{1... | collective-permute-start | bytes 1597448 | tf_op jit(solution)/shard_map/ppermute | solution.py:347
  29.8 16.2 %collective-permute-start.1 = (f32[1032,128]{1,0:T(8,128)S(1)}, f32[1032,128]{1,0:T(8,128)S(1)}, u32[]{:S(2)}, u32[]{:S(2)}) collective-permute-start(f32[1032,128]{1,0:T(8,128)S(1)} %get-tuple-element.50.outer.refs_2_), channel_id=1, source_target_pairs={{240,1},{1,240},{241,2},{2,241},{242,3},{3,242},{243,4},{4,243},{2... | collective-permute-start | bytes 1585160 | tf_op jit(solution)/shard_map/ppermute | solution.py:345
  31.8 9.0 %collective-permute-start = (f32[520,128]{1,0:T(8,128)S(1)}, f32[520,128]{1,0:T(8,128)S(1)}, u32[]{:S(2)}, u32[]{:S(2)}) collective-permute-start(f32[520,128]{1,0:T(8,128)S(1)} %get-tuple-element.61), channel_id=1, source_target_pairs={{16,32},{32,16},{48,64},{64,48},{80,96},{96,80},{112,128},{128,112... | collective-permute-start | bytes 798728 | tf_op jit(solution)/shard_map/ppermute | solution.py:344
  35.0 20.3 %collective-permute-start.3 = (f32[1024,128]{1,0:T(8,128)S(1)}, f32[1024,128]{1,0:T(8,128)S(1)}, u32[]{:S(2)}, u32[]{:S(2)}) collective-permute-start(f32[1024,128]{1,0:T(8,128)S(1)} %get-tuple-element.59.refs_0_), channel_id=1, source_target_pairs={{16,32},{32,16},{48,64},{64,48},{80,96},{96,80},{112,128},{128,112... | collective-permute-start | bytes 1572872 | tf_op jit(solution)/shard_map/ppermute | solution.py:329
  40.6 14.7 %collective-permute-start.4 = (f32[1024,128]{1,0:T(8,128)S(1)}, f32[1024,128]{1,0:T(8,128)S(1)}, u32[]{:S(2)}, u32[]{:S(2)}) collective-permute-start(f32[1024,128]{1,0:T(8,128)S(1)} %get-tuple-element.60.refs_1_), channel_id=1, source_target_pairs={{0,16},{16,0},{32,48},{48,32},{64,80},{80,64},{96,112},{112,96},{1... | collective-permute-start | bytes 1572872 | tf_op jit(solution)/shard_map/ppermute | solution.py:329
  47.7 17.0 %collective-permute-start.5 = (f32[1024,128]{1,0:T(8,128)S(1)}, f32[1024,128]{1,0:T(8,128)S(1)}, u32[]{:S(2)}, u32[]{:S(2)}) collective-permute-start(f32[1024,128]{1,0:T(8,128)S(1)} %get-tuple-element.63.refs_0_), channel_id=1, source_target_pairs={{16,32},{32,16},{48,64},{64,48},{80,96},{96,80},{112,128},{128,112... | collective-permute-start | bytes 1572872 | tf_op jit(solution)/shard_map/ppermute | solution.py:329
  49.7 15.1 %collective-permute-start.6 = (f32[1024,128]{1,0:T(8,128)S(1)}, f32[1024,128]{1,0:T(8,128)S(1)}, u32[]{:S(2)}, u32[]{:S(2)}) collective-permute-start(f32[1024,128]{1,0:T(8,128)S(1)} %get-tuple-element.64.refs_1_), channel_id=1, source_target_pairs={{0,16},{16,0},{32,48},{48,32},{64,80},{80,64},{96,112},{112,96},{1... | collective-permute-start | bytes 1572872 | tf_op jit(solution)/shard_map/ppermute | solution.py:329
  57.1 16.2 %collective-permute-start.7 = (f32[1024,128]{1,0:T(8,128)S(1)}, f32[1024,128]{1,0:T(8,128)S(1)}, u32[]{:S(2)}, u32[]{:S(2)}) collective-permute-start(f32[1024,128]{1,0:T(8,128)S(1)} %get-tuple-element.70.refs_0_), channel_id=1, source_target_pairs={{240,1},{1,240},{241,2},{2,241},{242,3},{3,242},{243,4},{4,243},{2... | collective-permute-start | bytes 1572872 | tf_op jit(solution)/shard_map/ppermute | solution.py:329
  59.4 14.0 %collective-permute-start.8 = (f32[1024,128]{1,0:T(8,128)S(1)}, f32[1024,128]{1,0:T(8,128)S(1)}, u32[]{:S(2)}, u32[]{:S(2)}) collective-permute-start(f32[1024,128]{1,0:T(8,128)S(1)} %get-tuple-element.71.refs_1_), channel_id=1, source_target_pairs={{0,16},{16,0},{32,48},{48,32},{64,80},{80,64},{96,112},{112,96},{1... | collective-permute-start | bytes 1572872 | tf_op jit(solution)/shard_map/ppermute | solution.py:329

commit v12 on v11

--- a/solution.py
+++ b/solution.py
@@ -140,7 +140,6 @@
         out[pl.ds(2 * K, 8), :] = own
         if side == 0:
             pot_rim[pl.ds(K, 8), :] = own
-        else:
             out[pl.ds(2 * K + 8, 8), :] = own
         for src in range(PEERS):
             for field in range(2):
@@ -335,7 +334,7 @@
     got, place, diffusivity, table = lax.optimization_barrier((got, place, diffusivity, table))
     *start, pot_rim, beyond = call(
         split_kernel,
-        [shape((2 * K + rows, NR), F32) for rows in (8, 16)] + [shape((K + 8, NR), F32), shape((K, NR), F32)],
+        [shape((2 * K + rows, NR), F32) for rows in (16, 8)] + [shape((K + 8, NR), F32), shape((K, NR), F32)],
         [place, got, diffusivity],
         0,
         smem=1,

time: 104 us -> 106 us (1.019)
  waiting for transfers between devices: 21.7 us -> 17 us
  starting transfers between devices: 14 us -> 18.6 us
  blocking collectives: 55.7 us -> 57.9 us
    ppermute x3, starting transfers between devices: 1.32 us -> 3.79 us  [swap(): lax.ppermute(planes[1], AXES, inner_pairs)]
    ppermute x3, waiting for transfers between devices: 16.5 us -> 14.1 us  [swap(): lax.ppermute(planes[0], AXES, pairs)]
    ppermute x1, waiting for transfers between devices: 5.18 us -> 2.86 us  [on_device(): lax.ppermute(start[0], AXES, slab_pairs)]
    all_to_all x2, blocking collectives: 55.7 us -> 57.9 us  [on_device(): got = lax.all_to_all(sent, 'modes', split_axis=0, concat_axis=0, tiled=True)]
    ppermute x3, starting transfers between devices: 9.86 us -> 11.9 us  [swap(): lax.ppermute(planes[0], AXES, pairs)]
  transfers between devices with their start and end apart: 9 -> 9, of which waited for: 4 -> 4; matrix products, arithmetic and copies ran while one was open for 0% -> 0% of each run, Pallas kernels for 8% -> 7%
where the time goes in v12:
time: 106 us
  blocking collectives  57.9 us (55%)
  starting transfers between devices  18.6 us (18%)
  waiting for transfers between devices  17 us (16%)
  Pallas kernels  11.6 us (11%)
    all_to_all x2, blocking collectives, on_device(): got = lax.all_to_all(sent, 'modes', split_axis=0, concat_axis=0, tiled=True)  57.9 us
    ppermute x3, waiting for transfers between devices, swap(): lax.ppermute(planes[0], AXES, pairs)  14.1 us
    ppermute x3, starting transfers between devices, swap(): lax.ppermute(planes[0], AXES, pairs)  11.9 us
    pallas_call x7, Pallas kernels, call(): pl.pallas_call(body, out_shape=out_shapes, in_specs=space, out_specs=[pl....  8.55 us
    ppermute x3, starting transfers between devices, swap(): lax.ppermute(planes[1], AXES, inner_pairs)  3.79 us
    pallas_call x2, Pallas kernels, moved(): pl.pallas_call(body, out_shape=out_shapes, in_specs=[pl.BlockSpec(memory_...  3.04 us
    ppermute x1, waiting for transfers between devices, on_device(): lax.ppermute(start[0], AXES, slab_pairs)  2.86 us
  transfers between devices with their start and end apart: 9, of which 4 were waited for; matrix products, arithmetic and copies ran while one was open for 0% of the time, Pallas kernels for 7%

profile of v12, /device:TPU:104, one launch (start us, length us, event | category | flops | bytes accessed | tf_op | source)
XLA Modules:
  0.0 106.0 jit_solution(9201773418936934131)
XLA Ops:
  0.6 0.1 pad_add_fusion.core_ref
  0.7 1.6 %shard_map.95 = f32[16,5,32,128]{3,2,1,0:T(8,128)S(1)} custom-call(f32[1024,128]{1,0:T(8,128)} %bitcast.14, f32[1024,128]{1,0:T(8,128)} %bitcast.15), custom_call_target="tpu_custom_call" | custom-call | bytes 2097152 | tf_op jit(solution)/shard_map/pallas_call | solution.py:124
  2.4 0.0 copy-start.4
  2.4 0.0 copy-start
  2.4 0.0 copy-start.1
  2.4 0.0 copy-start.2
  2.4 0.0 copy-start.3
  2.4 26.5 %all_to_all.10.in_ref = f32[16,5,32,128]{3,2,1,0:T(8,128)S(1)} all-to-all(f32[16,5,32,128]{3,2,1,0:T(8,128)S(1)} %shard_map.95), channel_id=1, replica_groups=mesh['modes'=16,'axial'=16] {'modes'}, dimensions={0} | all-to-all | bytes 2621440 | tf_op jit(solution)/shard_map/all_to_all | solution.py:333
  28.9 0.0 copy-done.4
  28.9 0.0 copy-start.5
  28.9 0.6 shard_map.96
  29.6 2.1 %collective-permute-start.1 = (f32[1040,128]{1,0:T(8,128)S(1)}, f32[1040,128]{1,0:T(8,128)S(1)}, u32[]{:S(2)}, u32[]{:S(2)}) collective-permute-start(f32[1040,128]{1,0:T(8,128)S(1)} %get-tuple-element.50.outer.refs_2_), channel_id=1, source_target_pairs={{240,1},{1,240},{241,2},{2,241},{242,3},{3,242},{243,4},{4,243},{2... | collective-permute-start | bytes 1597448 | tf_op jit(solution)/shard_map/ppermute | solution.py:344
  31.7 0.1 collective-permute-start.2
  31.8 0.7 collective-permute-start
  32.5 0.0 copy-done
  32.5 0.0 copy-done.1
  32.5 0.0 copy-done.2
  32.5 0.0 copy-done.3
  32.5 0.9 shard_map.97
  33.4 0.0 copy-done.5
  33.4 1.6 %shard_map.98 = (f32[1024,128]{1,0:T(8,128)S(1)}, f32[1024,128]{1,0:T(8,128)S(1)}) custom-call(f32[1040,128]{1,0:T(8,128)S(1)} %get-tuple-element.50.outer.refs_2_, f32[1032,128]{1,0:T(8,128)S(1)} %get-tuple-element.51.inner.refs_3_, f32[4,2,512,128]{3,2,1,0:T(8,128)S(1)} %get-tuple-element.56.factor_ref.refs_8_.refs_9_, bf16[3,256,768]{2,1,0:T(8,128)(2,1)S(1)} %copy-done.5, ...), custom_call_target="tpu_custom_call" | custom-call | flops 17179869184 | bytes 5402624 | tf_op jit(solution)/shard_map/pallas_call | solution.py:46
  34.9 5.6 %collective-permute-start.3 = (f32[1024,128]{1,0:T(8,128)S(1)}, f32[1024,128]{1,0:T(8,128)S(1)}, u32[]{:S(2)}, u32[]{:S(2)}) collective-permute-start(f32[1024,128]{1,0:T(8,128)S(1)} %get-tuple-element.59.refs_0_), channel_id=1, source_target_pairs={{16,32},{32,16},{48,64},{64,48},{80,96},{96,80},{112,128},{128,112... | collective-permute-start | bytes 1572872 | tf_op jit(solution)/shard_map/ppermute | solution.py:328
  40.5 1.4 %collective-permute-start.4 = (f32[1024,128]{1,0:T(8,128)S(1)}, f32[1024,128]{1,0:T(8,128)S(1)}, u32[]{:S(2)}, u32[]{:S(2)}) collective-permute-start(f32[1024,128]{1,0:T(8,128)S(1)} %get-tuple-element.60.refs_1_), channel_id=1, source_target_pairs={{0,16},{16,0},{32,48},{48,32},{64,80},{80,64},{96,112},{112,96},{1... | collective-permute-start | bytes 1572872 | tf_op jit(solution)/shard_map/ppermute | solution.py:328
  41.9 0.0 collective-permute-done.refs_4_
  41.9 0.0 collective-permute-done.2.refs_7_
  41.9 2.9 %collective-permute-done.1.refs_5_ = f32[1040,128]{1,0:T(8,128)S(1)} collective-permute-done((f32[1040,128]{1,0:T(8,128)S(1)}, f32[1040,128]{1,0:T(8,128)S(1)}, u32[]{:S(2)}, u32[]{:S(2)}) %collective-permute-start.1) | collective-permute-done | bytes 532512 | tf_op jit(solution)/shard_map/ppermute | solution.py:344
  44.8 1.8 %shard_map.99 = (f32[1024,128]{1,0:T(8,128)S(1)}, f32[1024,128]{1,0:T(8,128)S(1)}, f32[1024,128]{1,0:T(8,128)S(1)}, f32[1024,128]{1,0:T(8,128)S(1)}, f32[1024,12...) custom-call(f32[1024,128]{1,0:T(8,128)S(1)} %get-tuple-element.59.refs_0_, ...), custom_call_target="tpu_custom_call" | custom-call | flops 17179869184 | bytes 10145792 | tf_op jit(solution)/shard_map/pallas_call | solution.py:46
  46.5 2.7 %collective-permute-start.5 = (f32[1024,128]{1,0:T(8,128)S(1)}, f32[1024,128]{1,0:T(8,128)S(1)}, u32[]{:S(2)}, u32[]{:S(2)}) collective-permute-start(f32[1024,128]{1,0:T(8,128)S(1)} %get-tuple-element.63.refs_0_), channel_id=1, source_target_pairs={{16,32},{32,16},{48,64},{64,48},{80,96},{96,80},{112,128},{128,112... | collective-permute-start | bytes 1572872 | tf_op jit(solution)/shard_map/ppermute | solution.py:328
  49.3 0.1 collective-permute-start.6
  49.4 4.8 %collective-permute-done.3.refs_4_ = f32[1024,128]{1,0:T(8,128)S(1)} collective-permute-done((f32[1024,128]{1,0:T(8,128)S(1)}, f32[1024,128]{1,0:T(8,128)S(1)}, u32[]{:S(2)}, u32[]{:S(2)}) %collective-permute-start.3) | collective-permute-done | bytes 524320 | tf_op jit(solution)/shard_map/ppermute | solution.py:328
  54.1 0.0 collective-permute-done.4.refs_5_
  54.1 1.7 %shard_map.100 = (f32[1024,128]{1,0:T(8,128)S(1)}, f32[1024,128]{1,0:T(8,128)S(1)}, f32[1024,128]{1,0:T(8,128)S(1)}, f32[1024,128]{1,0:T(8,128)S(1)}, f32[1024,128]{1,0:T(8,128)S(1)}, /*index=5*/f32[1024,128]{1,0:T(8,128)S(1)}) custom-call(f32[1024,128]{1,0:T(8,128)S(1)} %get-tuple-element.63.refs_0_, f32[1024,128]{1,0:T(8,128)S(1)} %get-tuple-element.64.refs_1_, ...), custom_call_target="tpu_custom_call" | custom-call | flops 17179869184 | bytes 10641408 | tf_op jit(solution)/shard_map/pallas_call | solution.py:46
  55.9 3.6 %collective-permute-start.7 = (f32[1024,128]{1,0:T(8,128)S(1)}, f32[1024,128]{1,0:T(8,128)S(1)}, u32[]{:S(2)}, u32[]{:S(2)}) collective-permute-start(f32[1024,128]{1,0:T(8,128)S(1)} %get-tuple-element.70.refs_0_), channel_id=1, source_target_pairs={{240,1},{1,240},{241,2},{2,241},{242,3},{3,242},{243,4},{4,243},{2... | collective-permute-start | bytes 1572872 | tf_op jit(solution)/shard_map/ppermute | solution.py:328
  59.5 2.3 %collective-permute-start.8 = (f32[1024,128]{1,0:T(8,128)S(1)}, f32[1024,128]{1,0:T(8,128)S(1)}, u32[]{:S(2)}, u32[]{:S(2)}) collective-permute-start(f32[1024,128]{1,0:T(8,128)S(1)} %get-tuple-element.71.refs_1_), channel_id=1, source_target_pairs={{0,16},{16,0},{32,48},{48,32},{64,80},{80,64},{96,112},{112,96},{1... | collective-permute-start | bytes 1572872 | tf_op jit(solution)/shard_map/ppermute | solution.py:328
  61.8 1.8 %collective-permute-done.5.refs_4_ = f32[1024,128]{1,0:T(8,128)S(1)} collective-permute-done((f32[1024,128]{1,0:T(8,128)S(1)}, f32[1024,128]{1,0:T(8,128)S(1)}, u32[]{:S(2)}, u32[]{:S(2)}) %collective-permute-start.5) | collective-permute-done | bytes 524320 | tf_op jit(solution)/shard_map/ppermute | solution.py:328
  63.6 0.0 collective-permute-done.6.refs_5_
  63.6 1.8 %shard_map.101 = (f32[1024,128]{1,0:T(8,128)S(1)}, f32[1024,128]{1,0:T(8,128)S(1)}, f32[1024,128]{1,0:T(8,128)S(1)}, f32[1024,128]{1,0:T(8,128)S(1)}, f32[1024,128]{1,0:T(8,128)S(1)}, /*index=5*/f32[1024,128]{1,0:T(8,128)S(1)}) custom-call(f32[1024,128]{1,0:T(8,128)S(1)} %get-tuple-element.70.refs_0_, f32[1024,128]{1,0:T(8,128)S(1)} %get-tuple-element.71.refs_1_, ...), custom_call_target="tpu_custom_call" | custom-call | flops 17179869184 | bytes 10641408 | tf_op jit(solution)/shard_map/pallas_call | solution.py:46
  65.4 7.6 %collective-permute-done.7.refs_4_ = f32[1024,128]{1,0:T(8,128)S(1)} collective-permute-done((f32[1024,128]{1,0:T(8,128)S(1)}, f32[1024,128]{1,0:T(8,128)S(1)}, u32[]{:S(2)}, u32[]{:S(2)}) %collective-permute-start.7) | collective-permute-done | bytes 524320 | tf_op jit(solution)/shard_map/ppermute | solution.py:328
  73.0 0.0 collective-permute-done.8.refs_5_
  73.0 0.2 shard_map.102
  73.2 31.4 %all_to_all.11.in_ref = f32[16,6,32,128]{3,2,1,0:T(8,128)S(1)} all-to-all(f32[16,6,32,128]{3,2,1,0:T(8,128)S(1)} %shard_map.102), channel_id=1, replica_groups=mesh['modes'=16,'axial'=16] {'modes'}, dimensions={0} | all-to-all | bytes 3145728 | tf_op jit(solution)/shard_map/all_to_all | solution.py:372
  104.6 1.4 %shard_map.103 = (f32[1024,128]{1,0:T(8,128)}, f32[1024,128]{1,0:T(8,128)}) custom-call(f32[16,6,32,128]{3,2,1,0:T(8,128)S(1)} %all_to_all.11.in_ref, f32[32,128]{1,0:T(8,128)S(1)} %copy-done.4), custom_call_target="tpu_custom_call" | custom-call | bytes 2097152 | tf_op jit(solution)/shard_map/pallas_call | solution.py:124
Async XLA Ops:
  2.4 26.6 %copy-start.4 = (f32[32,128]{1,0:T(8,128)S(1)}, f32[32,128]{1,0:T(8,128)}, u32[]{:S(2)}) copy-start(f32[32,128]{1,0:T(8,128)} %diff_ref.2) | copy-start | bytes 49156
  2.4 30.1 %copy-start = (f32[512,2,128]{2,1,0:T(2,128)S(1)}, f32[512,2,128]{2,1,0:T(2,128)}, u32[]{:S(2)}) copy-start(f32[512,2,128]{2,1,0:T(2,128)} %param.11) | copy-start | bytes 1572868
  2.4 30.1 %copy-start.1 = (f32[512,2,128]{2,1,0:T(2,128)S(1)}, f32[512,2,128]{2,1,0:T(2,128)}, u32[]{:S(2)}) copy-start(f32[512,2,128]{2,1,0:T(2,128)} %param.12) | copy-start | bytes 1572868
  2.4 30.1 %copy-start.2 = (f32[512,2,128]{2,1,0:T(2,128)S(1)}, f32[512,2,128]{2,1,0:T(2,128)}, u32[]{:S(2)}) copy-start(f32[512,2,128]{2,1,0:T(2,128)} %param.13) | copy-start | bytes 1572868
  2.4 30.1 %copy-start.3 = (f32[512,2,128]{2,1,0:T(2,128)S(1)}, f32[512,2,128]{2,1,0:T(2,128)}, u32[]{:S(2)}) copy-start(f32[512,2,128]{2,1,0:T(2,128)} %param.14) | copy-start | bytes 1572868
  28.9 4.4 %copy-start.5 = (bf16[3,256,768]{2,1,0:T(8,128)(2,1)S(1)}, bf16[3,256,768]{2,1,0:T(8,128)(2,1)}, u32[]{:S(2)}) copy-start(bf16[3,256,768]{2,1,0:T(8,128)(2,1)} %constant.20.clone.table_ref.refs_9_.refs_10_) | copy-start | bytes 3538948
  29.6 15.2 %collective-permute-start.1 = (f32[1040,128]{1,0:T(8,128)S(1)}, f32[1040,128]{1,0:T(8,128)S(1)}, u32[]{:S(2)}, u32[]{:S(2)}) collective-permute-start(f32[1040,128]{1,0:T(8,128)S(1)} %get-tuple-element.50.outer.refs_2_), channel_id=1, source_target_pairs={{240,1},{1,240},{241,2},{2,241},{242,3},{3,242},{243,4},{4,243},{2... | collective-permute-start | bytes 1597448 | tf_op jit(solution)/shard_map/ppermute | solution.py:344
  31.7 10.3 %collective-permute-start.2 = (f32[1032,128]{1,0:T(8,128)S(1)}, f32[1032,128]{1,0:T(8,128)S(1)}, u32[]{:S(2)}, u32[]{:S(2)}) collective-permute-start(f32[1032,128]{1,0:T(8,128)S(1)} %get-tuple-element.51.inner.refs_3_), channel_id=1, source_target_pairs={{0,16},{16,0},{32,48},{48,32},{64,80},{80,64},{96,112},{112,96},{1... | collective-permute-start | bytes 1585160 | tf_op jit(solution)/shard_map/ppermute | solution.py:346
  31.8 10.2 %collective-permute-start = (f32[520,128]{1,0:T(8,128)S(1)}, f32[520,128]{1,0:T(8,128)S(1)}, u32[]{:S(2)}, u32[]{:S(2)}) collective-permute-start(f32[520,128]{1,0:T(8,128)S(1)} %get-tuple-element.61), channel_id=1, source_target_pairs={{16,32},{32,16},{48,64},{64,48},{80,96},{96,80},{112,128},{128,112... | collective-permute-start | bytes 798728 | tf_op jit(solution)/shard_map/ppermute | solution.py:343
  34.9 19.2 %collective-permute-start.3 = (f32[1024,128]{1,0:T(8,128)S(1)}, f32[1024,128]{1,0:T(8,128)S(1)}, u32[]{:S(2)}, u32[]{:S(2)}) collective-permute-start(f32[1024,128]{1,0:T(8,128)S(1)} %get-tuple-element.59.refs_0_), channel_id=1, source_target_pairs={{16,32},{32,16},{48,64},{64,48},{80,96},{96,80},{112,128},{128,112... | collective-permute-start | bytes 1572872 | tf_op jit(solution)/shard_map/ppermute | solution.py:328
  40.5 13.6 %collective-permute-start.4 = (f32[1024,128]{1,0:T(8,128)S(1)}, f32[1024,128]{1,0:T(8,128)S(1)}, u32[]{:S(2)}, u32[]{:S(2)}) collective-permute-start(f32[1024,128]{1,0:T(8,128)S(1)} %get-tuple-element.60.refs_1_), channel_id=1, source_target_pairs={{0,16},{16,0},{32,48},{48,32},{64,80},{80,64},{96,112},{112,96},{1... | collective-permute-start | bytes 1572872 | tf_op jit(solution)/shard_map/ppermute | solution.py:328
  46.5 17.0 %collective-permute-start.5 = (f32[1024,128]{1,0:T(8,128)S(1)}, f32[1024,128]{1,0:T(8,128)S(1)}, u32[]{:S(2)}, u32[]{:S(2)}) collective-permute-start(f32[1024,128]{1,0:T(8,128)S(1)} %get-tuple-element.63.refs_0_), channel_id=1, source_target_pairs={{16,32},{32,16},{48,64},{64,48},{80,96},{96,80},{112,128},{128,112... | collective-permute-start | bytes 1572872 | tf_op jit(solution)/shard_map/ppermute | solution.py:328
  49.3 14.3 %collective-permute-start.6 = (f32[1024,128]{1,0:T(8,128)S(1)}, f32[1024,128]{1,0:T(8,128)S(1)}, u32[]{:S(2)}, u32[]{:S(2)}) collective-permute-start(f32[1024,128]{1,0:T(8,128)S(1)} %get-tuple-element.64.refs_1_), channel_id=1, source_target_pairs={{0,16},{16,0},{32,48},{48,32},{64,80},{80,64},{96,112},{112,96},{1... | collective-permute-start | bytes 1572872 | tf_op jit(solution)/shard_map/ppermute | solution.py:328
  55.9 17.1 %collective-permute-start.7 = (f32[1024,128]{1,0:T(8,128)S(1)}, f32[1024,128]{1,0:T(8,128)S(1)}, u32[]{:S(2)}, u32[]{:S(2)}) collective-permute-start(f32[1024,128]{1,0:T(8,128)S(1)} %get-tuple-element.70.refs_0_), channel_id=1, source_target_pairs={{240,1},{1,240},{241,2},{2,241},{242,3},{3,242},{243,4},{4,243},{2... | collective-permute-start | bytes 1572872 | tf_op jit(solution)/shard_map/ppermute | solution.py:328
  59.5 13.5 %collective-permute-start.8 = (f32[1024,128]{1,0:T(8,128)S(1)}, f32[1024,128]{1,0:T(8,128)S(1)}, u32[]{:S(2)}, u32[]{:S(2)}) collective-permute-start(f32[1024,128]{1,0:T(8,128)S(1)} %get-tuple-element.71.refs_1_), channel_id=1, source_target_pairs={{0,16},{16,0},{32,48},{48,32},{64,80},{80,64},{96,112},{112,96},{1... | collective-permute-start | bytes 1572872 | tf_op jit(solution)/shard_map/ppermute | solution.py:328
